TPU v7x, 128 devices: a whole 4x4x4 slice. The times are simulated.
128 devices in a mesh: section: 2 (over core), sht: 16 (over z, x), dp: 4 (over y).
Axes of the slice: x: 4, y: 4, z: 4, core: 2. Of those that a mesh axis runs over, the one named last changes fastest.
Arguments:
- fields_in: bfloat16 [32, 64, 128, 256], P('dp', 'sht'), may hold values from -6 to 6
- cotangent: bfloat16 [32, 64, 128, 256], P('dp', 'sht'), may hold values from -6 to 6
- weights: bfloat16 [2, 64, 256, 256], P('section'), may hold values from -0.375 to 0.375
Outputs:
- section_ends: bfloat16 [2, 32, 64, 128, 256], P('section', 'dp', 'sht')
- weight_grads: float32 [2, 64, 256, 256], P('section', ('sht', 'dp'))
All inputs are finite; a program needn't handle non-finite values.
Results may differ from a plain program's by a relative error of at most 0.023.
Values may be sent and summed in bfloat16 or wider, within the bound.
No kernel may reach another device: no remote copies, remote signals or barrier semaphores. Data moves between devices by JAX's collectives and lax.ppermute only.
A program may use at most 192 MiB of HBM per device.

v0:
```python
import math

import jax
import jax.numpy as jnp
import numpy as np
from jax import lax
from jax.sharding import PartitionSpec as P

MICRO = 4


def shifted(value, axis, steps):
    count = lax.axis_size(axis)
    first, last = (max(0, -steps), min(count, count - steps))
    return lax.ppermute(value, axis, [(source, source + steps) for source in range(first, last)])


def gauss_nodes(resolution):
    counter = np.arange(resolution) * 1.0
    guesses = np.cos(math.pi * (counter + 0.75) / (resolution + 0.5))
    for sweep in range(100):
        current = np.ones(resolution)
        previous = np.zeros(resolution)
        for degree in range(1, resolution + 1):
            following = (
                (2.0 * degree - 1.0) * guesses * current - (degree - 1.0) * previous
            ) / degree
            previous = current
            current = following
        slope_val = resolution * (guesses * current - previous) / (guesses * guesses - 1.0)
        guesses = guesses - current / slope_val
    current = np.ones(resolution)
    previous = np.zeros(resolution)
    for degree in range(1, resolution + 1):
        following = ((2.0 * degree - 1.0) * guesses * current - (degree - 1.0) * previous) / degree
        previous = current
        current = following
    slope_val = resolution * (guesses * current - previous) / (guesses * guesses - 1.0)
    weights_q = 2.0 / ((1.0 - guesses * guesses) * slope_val * slope_val)
    return (guesses[::-1].copy(), weights_q[::-1].copy())


def legendre_table(resolution):
    points, quadrature = gauss_nodes(resolution)
    sine_row = np.sqrt(1.0 - points * points)
    basis = np.zeros((resolution, resolution, resolution))
    diagonal = np.full(resolution, math.sqrt(1.0 / (4.0 * math.pi)))
    for harmonic in range(resolution):
        if harmonic > 0:
            diagonal = diagonal * sine_row * math.sqrt((2.0 * harmonic + 1.0) / (2.0 * harmonic))
        basis[harmonic, harmonic] = diagonal
        if harmonic + 1 < resolution:
            basis[harmonic, harmonic + 1] = points * math.sqrt(2.0 * harmonic + 3.0) * diagonal
        for degree in range(harmonic + 2, resolution):
            alpha_coef = math.sqrt(
                (4.0 * degree * degree - 1.0) / (degree * degree - harmonic * harmonic)
            )
            beta_coef = math.sqrt(
                ((degree - 1.0) ** 2 - harmonic * harmonic) / (4.0 * (degree - 1.0) ** 2 - 1.0)
            )
            basis[harmonic, degree] = alpha_coef * (
                points * basis[harmonic, degree - 1] - beta_coef * basis[harmonic, degree - 2]
            )
    return basis * np.sqrt(2.0 * math.pi * quadrature)[None, None, :]


def longitude_table(longitudes, degrees):
    column = jnp.arange(2 * degrees, dtype=jnp.int32)
    harmonic = column // 2
    parity = column % 2
    sample = jnp.arange(longitudes, dtype=jnp.int32)
    phase_step = sample[:, None] * harmonic[None, :] % longitudes
    angles = phase_step.astype(jnp.float32) * (2.0 * math.pi / longitudes)
    scales = jnp.where(
        harmonic == 0, 1.0 / math.sqrt(longitudes), math.sqrt(2.0 / longitudes)
    ).astype(jnp.float32)
    basis = jnp.where(parity[None, :] == 0, jnp.cos(angles), -jnp.sin(angles)) * scales[None, :]
    return basis.astype(jnp.bfloat16)


def normal_cdf(values):
    return 0.5 * (1.0 + lax.erf(values * (1.0 / math.sqrt(2.0))))


def gelu_value(values):
    return values * normal_cdf(values)


def gelu_slope(values):
    density = jnp.exp(-0.5 * values * values) * (1.0 / math.sqrt(2.0 * math.pi))
    return normal_cdf(values) + values * density


def spectral_pass(field_in, polar_basis, long_basis, weight, backward):
    spectral = jnp.einsum(
        "sanc,nk->sakc", field_in, long_basis, preferred_element_type=jnp.float32
    ).astype(jnp.bfloat16)
    by_order = lax.all_to_all(spectral, "sht", split_axis=2, concat_axis=1, tiled=True)
    samples, latitudes, columns, channels = by_order.shape
    shaped = by_order.reshape(samples, latitudes, columns // 2, 2 * channels)
    coefficients = jnp.einsum(
        "mla,samx->mlsx", polar_basis, shaped, preferred_element_type=jnp.float32
    ).astype(jnp.bfloat16)
    orders_here, degrees = (coefficients.shape[0], coefficients.shape[1])
    reshaped = coefficients.reshape(orders_here, degrees, samples, 2, channels)
    if backward:
        mixed_coef = jnp.einsum(
            "mlspd,lcd->mlspc", reshaped, weight, preferred_element_type=jnp.float32
        )
    else:
        mixed_coef = jnp.einsum(
            "mlspc,lcd->mlspd", reshaped, weight, preferred_element_type=jnp.float32
        )
    mixed_coef = mixed_coef.astype(jnp.bfloat16).reshape(
        orders_here, degrees, samples, 2 * channels
    )
    grid_part = jnp.einsum(
        "mla,mlsx->samx", polar_basis, mixed_coef, preferred_element_type=jnp.float32
    ).astype(jnp.bfloat16)
    grid_part = grid_part.reshape(samples, latitudes, 2 * orders_here, channels)
    by_row = lax.all_to_all(grid_part, "sht", split_axis=1, concat_axis=2, tiled=True)
    return (
        coefficients,
        jnp.einsum("sakc,nk->sanc", by_row, long_basis, preferred_element_type=jnp.float32),
    )


def degree_products(coefficients, gradients):
    orders_all, degrees, samples, packed = coefficients.shape
    left_side = coefficients.reshape(orders_all, degrees, samples, 2, packed // 2)
    right_side = gradients.reshape(orders_all, degrees, samples, 2, packed // 2)
    return jnp.einsum("mlspc,mlspd->lcd", left_side, right_side, preferred_element_type=jnp.float32)


def local(fields_in, cotangent, weights):
    rows_all, lat_rows, longitudes, channels = fields_in.shape
    degrees = longitudes // 2
    shards = lax.axis_size("sht")
    orders_here = degrees // shards
    samples = rows_all // MICRO
    front_section = lax.axis_index("section") == 0
    long_basis = longitude_table(longitudes, degrees)
    leg_full = jnp.asarray(legendre_table(degrees), jnp.float32).astype(jnp.bfloat16)
    polar_basis = lax.dynamic_slice_in_dim(
        leg_full, lax.axis_index("sht") * orders_here, orders_here, 0
    )
    weight = weights[0]
    empty_block = jnp.zeros((samples, lat_rows, longitudes, channels), jnp.bfloat16)
    outgoing = empty_block
    stored = []
    last_outputs = []
    for period in range(MICRO + 1):
        if period == 0:
            arrived = empty_block
        else:
            arrived = shifted(outgoing, "section", 1)
        local_part = (
            fields_in[period * samples : (period + 1) * samples] if period < MICRO else empty_block
        )
        layer_in = jnp.where(front_section, local_part, arrived)
        coefficients, preact = spectral_pass(layer_in, polar_basis, long_basis, weight, False)
        outgoing = (layer_in.astype(jnp.float32) + gelu_value(preact)).astype(jnp.bfloat16)
        stored.append((coefficients, preact))
        if period > 0:
            last_outputs.append(outgoing)
    accumulated = jnp.zeros((degrees, channels, channels), jnp.float32)
    upstream = empty_block
    first_grads = []
    for period in range(MICRO + 1):
        if period == 0:
            arrived = empty_block
        else:
            arrived = shifted(upstream, "section", -1)
        local_part = (
            cotangent[period * samples : (period + 1) * samples] if period < MICRO else empty_block
        )
        incoming = jnp.where(front_section, arrived, local_part)
        from_before = stored[max(period - 1, 0)]
        from_after = stored[min(period + 1, MICRO)]
        coefficients = jnp.where(front_section, from_before[0], from_after[0])
        preact = jnp.where(front_section, from_before[1], from_after[1])
        live_mask = jnp.where(
            front_section, 1.0 if period >= 1 else 0.0, 1.0 if period < MICRO else 0.0
        ).astype(jnp.bfloat16)
        grad_pre = (incoming.astype(jnp.float32) * gelu_slope(preact)).astype(jnp.bfloat16)
        grad_mixed, returned = spectral_pass(grad_pre, polar_basis, long_basis, weight, True)
        upstream = (incoming.astype(jnp.float32) + returned).astype(jnp.bfloat16)
        if period > 0:
            first_grads.append(upstream)
        grad_live = grad_mixed * live_mask
        accumulated = accumulated + degree_products(coefficients, grad_live)
    section_ends = jnp.where(
        front_section, jnp.concatenate(first_grads, axis=0), jnp.concatenate(last_outputs, axis=0)
    )[None]
    batch_count = MICRO * samples * lax.axis_size("dp")
    summed = lax.psum_scatter(accumulated, ("sht", "dp"), scatter_dimension=0, tiled=True)
    return (section_ends, (summed / batch_count)[None])


def solution(mesh):
    in_specs = (
        P("dp", "sht", None, None),
        P("dp", "sht", None, None),
        P("section", None, None, None),
    )
    out_specs = (P("section", "dp", "sht", None, None), P("section", ("sht", "dp"), None, None))
    return jax.shard_map(local, mesh=mesh, in_specs=in_specs, out_specs=out_specs, check_vma=False)
```

profile of v0, /device:TPU:0, one launch (start us, length us, event | category | flops | bytes accessed | tf_op | source)
XLA Modules:
  0.0 859.0 jit_solution(11656876021610213364)
XLA Ops:
  10.1 8.0 all-to-all-start
  18.0 11.5 %all-to-all-done = bf16[2,4,128,256]{3,1,0,2:T(4,128)(2,1)S(1)} async-done(((bf16[2,4,128,256]{3,1,0,2:T(4,128)(2,1)}), bf16[2,4,128,256]{3,1,0,2:T(4,128)(2,1)S(1)}, u32[]{:S(2)}, u32[]{:S(2)}) %all-to-all-start) | async-done | bytes 524320 | tf_op jit(solution)/shard_map/all_to_all | solution.py:98
  38.4 13.7 %all_to_all.330 = bf16[2,64,8,256]{3,2,0,1:T(8,128)(2,1)S(1)} all-to-all(bf16[2,64,8,256]{3,2,0,1:T(8,128)(2,1)S(1)} %reshape.368), channel_id=1, replica_groups=mesh['section'=2,'sht'=16,'dp'=4] {'sht'}, dimensions={1} | all-to-all | bytes 1048576 | tf_op jit(solution)/shard_map/all_to_all | solution.py:121
  59.6 15.0 %all_to_all.331 = bf16[2,4,128,256]{3,1,0,2:T(4,128)(2,1)S(1)} all-to-all(bf16[2,4,128,256]{3,1,0,2:T(4,128)(2,1)S(1)} %copy.148), channel_id=1, replica_groups=mesh['section'=2,'sht'=16,'dp'=4] {'sht'}, dimensions={2} | all-to-all | bytes 1048576 | tf_op jit(solution)/shard_map/all_to_all | solution.py:98
  83.5 14.1 %all_to_all.332 = bf16[2,64,8,256]{3,2,0,1:T(8,128)(2,1)S(1)} all-to-all(bf16[2,64,8,256]{3,2,0,1:T(8,128)(2,1)S(1)} %reshape.369), channel_id=1, replica_groups=mesh['section'=2,'sht'=16,'dp'=4] {'sht'}, dimensions={1} | all-to-all | bytes 1048576 | tf_op jit(solution)/shard_map/all_to_all | solution.py:121
  108.9 8.7 %all-to-all-done.4 = bf16[2,4,128,256]{3,1,0,2:T(4,128)(2,1)S(1)} async-done(((bf16[2,4,128,256]{3,1,0,2:T(4,128)(2,1)}), bf16[2,4,128,256]{3,1,0,2:T(4,128)(2,1)S(1)}, u32[]{:S(2)}, u32[]{:S(2)}) %all-to-all-start.4) | async-done | bytes 524320 | tf_op jit(solution)/shard_map/all_to_all | solution.py:98
  136.7 6.1 all-to-all-start.5
  153.0 6.9 all-to-all-start.7
  163.7 6.3 all-to-all-done.7
  182.9 8.0 all-to-all-done.8
  209.8 7.6 all-to-all-start.9
  230.0 7.4 all-to-all-start.11
  240.6 7.0 all-to-all-done.11
  260.6 8.8 %all-to-all-done.12 = bf16[2,4,128,256]{3,1,0,2:T(4,128)(2,1)} async-done(((bf16[2,4,128,256]{3,1,0,2:T(4,128)(2,1)}), bf16[2,4,128,256]{3,1,0,2:T(4,128)(2,1)}, u32[]{:S(2)}, u32[]{:S(2)}) %all-to-all-start.12) | async-done | bytes 524320 | tf_op jit(solution)/shard_map/all_to_all | solution.py:98
  297.7 7.3 all-to-all-start.13
  321.6 7.2 all-to-all-start.15
  348.8 9.8 %fusion.425 = f32[64,256,256,1,1]{2,1,0,4,3:T(8,128)} fusion(bf16[4,64,2,2,256]{4,3,1,2,0:T(2,128)(2,1)} %reshape.336, bf16[4,64,2,2,256]{4,3,1,2,0:T(2,128)(2,1)S(1)} %copy-done.2), kind=kOutput, calls=%fused_computation.458 | convolution fusion | flops 134217728 | bytes 17825792 | tf_op jit(solution)/shard_map/mlspc,mlspd->lcd/dot_general | solution.py:132
  366.7 5.8 fusion.63
  382.5 9.7 %fusion.424 = f32[64,256,256,1,1]{2,1,0,4,3:T(8,128)} fusion(bf16[4,64,2,2,256]{4,3,1,2,0:T(2,128)(2,1)} %reshape.335, bf16[4,64,2,2,256]{4,3,1,2,0:T(2,128)(2,1)S(1)} %reshape.310), kind=kOutput, calls=%fused_computation.457 | convolution fusion | flops 134217728 | bytes 17825792 | tf_op jit(solution)/shard_map/mlspc,mlspd->lcd/dot_general | solution.py:132
  399.0 9.8 %fusion.423 = f32[64,256,256,1,1]{2,1,0,4,3:T(8,128)} fusion(bf16[4,64,2,2,256]{4,3,1,2,0:T(2,128)(2,1)} %reshape.333, bf16[4,64,2,2,256]{4,3,1,2,0:T(2,128)(2,1)} %reshape.334), kind=kOutput, calls=%fused_computation.456 | convolution fusion | flops 134217728 | bytes 17825792 | tf_op jit(solution)/shard_map/mlspc,mlspd->lcd/dot_general | solution.py:132
  419.2 8.6 %fusion.426 = f32[64,256,256,1,1]{2,1,0,4,3:T(8,128)} fusion(bf16[4,64,2,2,256]{4,3,1,2,0:T(2,128)(2,1)S(1)} %reshape.337, bf16[4,64,2,2,256]{4,3,1,2,0:T(2,128)(2,1)S(1)} %copy-done.6), kind=kOutput, calls=%fused_computation.459 | convolution fusion | flops 134217728 | bytes 17825792 | tf_op jit(solution)/shard_map/mlspc,mlspd->lcd/dot_general | solution.py:132
  433.1 28.6 %bitcast_add_fusion = f32[64,256,256]{2,1,0:T(8,128)} fusion(f32[64,256,256,1,1]{2,1,0,4,3:T(8,128)} %fusion.426, f32[64,256,256,1,1]{2,1,0,4,3:T(8,128)} %fusion.425, f32[64,256,256,1,1]{2,1,0,4,3:T(8,128)} %fusion.424, f32[64,256,256,1,1]{2,1,0,4,3:T(8,128)} %fusion.423, bf16[4,64,2,2,256]{4,3,1,2,0:T(2,128)(2,1)} %reshape.338, ...), kind=kOutput, calls=%fused_computation | convolution fusion | flops 150994944 | bytes 84934656 | tf_op jit(solution)/shard_map/mlspc,mlspd->lcd/dot_general | solution.py:132
  474.8 13.7 %all-to-all-done.19 = bf16[2,64,8,256]{3,2,0,1:T(8,128)(2,1)S(1)} async-done(((bf16[2,64,8,256]{3,2,0,1:T(8,128)(2,1)}), bf16[2,64,8,256]{3,2,0,1:T(8,128)(2,1)S(1)}, u32[]{:S(2)}, u32[]{:S(2)}) %all-to-all-start.19) | async-done | bytes 524320 | tf_op jit(solution)/shard_map/all_to_all | solution.py:121
  493.2 356.9 %reduce-scatter.2.cloned.1.call-done = f32[1,256,256]{2,1,0:T(8,128)} async-done(((f32[64,256,256]{2,1,0:T(8,128)}), f32[1,256,256]{2,1,0:T(8,128)}) %reduce-scatter.2.cloned.1.call-update) | async-done | bytes 262160 | tf_op jit(solution)/shard_map/reduce_scatter | solution.py:196
  (208 shorter events, 256.9 us)
Async XLA Ops:
  10.1 19.5 %all-to-all-start = ((bf16[2,4,128,256]{3,1,0,2:T(4,128)(2,1)}), bf16[2,4,128,256]{3,1,0,2:T(4,128)(2,1)S(1)}, u32[]{:S(2)}, u32[]{:S(2)}) async-start(bf16[2,4,128,256]{3,1,0,2:T(4,128)(2,1)} %copy.137), calls=%async_computation | async-start | bytes 1048576 | tf_op jit(solution)/shard_map/all_to_all | solution.py:98
  103.9 13.6 %all-to-all-start.4 = ((bf16[2,4,128,256]{3,1,0,2:T(4,128)(2,1)}), bf16[2,4,128,256]{3,1,0,2:T(4,128)(2,1)S(1)}, u32[]{:S(2)}, u32[]{:S(2)}) async-start(bf16[2,4,128,256]{3,1,0,2:T(4,128)(2,1)} %copy.159), calls=%async_computation.4 | async-start | bytes 1048576 | tf_op jit(solution)/shard_map/all_to_all | solution.py:98
  107.5 12.6 %collective-permute-start.2 = (bf16[2,4,128,256]{3,2,1,0:T(8,128)(2,1)S(1)}, bf16[2,4,128,256]{3,2,1,0:T(8,128)(2,1)S(1)}, u32[]{:S(2)}, u32[]{:S(2)}) collective-permute-start(bf16[2,4,128,256]{3,2,1,0:T(8,128)(2,1)S(1)} %get-tuple-element.9), channel_id=1, source_target_pairs={{0,64},{1,65},{2,66},{3,67},{4,68},{5,69},{6,70},{7,71},{8,72},{9,... | collective-permute-start | bytes 1572872 | tf_op jit(solution)/shard_map/ppermute | solution.py:15
  123.0 13.7 %all-to-all-start.6 = ((bf16[2,4,128,256]{3,1,0,2:T(4,128)(2,1)}), bf16[2,4,128,256]{3,1,0,2:T(4,128)(2,1)S(1)}, u32[]{:S(2)}, u32[]{:S(2)}) async-start(bf16[2,4,128,256]{3,1,0,2:T(4,128)(2,1)} %copy.170), calls=%async_computation.6 | async-start | bytes 1048576 | tf_op jit(solution)/shard_map/all_to_all | solution.py:98
  136.7 16.3 %all-to-all-start.5 = ((bf16[2,64,8,256]{3,2,0,1:T(8,128)(2,1)}), bf16[2,64,8,256]{3,2,0,1:T(8,128)(2,1)}, u32[]{:S(2)}, u32[]{:S(2)}) async-start(bf16[2,64,8,256]{3,2,0,1:T(8,128)(2,1)} %reshape.370), calls=%async_computation.5 | async-start | bytes 1048576 | tf_op jit(solution)/shard_map/all_to_all | solution.py:121
  153.0 17.0 %all-to-all-start.7 = ((bf16[2,64,8,256]{3,2,0,1:T(8,128)(2,1)}), bf16[2,64,8,256]{3,2,0,1:T(8,128)(2,1)S(1)}, u32[]{:S(2)}, u32[]{:S(2)}) async-start(bf16[2,64,8,256]{3,2,0,1:T(8,128)(2,1)} %reshape.371), calls=%async_computation.7 | async-start | bytes 1048576 | tf_op jit(solution)/shard_map/all_to_all | solution.py:121
  162.4 10.1 %collective-permute-start.1 = (bf16[2,4,128,256]{3,2,1,0:T(8,128)(2,1)}, bf16[2,4,128,256]{3,2,1,0:T(8,128)(2,1)S(1)}, u32[]{:S(2)}, u32[]{:S(2)}) collective-permute-start(bf16[2,4,128,256]{3,2,1,0:T(8,128)(2,1)} %fusion.29), channel_id=1, source_target_pairs={{64,0},{65,1},{66,2},{67,3},{68,4},{69,5},{70,6},{71,7},{72,8},{73... | collective-permute-start | bytes 1572872 | tf_op jit(solution)/shard_map/ppermute | solution.py:15
  177.2 13.6 %all-to-all-start.8 = ((bf16[2,4,128,256]{3,1,0,2:T(4,128)(2,1)}), bf16[2,4,128,256]{3,1,0,2:T(4,128)(2,1)S(1)}, u32[]{:S(2)}, u32[]{:S(2)}) async-start(bf16[2,4,128,256]{3,1,0,2:T(4,128)(2,1)} %copy.181), calls=%async_computation.8 | async-start | bytes 1048576 | tf_op jit(solution)/shard_map/all_to_all | solution.py:98
  180.8 11.8 %collective-permute-start.4 = (bf16[2,4,128,256]{3,2,1,0:T(8,128)(2,1)}, bf16[2,4,128,256]{3,2,1,0:T(8,128)(2,1)}, u32[]{:S(2)}, u32[]{:S(2)}) collective-permute-start(bf16[2,4,128,256]{3,2,1,0:T(8,128)(2,1)} %get-tuple-element.11), channel_id=1, source_target_pairs={{0,64},{1,65},{2,66},{3,67},{4,68},{5,69},{6,70},{7,71},{8,72},{9,... | collective-permute-start | bytes 1572872 | tf_op jit(solution)/shard_map/ppermute | solution.py:15
  195.4 14.4 %all-to-all-start.10 = ((bf16[2,4,128,256]{3,1,0,2:T(4,128)(2,1)}), bf16[2,4,128,256]{3,1,0,2:T(4,128)(2,1)S(1)}, u32[]{:S(2)}, u32[]{:S(2)}) async-start(bf16[2,4,128,256]{3,1,0,2:T(4,128)(2,1)} %copy.192), calls=%async_computation.10 | async-start | bytes 1048576 | tf_op jit(solution)/shard_map/all_to_all | solution.py:98
  209.8 20.1 %all-to-all-start.9 = ((bf16[2,64,8,256]{3,2,0,1:T(8,128)(2,1)}), bf16[2,64,8,256]{3,2,0,1:T(8,128)(2,1)}, u32[]{:S(2)}, u32[]{:S(2)}) async-start(bf16[2,64,8,256]{3,2,0,1:T(8,128)(2,1)} %reshape.372), calls=%async_computation.9 | async-start | bytes 1048576 | tf_op jit(solution)/shard_map/all_to_all | solution.py:121
  230.0 17.6 %all-to-all-start.11 = ((bf16[2,64,8,256]{3,2,0,1:T(8,128)(2,1)}), bf16[2,64,8,256]{3,2,0,1:T(8,128)(2,1)}, u32[]{:S(2)}, u32[]{:S(2)}) async-start(bf16[2,64,8,256]{3,2,0,1:T(8,128)(2,1)} %reshape.373), calls=%async_computation.11 | async-start | bytes 1048576 | tf_op jit(solution)/shard_map/all_to_all | solution.py:121
  239.3 11.0 %collective-permute-start.3 = (bf16[2,4,128,256]{3,2,1,0:T(8,128)(2,1)S(1)}, bf16[2,4,128,256]{3,2,1,0:T(8,128)(2,1)}, u32[]{:S(2)}, u32[]{:S(2)}) collective-permute-start(bf16[2,4,128,256]{3,2,1,0:T(8,128)(2,1)S(1)} %fusion.28), channel_id=1, source_target_pairs={{64,0},{65,1},{66,2},{67,3},{68,4},{69,5},{70,6},{71,7},{72,8},{73... | collective-permute-start | bytes 1572872 | tf_op jit(solution)/shard_map/ppermute | solution.py:15
  255.0 14.4 %all-to-all-start.12 = ((bf16[2,4,128,256]{3,1,0,2:T(4,128)(2,1)}), bf16[2,4,128,256]{3,1,0,2:T(4,128)(2,1)}, u32[]{:S(2)}, u32[]{:S(2)}) async-start(bf16[2,4,128,256]{3,1,0,2:T(4,128)(2,1)} %copy.203), calls=%async_computation.12 | async-start | bytes 1048576 | tf_op jit(solution)/shard_map/all_to_all | solution.py:98
  259.3 18.4 %collective-permute-start.6 = (bf16[2,4,128,256]{3,2,1,0:T(8,128)(2,1)}, bf16[2,4,128,256]{3,2,1,0:T(8,128)(2,1)S(1)}, u32[]{:S(2)}, u32[]{:S(2)}) collective-permute-start(bf16[2,4,128,256]{3,2,1,0:T(8,128)(2,1)} %get-tuple-element.13), channel_id=1, source_target_pairs={{0,64},{1,65},{2,66},{3,67},{4,68},{5,69},{6,70},{7,71},{8,72},{9,... | collective-permute-start | bytes 1572872 | tf_op jit(solution)/shard_map/ppermute | solution.py:15
  279.5 18.2 %all-to-all-start.14 = ((bf16[2,4,128,256]{3,1,0,2:T(4,128)(2,1)}), bf16[2,4,128,256]{3,1,0,2:T(4,128)(2,1)}, u32[]{:S(2)}, u32[]{:S(2)}) async-start(bf16[2,4,128,256]{3,1,0,2:T(4,128)(2,1)} %copy.214), calls=%async_computation.14 | async-start | bytes 1048576 | tf_op jit(solution)/shard_map/all_to_all | solution.py:98
  297.7 23.8 %all-to-all-start.13 = ((bf16[2,64,8,256]{3,2,0,1:T(8,128)(2,1)}), bf16[2,64,8,256]{3,2,0,1:T(8,128)(2,1)}, u32[]{:S(2)}, u32[]{:S(2)}) async-start(bf16[2,64,8,256]{3,2,0,1:T(8,128)(2,1)} %reshape.374), calls=%async_computation.13 | async-start | bytes 1048576 | tf_op jit(solution)/shard_map/all_to_all | solution.py:121
  321.6 17.4 %all-to-all-start.15 = ((bf16[2,64,8,256]{3,2,0,1:T(8,128)(2,1)}), bf16[2,64,8,256]{3,2,0,1:T(8,128)(2,1)}, u32[]{:S(2)}, u32[]{:S(2)}) async-start(bf16[2,64,8,256]{3,2,0,1:T(8,128)(2,1)} %reshape.375), calls=%async_computation.15 | async-start | bytes 1048576 | tf_op jit(solution)/shard_map/all_to_all | solution.py:121
  344.4 17.7 %all-to-all-start.16 = ((bf16[2,4,128,256]{3,1,0,2:T(4,128)(2,1)}), bf16[2,4,128,256]{3,1,0,2:T(4,128)(2,1)}, u32[]{:S(2)}, u32[]{:S(2)}) async-start(bf16[2,4,128,256]{3,1,0,2:T(4,128)(2,1)} %copy.225), calls=%async_computation.16 | async-start | bytes 1048576 | tf_op jit(solution)/shard_map/all_to_all | solution.py:98
  377.6 17.2 %all-to-all-start.17 = ((bf16[2,64,8,256]{3,2,0,1:T(8,128)(2,1)}), bf16[2,64,8,256]{3,2,0,1:T(8,128)(2,1)S(1)}, u32[]{:S(2)}, u32[]{:S(2)}) async-start(bf16[2,64,8,256]{3,2,0,1:T(8,128)(2,1)} %reshape.376), calls=%async_computation.17 | async-start | bytes 1048576 | tf_op jit(solution)/shard_map/all_to_all | solution.py:121
  397.4 12.6 %collective-permute-start.7 = (bf16[2,4,128,256]{3,2,1,0:T(8,128)(2,1)}, bf16[2,4,128,256]{3,2,1,0:T(8,128)(2,1)}, u32[]{:S(2)}, u32[]{:S(2)}) collective-permute-start(bf16[2,4,128,256]{3,2,1,0:T(8,128)(2,1)} %fusion.26), channel_id=1, source_target_pairs={{64,0},{65,1},{66,2},{67,3},{68,4},{69,5},{70,6},{71,7},{72,8},{73... | collective-permute-start | bytes 1572872 | tf_op jit(solution)/shard_map/ppermute | solution.py:15
  413.6 17.8 %all-to-all-start.18 = ((bf16[2,4,128,256]{3,1,0,2:T(4,128)(2,1)}), bf16[2,4,128,256]{3,1,0,2:T(4,128)(2,1)S(1)}, u32[]{:S(2)}, u32[]{:S(2)}) async-start(bf16[2,4,128,256]{3,1,0,2:T(4,128)(2,1)} %copy.236), calls=%async_computation.18 | async-start | bytes 1048576 | tf_op jit(solution)/shard_map/all_to_all | solution.py:98
  419.1 430.9 %reduce-scatter.2.cloned.1.call-start = ((), (), s32[]{:S(2)}) async-start(), calls=%async_computation.21 | async-start | bytes 17039360 | tf_op jit(solution)/shard_map/reduce_scatter | solution.py:196
  470.8 17.6 %all-to-all-start.19 = ((bf16[2,64,8,256]{3,2,0,1:T(8,128)(2,1)}), bf16[2,64,8,256]{3,2,0,1:T(8,128)(2,1)S(1)}, u32[]{:S(2)}, u32[]{:S(2)}) async-start(bf16[2,64,8,256]{3,2,0,1:T(8,128)(2,1)} %reshape.377), calls=%async_computation.19 | async-start | bytes 1048576 | tf_op jit(solution)/shard_map/all_to_all | solution.py:121
  (16 other events, 208.8 us)
Sparse Core Ops, SparseCore 0:
  461.9 388.1 reduce-scatter.1
where the time goes:
time: 872 us; the launch traced here: 859 us
  waiting for transfers between devices  435 us (50%)
  matrix products  189 us (22%)
  starting transfers between devices  103 us (12%)
  local copies, waits for them, and re-layouts  68.2 us (8%)
  blocking collectives  42.8 us (5%)
  between operations  15.5 us (2%)
    reduce_scatter x1, waiting for transfers between devices, local(): lax.psum_scatter(accumulated, ('sht', 'dp'), scatter_dimension=0, tiled=T...  357 us
    dot_general x5, matrix products, degree_products(): jnp.einsum('mlspc,mlspd->lcd', left_side, right_side, preferred_element_t...  66.6 us
    all_to_all x8, starting transfers between devices, spectral_pass(): lax.all_to_all(grid_part, 'sht', split_axis=1, concat_axis=2, tiled=True)  51 us
    all_to_all x9, waiting for transfers between devices, spectral_pass(): lax.all_to_all(spectral, 'sht', split_axis=2, concat_axis=1, tiled=True)  44.1 us
    all_to_all x9, starting transfers between devices, spectral_pass(): lax.all_to_all(spectral, 'sht', split_axis=2, concat_axis=1, tiled=True)  40.9 us
    all_to_all x8, waiting for transfers between devices, spectral_pass(): lax.all_to_all(grid_part, 'sht', split_axis=1, concat_axis=2, tiled=True)  32.4 us
    dot_general x5, matrix products, spectral_pass(): jnp.einsum('mlspd,lcd->mlspc', reshaped, weight, preferred_element_type=j...  28.6 us
    all_to_all x2, blocking collectives, spectral_pass(): lax.all_to_all(grid_part, 'sht', split_axis=1, concat_axis=2, tiled=True)  27.8 us
  transfers between devices with their start and end apart: 26, of which 15 were waited for; matrix products, arithmetic and copies ran while one was open for 18% of the time, Pallas kernels for 0%

commit v1 on v0

v1 whole, which is shorter than its diff:
```python
import math

import jax
import jax.numpy as jnp
import ml_dtypes
import numpy as np
from jax import lax
from jax.experimental import pallas as pl
from jax.experimental.pallas import tpu as pltpu
from jax.sharding import PartitionSpec as P

BF16 = jnp.bfloat16
F32 = jnp.float32


def gauss_nodes(resolution):
    counter = np.arange(resolution) * 1.0
    guesses = np.cos(math.pi * (counter + 0.75) / (resolution + 0.5))
    for sweep in range(100):
        current = np.ones(resolution)
        previous = np.zeros(resolution)
        for degree in range(1, resolution + 1):
            following = (
                (2.0 * degree - 1.0) * guesses * current - (degree - 1.0) * previous
            ) / degree
            previous = current
            current = following
        slope_val = resolution * (guesses * current - previous) / (guesses * guesses - 1.0)
        guesses = guesses - current / slope_val
    current = np.ones(resolution)
    previous = np.zeros(resolution)
    for degree in range(1, resolution + 1):
        following = ((2.0 * degree - 1.0) * guesses * current - (degree - 1.0) * previous) / degree
        previous = current
        current = following
    slope_val = resolution * (guesses * current - previous) / (guesses * guesses - 1.0)
    weights_q = 2.0 / ((1.0 - guesses * guesses) * slope_val * slope_val)
    return (guesses[::-1].copy(), weights_q[::-1].copy())


def legendre_table(resolution):
    points, quadrature = gauss_nodes(resolution)
    sine_row = np.sqrt(1.0 - points * points)
    basis = np.zeros((resolution, resolution, resolution))
    diagonal = np.full(resolution, math.sqrt(1.0 / (4.0 * math.pi)))
    for harmonic in range(resolution):
        if harmonic > 0:
            diagonal = diagonal * sine_row * math.sqrt((2.0 * harmonic + 1.0) / (2.0 * harmonic))
        basis[harmonic, harmonic] = diagonal
        if harmonic + 1 < resolution:
            basis[harmonic, harmonic + 1] = points * math.sqrt(2.0 * harmonic + 3.0) * diagonal
        for degree in range(harmonic + 2, resolution):
            alpha_coef = math.sqrt(
                (4.0 * degree * degree - 1.0) / (degree * degree - harmonic * harmonic)
            )
            beta_coef = math.sqrt(
                ((degree - 1.0) ** 2 - harmonic * harmonic) / (4.0 * (degree - 1.0) ** 2 - 1.0)
            )
            basis[harmonic, degree] = alpha_coef * (
                points * basis[harmonic, degree - 1] - beta_coef * basis[harmonic, degree - 2]
            )
    return basis * np.sqrt(2.0 * math.pi * quadrature)[None, None, :]


def longitude_table(longitudes, degrees):
    column = np.arange(2 * degrees)
    harmonic, parity = column // 2, column % 2
    phase = (np.arange(longitudes)[:, None] * harmonic[None, :]) % longitudes
    angles = phase.astype(np.float32) * np.float32(2.0 * math.pi / longitudes)
    scales = np.where(harmonic == 0, 1.0 / math.sqrt(longitudes), math.sqrt(2.0 / longitudes))
    basis = np.where(parity[None, :] == 0, np.cos(angles), -np.sin(angles))
    return (basis * scales[None, :].astype(np.float32)).astype(ml_dtypes.bfloat16)


def polar_tables(degrees, shards):
    leg = legendre_table(degrees).astype(np.float32).astype(ml_dtypes.bfloat16)
    orders = degrees // shards
    wide = 2 * orders
    table = np.zeros((shards, degrees, wide, degrees, wide), ml_dtypes.bfloat16)
    for shard in range(shards):
        for k in range(wide):
            table[shard, :, k, :, k] = leg[shard * orders + k // 2]
    return table.reshape(shards, degrees * wide, degrees * wide)


def params(megabytes=48):
    return pltpu.CompilerParams(vmem_limit_bytes=megabytes * 2**20)


def dot(left, right):
    return jnp.dot(left, right, preferred_element_type=F32)


def normal_cdf(values):
    return 0.5 * (1.0 + lax.erf(values * (1.0 / math.sqrt(2.0))))


def store_analysis(spectra, out_ref):
    shards = out_ref.shape[0]
    wide = spectra[0].shape[0] // shards
    for d in range(shards):
        rows = [s[d * wide : (d + 1) * wide] for s in spectra]
        out_ref[d, 0] = jnp.concatenate(rows, axis=0).astype(BF16)


def load_spectra(in_ref):
    shards, _, rows, _ = in_ref.shape
    wide = 128 // shards
    blocks = [in_ref[d, 0].astype(F32) for d in range(shards)]
    return [
        jnp.concatenate([b[a * wide : (a + 1) * wide] for b in blocks], axis=0).astype(BF16)
        for a in range(rows // wide)
    ]


def first_body(idx_ref, field_ref, ana_ref, out_ref):
    basis = ana_ref[...]
    store_analysis([dot(basis, field_ref[0, a]) for a in range(field_ref.shape[1])], out_ref)


def layer0_body(idx_ref, in_ref, field_ref, syn_ref, ana_ref, h_ref, slope_ref, out_ref):
    syn, ana = syn_ref[...], ana_ref[...]
    spectra = []
    for a, spec in enumerate(load_spectra(in_ref)):
        pre = dot(syn, spec)
        cdf = normal_cdf(pre)
        density = jnp.exp(-0.5 * pre * pre) * (1.0 / math.sqrt(2.0 * math.pi))
        slope_ref[0, a] = (cdf + pre * density).astype(BF16)
        h = (field_ref[0, a].astype(F32) + pre * cdf).astype(BF16)
        h_ref[0, a] = h
        spectra.append(dot(ana, h))
    store_analysis(spectra, out_ref)


def layer1_body(idx_ref, in_ref, h_ref, cot_ref, syn_ref, ana_ref, top_ref, out_ref):
    syn, ana = syn_ref[...], ana_ref[...]
    spectra = []
    for a, spec in enumerate(load_spectra(in_ref)):
        pre = dot(syn, spec)
        cdf = normal_cdf(pre)
        density = jnp.exp(-0.5 * pre * pre) * (1.0 / math.sqrt(2.0 * math.pi))
        top_ref[0, a] = (h_ref[0, a].astype(F32) + pre * cdf).astype(BF16)
        gpre = (cot_ref[0, a].astype(F32) * (cdf + pre * density)).astype(BF16)
        spectra.append(dot(ana, gpre))
    store_analysis(spectra, out_ref)


def back1_body(idx_ref, in_ref, cot_ref, slope_ref, syn_ref, ana_ref, g_ref, out_ref):
    syn, ana = syn_ref[...], ana_ref[...]
    spectra = []
    for a, spec in enumerate(load_spectra(in_ref)):
        g = (cot_ref[0, a].astype(F32) + dot(syn, spec)).astype(BF16)
        g_ref[0, a] = g
        gpre = (g.astype(F32) * slope_ref[0, a].astype(F32)).astype(BF16)
        spectra.append(dot(ana, gpre))
    store_analysis(spectra, out_ref)


def back0_body(idx_ref, in_ref, g_ref, syn_ref, out_ref):
    syn = syn_ref[...]
    for a, spec in enumerate(load_spectra(in_ref)):
        out_ref[0, a] = (g_ref[0, a].astype(F32) + dot(syn, spec)).astype(BF16)


def mix_body(layer, backward, chunks, idx_ref, in_ref, fwd_ref, bwd_ref, own_ref, far_ref, *rest):
    rest = rest if len(rest) == 5 else rest[1:]
    coef_ref, out_ref, w_ref, mixed_ref, sem = rest
    shards, samples, rows, channels = in_ref.shape
    degrees = w_ref.shape[0]
    wide = fwd_ref.shape[1] // degrees
    step = degrees // chunks

    def fetch(c, source):
        span = pl.ds(c * step, step)
        return pltpu.make_async_copy(source.at[0, span], w_ref.at[span], sem.at[c])

    mine = idx_ref[1] == layer

    @pl.when(mine)
    def _():
        for c in range(chunks):
            fetch(c, own_ref).start()

    @pl.when(jnp.logical_not(mine))
    def _():
        for c in range(chunks):
            fetch(c, far_ref).start()

    forward = fwd_ref[0]
    for pair in range(0, samples, 2):
        both = []
        for s in (pair, pair + 1):
            flat = in_ref[:, s].reshape(shards * rows, channels)
            both.append(dot(forward, flat).reshape(degrees, wide, channels))
        coef_ref[:, pair * wide : (pair + 2) * wide] = jnp.concatenate(both, axis=1).astype(BF16)
    contract = (((1,), (1 if backward else 0,)), ((), ()))
    for c in range(chunks):
        fetch(c, own_ref).wait()
        for l in range(c * step, (c + 1) * step):
            mixed = lax.dot_general(coef_ref[l], w_ref[l], contract, preferred_element_type=F32)
            for s in range(samples):
                mixed_ref[s, l * wide : (l + 1) * wide] = mixed[s * wide : (s + 1) * wide]
    inverse = bwd_ref[0]
    for s in range(samples):
        grid = dot(inverse, mixed_ref[s].astype(BF16)).astype(BF16)
        out_ref[:, s] = grid.reshape(shards, rows, channels)


def local(polar, polar_t, fields_in, cotangent, weights):
    rows_all, lat_rows, longitudes, channels = fields_in.shape
    degrees = longitudes // 2
    shards = lax.axis_size("sht")
    samples = rows_all // 2
    wide = 2 * degrees // shards
    rows = lat_rows * wide
    section = lax.axis_index("section")
    idx = jnp.stack([lax.axis_index("sht"), section]).astype(jnp.int32)
    syn_np = longitude_table(longitudes, degrees)
    syn = jnp.asarray(syn_np)
    ana = jnp.asarray(np.ascontiguousarray(syn_np.T))

    grid_block = (1, lat_rows, longitudes, channels)
    spec_block = (shards, 1, rows, channels)
    half = pl.BlockSpec(grid_block, lambda s, i: (s + i[1] * samples, 0, 0, 0))
    field = pl.BlockSpec(grid_block, lambda s, i: (s, 0, 0, 0))
    spectral = pl.BlockSpec(spec_block, lambda s, i: (0, s, 0, 0))
    basis = pl.BlockSpec((longitudes, longitudes), lambda s, i: (0, 0))
    field_shape = jax.ShapeDtypeStruct((samples, lat_rows, longitudes, channels), BF16)
    spec_shape = jax.ShapeDtypeStruct((shards, samples, rows, channels), BF16)

    def grid_call(body, ins, outs, shapes, *args):
        return pl.pallas_call(
            body,
            grid_spec=pltpu.PrefetchScalarGridSpec(
                num_scalar_prefetch=1, grid=(samples,), in_specs=ins, out_specs=outs
            ),
            out_shape=shapes,
            compiler_params=params(),
        )(idx, *args)

    full = pl.BlockSpec((shards, samples, rows, channels), lambda t, i: (0, 0, 0, 0))
    size = degrees * wide
    table = pl.BlockSpec((1, size, size), lambda t, i: (i[0], 0, 0))
    anywhere = pl.BlockSpec(memory_space=pl.ANY)
    height = samples * wide
    chunks = 8

    def mix_call(slot, layer, backward, value, own, far, held):
        ins = [full, table, table, anywhere, anywhere]
        args = [value, polar, polar_t, own, far]
        alias = {}
        if held is not None:
            ins.append(anywhere)
            args.append(held)
            alias = {6: 0}

        def body(*refs):
            mix_body(layer, backward, chunks, *refs)

        return pl.pallas_call(
            body,
            grid_spec=pltpu.PrefetchScalarGridSpec(
                num_scalar_prefetch=1,
                grid=(1,),
                in_specs=ins,
                out_specs=[
                    pl.BlockSpec((degrees, height, channels), lambda t, i: (0, slot, 0)),
                    full,
                ],
                scratch_shapes=[
                    pltpu.VMEM((degrees, channels, channels), BF16),
                    pltpu.VMEM((samples, size, channels), F32),
                    pltpu.SemaphoreType.DMA((chunks,)),
                ],
            ),
            out_shape=[
                jax.ShapeDtypeStruct((degrees, 4 * height, channels), BF16),
                spec_shape,
            ],
            input_output_aliases=alias,
            compiler_params=params(),
        )(idx, *args)

    def turn(value):
        return lax.all_to_all(value, "sht", 0, 0, tiled=True)

    far = lax.ppermute(weights, "section", [(0, 1), (1, 0)])
    value = grid_call(first_body, [half, basis], spectral, spec_shape, fields_in, ana)
    held, value = mix_call(0, 0, False, turn(value), weights, far, None)
    h1, slope, value = grid_call(
        layer0_body,
        [spectral, half, basis, basis],
        [field, field, spectral],
        [field_shape, field_shape, spec_shape],
        turn(value), fields_in, syn, ana,
    )
    held, value = mix_call(1, 1, False, turn(value), weights, far, held)
    top, value = grid_call(
        layer1_body,
        [spectral, field, half, basis, basis],
        [field, spectral],
        [field_shape, spec_shape],
        turn(value), h1, cotangent, syn, ana,
    )
    held, value = mix_call(3, 1, True, turn(value), weights, far, held)
    g1, value = grid_call(
        back1_body,
        [spectral, half, field, basis, basis],
        [field, spectral],
        [field_shape, spec_shape],
        turn(value), cotangent, slope, syn, ana,
    )
    held, value = mix_call(2, 0, True, turn(value), weights, far, held)
    value, held = lax.optimization_barrier((turn(value), held))
    bottom = grid_call(
        back0_body, [spectral, field, basis], field, field_shape, value, g1, syn
    )
    front = section == 0
    passed = lax.ppermute(jnp.where(front, top, bottom), "section", [(0, 1), (1, 0)])
    section_ends = jnp.concatenate(
        [jnp.where(front, bottom, passed), jnp.where(front, passed, top)], axis=0
    )[None]

    owned = lax.all_to_all(held, ("sht", "dp"), 0, 0, tiled=True)
    owned = owned.reshape(-1, 4, height, channels)

    def product(j):
        return jnp.einsum(
            "irc,ird->cd", owned[:, j], owned[:, j + 2], preferred_element_type=F32
        )

    first, second = product(0), product(1)
    keep = jnp.where(front, first, second)
    give = jnp.where(front, second, first)
    total = keep + lax.ppermute(give, "section", [(0, 1), (1, 0)])
    batch_count = rows_all * lax.axis_size("dp")
    return (section_ends, (total / batch_count)[None, None])


def solution(mesh):
    in_specs = (
        P("dp", "sht", None, None),
        P("dp", "sht", None, None),
        P("section", None, None, None),
    )
    out_specs = (P("section", "dp", "sht", None, None), P("section", ("sht", "dp"), None, None))
    shards = mesh.shape["sht"]
    table = polar_tables(64, shards)
    table_t = np.ascontiguousarray(table.transpose(0, 2, 1))

    def body(fields_in, cotangent, weights):
        return local(jnp.asarray(table), jnp.asarray(table_t), fields_in, cotangent, weights)

    return jax.shard_map(body, mesh=mesh, in_specs=in_specs, out_specs=out_specs, check_vma=False)
```

time: 872 us -> 263 us (0.30); the launches traced: 859 us -> 261 us
  waiting for transfers between devices: 435 us -> 43.2 us
  matrix products: 189 us -> 4.49 us
  blocking collectives: 42.8 us -> 147 us
  starting transfers between devices: 103 us -> 7.18 us
  local copies, waits for them, and re-layouts: 68.2 us -> 7.17 us
  Pallas kernels: 0 us -> 47.5 us
  between operations: 15.5 us -> 0.8 us
    reduce_scatter x1 -> x0, waiting for transfers between devices: 357 us -> none  [local(): lax.psum_scatter(accumulated, ('sht', 'dp'), scatter_dimension=0, tiled=T...]
    dot_general x55 -> x2, matrix products: 189 us -> 4.49 us  [product(): jnp.einsum('irc,ird->cd', owned[:, j], owned[:, j + 2], preferred_element...]
    all_to_all x3 -> x8, blocking collectives: 42.8 us -> 147 us  [turn(): return lax.all_to_all(value, 'sht', 0, 0, tiled=True)]
    all_to_all x17 -> x1, starting transfers between devices: 91.9 us -> 6.92 us  [local(): owned = lax.all_to_all(held, ('sht', 'dp'), 0, 0, tiled=True)]
    pallas_call x0 -> x9, Pallas kernels: none -> 47.5 us  [the longest x4 31.8 us: mix_call(): pl.pallas_call(body, grid_spec=pltpu.PrefetchScalarGridSpec(num_scalar_pr...]
    reshape x57 -> x0, local copies, waits for them, and re-layouts: 41.6 us -> none  [the longest x20 15.4 us: spectral_pass(): grid_part = grid_part.reshape(samples, latitudes, 2 * orders_here, channels)]
    all_to_all x17 -> x1, waiting for transfers between devices: 76.5 us -> 43.2 us  [local(): owned = lax.all_to_all(held, ('sht', 'dp'), 0, 0, tiled=True)]
    convert_element_type x20 -> x0, local copies, waits for them, and re-layouts: 17.8 us -> none  [the longest x10 11.3 us: spectral_pass(): spectral = jnp.einsum('sanc,nk->sakc', field_in, long_basis, preferred_el...]
  transfers between devices with their start and end apart: 26 -> 4, of which waited for: 15 -> 1; matrix products, arithmetic and copies ran while one was open for 18% -> 4% of each run, Pallas kernels for 0% -> 1%
where the time goes in v1:
time: 263 us; the launch traced here: 261 us
  blocking collectives  147 us (56%)
  Pallas kernels  47.5 us (18%)
  waiting for transfers between devices  43.2 us (16%)
  starting transfers between devices  7.18 us (3%)
  local copies, waits for them, and re-layouts  7.17 us (3%)
  matrix products  4.49 us (2%)
  other arithmetic  3.87 us (1%)
    all_to_all x8, blocking collectives, turn(): return lax.all_to_all(value, 'sht', 0, 0, tiled=True)  147 us
    all_to_all x1, waiting for transfers between devices, local(): owned = lax.all_to_all(held, ('sht', 'dp'), 0, 0, tiled=True)  43.2 us
    pallas_call x4, Pallas kernels, mix_call(): pl.pallas_call(body, grid_spec=pltpu.PrefetchScalarGridSpec(num_scalar_pr...  31.8 us
    pallas_call x5, Pallas kernels, grid_call(): pl.pallas_call(body, grid_spec=pltpu.PrefetchScalarGridSpec(num_scalar_pr...  15.7 us
    all_to_all x1, starting transfers between devices, local(): owned = lax.all_to_all(held, ('sht', 'dp'), 0, 0, tiled=True)  6.92 us
  transfers between devices with their start and end apart: 4, of which 1 were waited for; matrix products, arithmetic and copies ran while one was open for 4% of the time, Pallas kernels for 1%

profile of v1, /device:TPU:0, one launch (start us, length us, event | category | flops | bytes accessed | tf_op | source)
XLA Modules:
  0.0 261.1 jit_solution(276063657666970844)
XLA Ops:
  0.8 1.6 copy-done
  3.2 1.5 shard_map.86
  4.7 25.6 %all_to_all.45.refs_1_ = bf16[16,4,32,256]{3,2,1,0:T(8,128)(2,1)S(1)} all-to-all(bf16[16,4,32,256]{3,2,1,0:T(8,128)(2,1)S(1)} %shard_map.86), channel_id=1, replica_groups=mesh['section'=2,'sht'=16,'dp'=4] {'sht'}, dimensions={0} | all-to-all | bytes 2097152 | tf_op jit(solution)/shard_map/all_to_all | solution.py:285
  30.3 7.5 %shard_map.87 = (bf16[64,128,256]{2,1,0:T(8,128)(2,1)}, bf16[16,4,32,256]{3,2,1,0:T(8,128)(2,1)S(1)}) custom-call(s32[2]{0:T(128)S(1)} %pad_add_fusion.idx_ref.refs_0_, bf16[16,4,32,256]{3,2,1,0:T(8,128)(2,1)S(1)} %all_to_all.45.refs_1_, bf16[16,512,512]{2,1,0:T(8,128)(2,1)} %constant.25.clone.refs_2_, bf16[16,512,512]{2,1,0:T(8,128)(2,1)} %constant.26.clone.refs_3_, ...), custom_call_target="tpu_custom_call" | custom-call | tf_op jit(solution)/shard_map/pallas_call | solution.py:260
  37.8 19.7 %all_to_all.46.in_ref = bf16[16,4,32,256]{3,2,1,0:T(8,128)(2,1)S(1)} all-to-all(bf16[16,4,32,256]{3,2,1,0:T(8,128)(2,1)S(1)} %get-tuple-element.19), channel_id=1, replica_groups=mesh['section'=2,'sht'=16,'dp'=4] {'sht'}, dimensions={0} | all-to-all | bytes 2097152 | tf_op jit(solution)/shard_map/all_to_all | solution.py:285
  57.5 4.3 %shard_map.88 = (bf16[4,4,128,256]{3,2,1,0:T(8,128)(2,1)S(1)}, bf16[4,4,128,256]{3,2,1,0:T(8,128)(2,1)S(1)}, bf16[16,4,32,256]{3,2,1,0:T(8,128)(2,1)S(1)}) custom-call(s32[2]{0:T(128)S(1)} %pad_add_fusion.idx_ref.refs_0_, bf16[16,4,32,256]{3,2,1,0:T(8,128)(2,1)S(1)} %all_to_all.46.in_ref, bf16[8,4,128,256]{3,2,1,0:T(8,128)(2,1)} %field_ref.3, ...), custom_call_target="tpu_custom_call" | custom-call | tf_op jit(solution)/shard_map/pallas_call | solution.py:232
  61.9 19.2 %all_to_all.47.refs_1_ = bf16[16,4,32,256]{3,2,1,0:T(8,128)(2,1)S(1)} all-to-all(bf16[16,4,32,256]{3,2,1,0:T(8,128)(2,1)S(1)} %get-tuple-element.20), channel_id=1, replica_groups=mesh['section'=2,'sht'=16,'dp'=4] {'sht'}, dimensions={0} | all-to-all | bytes 2097152 | tf_op jit(solution)/shard_map/all_to_all | solution.py:285
  81.1 7.5 %shard_map.89 = (bf16[64,128,256]{2,1,0:T(8,128)(2,1)}, bf16[16,4,32,256]{3,2,1,0:T(8,128)(2,1)S(1)}) custom-call(s32[2]{0:T(128)S(1)} %pad_add_fusion.idx_ref.refs_0_, bf16[16,4,32,256]{3,2,1,0:T(8,128)(2,1)S(1)} %all_to_all.47.refs_1_, bf16[16,512,512]{2,1,0:T(8,128)(2,1)} %constant.25.clone.refs_2_, ...), custom_call_target="tpu_custom_call", output_to_operand_aliasing={{0}: (6, {})} | custom-call | tf_op jit(solution)/shard_map/pallas_call | solution.py:260
  88.6 17.9 %all_to_all.48.in_ref = bf16[16,4,32,256]{3,2,1,0:T(8,128)(2,1)S(1)} all-to-all(bf16[16,4,32,256]{3,2,1,0:T(8,128)(2,1)S(1)} %get-tuple-element.22), channel_id=1, replica_groups=mesh['section'=2,'sht'=16,'dp'=4] {'sht'}, dimensions={0} | all-to-all | bytes 2097152 | tf_op jit(solution)/shard_map/all_to_all | solution.py:285
  106.4 4.4 %shard_map.90 = (bf16[4,4,128,256]{3,2,1,0:T(8,128)(2,1)S(1)}, bf16[16,4,32,256]{3,2,1,0:T(8,128)(2,1)S(1)}) custom-call(s32[2]{0:T(128)S(1)} %pad_add_fusion.idx_ref.refs_0_, bf16[16,4,32,256]{3,2,1,0:T(8,128)(2,1)S(1)} %all_to_all.48.in_ref, bf16[4,4,128,256]{3,2,1,0:T(8,128)(2,1)S(1)} %get-tuple-element.23.h_ref, bf16[8,4,128,256]{3,2,1,0:T(8,128)(2,1)} %cot_ref.3, ...), custom_call_target="tpu_custom_call" | custom-call | tf_op jit(solution)/shard_map/pallas_call | solution.py:232
  110.9 16.8 %all_to_all.49.refs_1_ = bf16[16,4,32,256]{3,2,1,0:T(8,128)(2,1)S(1)} all-to-all(bf16[16,4,32,256]{3,2,1,0:T(8,128)(2,1)S(1)} %get-tuple-element.24), channel_id=1, replica_groups=mesh['section'=2,'sht'=16,'dp'=4] {'sht'}, dimensions={0} | all-to-all | bytes 2097152 | tf_op jit(solution)/shard_map/all_to_all | solution.py:285
  127.6 8.4 %shard_map.91 = (bf16[64,128,256]{2,1,0:T(8,128)(2,1)}, bf16[16,4,32,256]{3,2,1,0:T(8,128)(2,1)S(1)}) custom-call(s32[2]{0:T(128)S(1)} %pad_add_fusion.idx_ref.refs_0_, bf16[16,4,32,256]{3,2,1,0:T(8,128)(2,1)S(1)} %all_to_all.49.refs_1_, bf16[16,512,512]{2,1,0:T(8,128)(2,1)} %constant.25.clone.refs_2_, ...), custom_call_target="tpu_custom_call", output_to_operand_aliasing={{0}: (6, {})} | custom-call | tf_op jit(solution)/shard_map/pallas_call | solution.py:260
  136.0 16.0 %all_to_all.50.in_ref = bf16[16,4,32,256]{3,2,1,0:T(8,128)(2,1)S(1)} all-to-all(bf16[16,4,32,256]{3,2,1,0:T(8,128)(2,1)S(1)} %get-tuple-element.26), channel_id=1, replica_groups=mesh['section'=2,'sht'=16,'dp'=4] {'sht'}, dimensions={0} | all-to-all | bytes 2097152 | tf_op jit(solution)/shard_map/all_to_all | solution.py:285
  152.0 3.9 %shard_map.92 = (bf16[4,4,128,256]{3,2,1,0:T(8,128)(2,1)S(1)}, bf16[16,4,32,256]{3,2,1,0:T(8,128)(2,1)S(1)}) custom-call(s32[2]{0:T(128)S(1)} %pad_add_fusion.idx_ref.refs_0_, bf16[16,4,32,256]{3,2,1,0:T(8,128)(2,1)S(1)} %all_to_all.50.in_ref, bf16[8,4,128,256]{3,2,1,0:T(8,128)(2,1)} %cot_ref.3, bf16[4,4,128,256]{3,2,1,0:T(8,128)(2,1)S(1)} %get-tuple-element.27.slope_ref, ...), custom_call_target="tpu_custom_call" | custom-call | tf_op jit(solution)/shard_map/pallas_call | solution.py:232
  156.9 15.8 %all_to_all.51.refs_1_ = bf16[16,4,32,256]{3,2,1,0:T(8,128)(2,1)S(1)} all-to-all(bf16[16,4,32,256]{3,2,1,0:T(8,128)(2,1)S(1)} %get-tuple-element.28), channel_id=1, replica_groups=mesh['section'=2,'sht'=16,'dp'=4] {'sht'}, dimensions={0} | all-to-all | bytes 2097152 | tf_op jit(solution)/shard_map/all_to_all | solution.py:285
  172.7 8.4 %shard_map.93 = (bf16[64,128,256]{2,1,0:T(8,128)(2,1)}, bf16[16,4,32,256]{3,2,1,0:T(8,128)(2,1)S(1)}) custom-call(s32[2]{0:T(128)S(1)} %pad_add_fusion.idx_ref.refs_0_, bf16[16,4,32,256]{3,2,1,0:T(8,128)(2,1)S(1)} %all_to_all.51.refs_1_, bf16[16,512,512]{2,1,0:T(8,128)(2,1)} %constant.25.clone.refs_2_, ...), custom_call_target="tpu_custom_call", output_to_operand_aliasing={{0}: (6, {})} | custom-call | tf_op jit(solution)/shard_map/pallas_call | solution.py:260
  181.1 15.9 %all_to_all.52.in_ref = bf16[16,4,32,256]{3,2,1,0:T(8,128)(2,1)S(1)} all-to-all(bf16[16,4,32,256]{3,2,1,0:T(8,128)(2,1)S(1)} %get-tuple-element.30), channel_id=1, replica_groups=mesh['section'=2,'sht'=16,'dp'=4] {'sht'}, dimensions={0} | all-to-all | bytes 2097152 | tf_op jit(solution)/shard_map/all_to_all | solution.py:285
  197.0 6.9 %all-to-all-start.8 = ((bf16[64,128,256]{2,1,0:T(8,128)(2,1)}), bf16[64,128,256]{2,1,0:T(8,128)(2,1)}, u32[]{:S(2)}, u32[]{:S(2)}) async-start(bf16[64,128,256]{2,1,0:T(8,128)(2,1)} %get-tuple-element.35), calls=%async_computation.8 | async-start | bytes 8388608 | tf_op jit(solution)/shard_map/all_to_all | solution.py:324
  205.2 1.6 shard_map.94
  207.0 43.2 %all-to-all-done.8 = bf16[64,128,256]{2,1,0:T(8,128)(2,1)} async-done(((bf16[64,128,256]{2,1,0:T(8,128)(2,1)}), bf16[64,128,256]{2,1,0:T(8,128)(2,1)}, u32[]{:S(2)}, u32[]{:S(2)}) %all-to-all-start.8) | async-done | bytes 4194336 | tf_op jit(solution)/shard_map/all_to_all | solution.py:324
  250.1 2.6 %fusion = (bf16[64,1,32,256]{3,2,1,0:T(8,128)(2,1)S(1)}, bf16[64,1,32,256]{3,2,1,0:T(8,128)(2,1)S(1)}, bf16[64,1,32,256]{3,2,1,0:T(8,128)(2,1)S(1)}, bf16[64,1,32,256]{3,2,1,0:T(8,128)(2,1)S(1)}) fusion(bf16[64,4,32,256]{3,2,1,0:T(8,128)(2,1)} %bitcast.3), kind=kLoop, calls=%fused_computation.13 | loop fusion | bytes 8388608 | tf_op jit(solution)/shard_map/slice | solution.py:329
  252.8 2.2 convolution_bitcast_fusion.1
  255.0 2.2 broadcast_select_fusion.3
  258.8 1.5 maximum_bitcast_fusion
  (21 shorter events, 5.6 us)
Async XLA Ops:
  0.6 29.7 %collective-permute-start = (bf16[1,64,256,256]{3,2,1,0:T(8,128)(2,1)}, bf16[1,64,256,256]{3,2,1,0:T(8,128)(2,1)}, u32[]{:S(2)}, u32[]{:S(2)}) collective-permute-start(bf16[1,64,256,256]{3,2,1,0:T(8,128)(2,1)} %refs_4_.7), channel_id=1, source_target_pairs={{0,64},{64,0},{1,65},{65,1},{2,66},{66,2},{3,67},{67,3},{4,68},{68... | collective-permute-start | bytes 25165832 | tf_op jit(solution)/shard_map/ppermute | solution.py:287
  0.8 1.6 copy-start
  2.4 0.8 copy-start.4
  30.3 27.3 %copy-start.3 = (bf16[128,128]{1,0:T(8,128)(2,1)S(1)}, bf16[128,128]{1,0:T(8,128)(2,1)}, u32[]{:S(2)}) copy-start(bf16[128,128]{1,0:T(8,128)(2,1)} %constant.27.clone.syn_ref) | copy-start | bytes 98308
  30.3 27.3 %copy-start.5 = (bf16[128,128]{1,0:T(8,128)(2,1)S(1)}, bf16[128,128]{1,0:T(8,128)(2,1)}, u32[]{:S(2)}) copy-start(bf16[128,128]{1,0:T(8,128)(2,1)} %constant.28.clone.ana_ref) | copy-start | bytes 98308
  155.9 1.0 copy-start.1
  197.0 53.1 %all-to-all-start.8 = ((bf16[64,128,256]{2,1,0:T(8,128)(2,1)}), bf16[64,128,256]{2,1,0:T(8,128)(2,1)}, u32[]{:S(2)}, u32[]{:S(2)}) async-start(bf16[64,128,256]{2,1,0:T(8,128)(2,1)} %get-tuple-element.35), calls=%async_computation.8 | async-start | bytes 8388608 | tf_op jit(solution)/shard_map/all_to_all | solution.py:324
  204.0 1.2 copy-start.2
  206.9 50.5 %collective-permute-start.1 = (bf16[4,4,128,256]{3,2,1,0:T(8,128)(2,1)S(1)}, bf16[4,4,128,256]{3,2,1,0:T(8,128)(2,1)}, u32[]{:S(2)}, u32[]{:S(2)}) collective-permute-start(bf16[4,4,128,256]{3,2,1,0:T(8,128)(2,1)S(1)} %broadcast_select_fusion.2), channel_id=1, source_target_pairs={{0,64},{64,0},{1,65},{65,1},{2,66},{66,2},{3,67},{67,3},{4,68},{68... | collective-permute-start | bytes 3145736 | tf_op jit(solution)/shard_map/ppermute | solution.py:319
  257.3 3.0 %collective-permute-start.2 = (f32[256,256]{1,0:T(8,128)S(1)}, f32[256,256]{1,0:T(8,128)S(1)}, u32[]{:S(2)}, u32[]{:S(2)}) collective-permute-start(f32[256,256]{1,0:T(8,128)S(1)} %get-tuple-element.42), channel_id=1, source_target_pairs={{0,64},{64,0},{1,65},{65,1},{2,66},{66,2},{3,67},{67,3},{4,68},{68... | collective-permute-start | bytes 786440 | tf_op jit(solution)/shard_map/ppermute | solution.py:335

commit v2 on v0

v2 whole, which is shorter than its diff:
```python
import math

import jax
import jax.numpy as jnp
import ml_dtypes
import numpy as np
from jax import lax
from jax.experimental import pallas as pl
from jax.experimental.pallas import tpu as pltpu
from jax.sharding import Mesh
from jax.sharding import PartitionSpec as P

BF16 = jnp.bfloat16
F32 = jnp.float32


def gauss_nodes(resolution):
    counter = np.arange(resolution) * 1.0
    guesses = np.cos(math.pi * (counter + 0.75) / (resolution + 0.5))
    for sweep in range(100):
        current = np.ones(resolution)
        previous = np.zeros(resolution)
        for degree in range(1, resolution + 1):
            following = (
                (2.0 * degree - 1.0) * guesses * current - (degree - 1.0) * previous
            ) / degree
            previous = current
            current = following
        slope_val = resolution * (guesses * current - previous) / (guesses * guesses - 1.0)
        guesses = guesses - current / slope_val
    current = np.ones(resolution)
    previous = np.zeros(resolution)
    for degree in range(1, resolution + 1):
        following = ((2.0 * degree - 1.0) * guesses * current - (degree - 1.0) * previous) / degree
        previous = current
        current = following
    slope_val = resolution * (guesses * current - previous) / (guesses * guesses - 1.0)
    weights_q = 2.0 / ((1.0 - guesses * guesses) * slope_val * slope_val)
    return (guesses[::-1].copy(), weights_q[::-1].copy())


def legendre_table(resolution):
    points, quadrature = gauss_nodes(resolution)
    sine_row = np.sqrt(1.0 - points * points)
    basis = np.zeros((resolution, resolution, resolution))
    diagonal = np.full(resolution, math.sqrt(1.0 / (4.0 * math.pi)))
    for harmonic in range(resolution):
        if harmonic > 0:
            diagonal = diagonal * sine_row * math.sqrt((2.0 * harmonic + 1.0) / (2.0 * harmonic))
        basis[harmonic, harmonic] = diagonal
        if harmonic + 1 < resolution:
            basis[harmonic, harmonic + 1] = points * math.sqrt(2.0 * harmonic + 3.0) * diagonal
        for degree in range(harmonic + 2, resolution):
            alpha_coef = math.sqrt(
                (4.0 * degree * degree - 1.0) / (degree * degree - harmonic * harmonic)
            )
            beta_coef = math.sqrt(
                ((degree - 1.0) ** 2 - harmonic * harmonic) / (4.0 * (degree - 1.0) ** 2 - 1.0)
            )
            basis[harmonic, degree] = alpha_coef * (
                points * basis[harmonic, degree - 1] - beta_coef * basis[harmonic, degree - 2]
            )
    return basis * np.sqrt(2.0 * math.pi * quadrature)[None, None, :]


def longitude_table(longitudes, degrees):
    column = np.arange(2 * degrees)
    harmonic, parity = column // 2, column % 2
    phase = (np.arange(longitudes)[:, None] * harmonic[None, :]) % longitudes
    angles = phase.astype(np.float32) * np.float32(2.0 * math.pi / longitudes)
    scales = np.where(harmonic == 0, 1.0 / math.sqrt(longitudes), math.sqrt(2.0 / longitudes))
    basis = np.where(parity[None, :] == 0, np.cos(angles), -np.sin(angles))
    return (basis * scales[None, :].astype(np.float32)).astype(ml_dtypes.bfloat16)


SLOTS = 72


def pair_degrees(degrees, blocks):
    quarter = degrees // 16
    return np.array(
        [
            16 * (r // quarter) + quarter * x + r % quarter
            for x in range(blocks)
            for r in range(degrees // 2 // blocks)
        ]
    )


def polar_tables(degrees, blocks):
    leg = legendre_table(degrees).astype(np.float32).astype(ml_dtypes.bfloat16)
    low = pair_degrees(degrees, blocks)
    pairs = degrees // 2
    ana = np.zeros((degrees + 1, 2, pairs, 2, pairs), ml_dtypes.bfloat16)
    syn = np.zeros((degrees, 2, pairs, 2, pairs), ml_dtypes.bfloat16)
    for half in range(2):
        for g, l in enumerate(low):
            for pos in range(degrees + 1):
                if l >= pos:
                    ana[pos, half, g, 0] = leg[pos, l, half::2]
                else:
                    ana[pos, half, g, 1] = leg[degrees - pos, degrees - 1 - l, half::2]
            for m in range(degrees):
                if l >= m:
                    syn[m, half, :, 0, g] = leg[m, l, half::2]
                if degrees - 1 - l >= m:
                    syn[m, half, :, 1, g] = leg[m, degrees - 1 - l, half::2]
    size = (2 * pairs, 2 * pairs)
    return ana.reshape((degrees + 1,) + size), syn.reshape((degrees,) + size)


def params(megabytes=48):
    return pltpu.CompilerParams(vmem_limit_bytes=megabytes * 2**20)


def dot(left, right):
    return jnp.dot(left, right, preferred_element_type=F32)


def normal_cdf(values):
    return 0.5 * (1.0 + lax.erf(values * (1.0 / math.sqrt(2.0))))


def low_lanes(shape):
    return lax.broadcasted_iota(jnp.int32, shape, len(shape) - 1) < shape[-1] // 2


def turned(value):
    return pltpu.roll(value, value.shape[-1] // 2, value.ndim - 1)


def interleave(first, second):
    low = low_lanes(first.shape)
    return jnp.where(low, first, turned(second)), jnp.where(low, turned(first), second)


def pack_body(idx_ref, field_ref, out_ref):
    _, rows, _, channels = field_ref.shape
    for q in range(rows // 2):
        one = field_ref[0, 2 * q].astype(F32)
        two = field_ref[0, 2 * q + 1].astype(F32)
        for t in range(channels // 128):
            span = slice(t * 128, (t + 1) * 128)
            left, right = interleave(one[:, span], two[:, span])
            out_ref[2 * t, q] = left.astype(BF16)
            out_ref[2 * t + 1, q] = right.astype(BF16)


def unpack_body(idx_ref, own_ref, far_ref, out_ref):
    _, rows, _, channels = out_ref.shape
    mine = (pl.program_id(0) // 4) == idx_ref[1]

    def write(ref):
        for q in range(rows // 2):
            for t in range(channels // 128):
                span = slice(t * 128, (t + 1) * 128)
                one, two = interleave(ref[2 * t, q].astype(F32), ref[2 * t + 1, q].astype(F32))
                out_ref[0, 2 * q, :, span] = one.astype(BF16)
                out_ref[0, 2 * q + 1, :, span] = two.astype(BF16)

    @pl.when(mine)
    def _():
        write(own_ref)

    @pl.when(jnp.logical_not(mine))
    def _():
        write(far_ref)


def repeat(count, body, unroll):
    def step(i, carry):
        body(i)
        return carry

    lax.fori_loop(0, count, step, 0, unroll=unroll)


def store_spectrum(q, value, spec_ref):
    spec_ref[pl.ds(q, 128, stride=32), :] = value


def analyse(spec_ref, table_ref, slot_ref, out_ref):
    degrees = table_ref.shape[0] - 1
    pairs = degrees // 2

    def slot(pos):
        m0 = jnp.minimum(pos, degrees - 1)
        m1 = jnp.minimum(degrees - pos, degrees - 1)
        one = spec_ref[pl.ds(pl.multiple_of(m0 * 64, 64), 64), :].astype(BF16)
        two = spec_ref[pl.ds(pl.multiple_of(m1 * 64, 64), 64), :].astype(BF16)
        right = jnp.concatenate(
            [
                jnp.concatenate([one[:pairs], two[:pairs]], axis=0),
                jnp.concatenate([one[pairs:], two[pairs:]], axis=0),
            ],
            axis=1,
        )
        both = dot(table_ref[pos], right)
        even, odd = both[:pairs], both[pairs:]
        low = low_lanes((pairs, 128))
        value = jnp.where(low, even[:, :128], odd[:, 128:]) + turned(
            jnp.where(low, even[:, 128:], odd[:, :128])
        )
        slot_ref[pl.ds(pos, pairs, stride=SLOTS), :] = value

    repeat(degrees + 1, slot, 5)
    for pos in range(degrees + 1, SLOTS):
        slot_ref[pl.ds(pos, pairs, stride=SLOTS), :] = jnp.zeros((pairs, 128), F32)
    blocks, rows, _ = out_ref.shape
    for b in range(blocks):
        out_ref[b] = slot_ref[b * rows : (b + 1) * rows, :].astype(BF16)


def synthesise(in_ref, table_ref, slot_ref, grid_ref):
    degrees = table_ref.shape[0]
    pairs = degrees // 2
    blocks, rows, _ = in_ref.shape
    for b in range(blocks):
        slot_ref[b * rows : (b + 1) * rows, :] = in_ref[b].astype(F32)

    def order(m):
        one = slot_ref[pl.ds(m, pairs, stride=SLOTS), :]
        two = slot_ref[pl.ds(degrees - m, pairs, stride=SLOTS), :]
        both = dot(table_ref[m], jnp.concatenate([one, two], axis=0).astype(BF16))
        real, imag = interleave(both[:pairs], both[pairs:])
        grid_ref[pl.ds(2 * m, pairs, stride=2 * degrees), :] = real
        grid_ref[pl.ds(2 * m + 1, pairs, stride=2 * degrees), :] = imag

    repeat(degrees, order, 4)


def spectrum_at(q, grid_ref):
    return grid_ref[pl.ds(pl.multiple_of(q * 128, 128), 128), :].astype(BF16)


def first_body(field_ref, ana_ref, ta_ref, out_ref, spec_ref, slot_ref):
    basis = ana_ref[...]
    repeat(field_ref.shape[0], lambda q: store_spectrum(q, dot(basis, field_ref[q]), spec_ref), 4)
    analyse(spec_ref, ta_ref, slot_ref, out_ref)


def layer0_body(in_ref, field_ref, syn_ref, ana_ref, ts_ref, ta_ref, h_ref, slope_ref, out_ref,
                spec_ref, grid_ref, slot_ref):
    synthesise(in_ref, ts_ref, slot_ref, grid_ref)
    syn, ana = syn_ref[...], ana_ref[...]

    def row(q):
        pre = dot(syn, spectrum_at(q, grid_ref))
        cdf = normal_cdf(pre)
        density = jnp.exp(-0.5 * pre * pre) * (1.0 / math.sqrt(2.0 * math.pi))
        slope_ref[q] = (cdf + pre * density).astype(BF16)
        h = (field_ref[q].astype(F32) + pre * cdf).astype(BF16)
        h_ref[q] = h
        store_spectrum(q, dot(ana, h), spec_ref)

    repeat(field_ref.shape[0], row, 2)
    analyse(spec_ref, ta_ref, slot_ref, out_ref)


def layer1_body(in_ref, h_ref, cot_ref, syn_ref, ana_ref, ts_ref, ta_ref, top_ref, out_ref,
                spec_ref, grid_ref, slot_ref):
    synthesise(in_ref, ts_ref, slot_ref, grid_ref)
    syn, ana = syn_ref[...], ana_ref[...]

    def row(q):
        pre = dot(syn, spectrum_at(q, grid_ref))
        cdf = normal_cdf(pre)
        density = jnp.exp(-0.5 * pre * pre) * (1.0 / math.sqrt(2.0 * math.pi))
        top_ref[q] = (h_ref[q].astype(F32) + pre * cdf).astype(BF16)
        gpre = (cot_ref[q].astype(F32) * (cdf + pre * density)).astype(BF16)
        store_spectrum(q, dot(ana, gpre), spec_ref)

    repeat(h_ref.shape[0], row, 2)
    analyse(spec_ref, ta_ref, slot_ref, out_ref)


def back1_body(in_ref, cot_ref, slope_ref, syn_ref, ana_ref, ts_ref, ta_ref, g_ref, out_ref,
               spec_ref, grid_ref, slot_ref):
    synthesise(in_ref, ts_ref, slot_ref, grid_ref)
    syn, ana = syn_ref[...], ana_ref[...]

    def row(q):
        g = (cot_ref[q].astype(F32) + dot(syn, spectrum_at(q, grid_ref))).astype(BF16)
        g_ref[q] = g
        gpre = (g.astype(F32) * slope_ref[q].astype(F32)).astype(BF16)
        store_spectrum(q, dot(ana, gpre), spec_ref)

    repeat(cot_ref.shape[0], row, 2)
    analyse(spec_ref, ta_ref, slot_ref, out_ref)


def back0_body(in_ref, g_ref, syn_ref, ts_ref, out_ref, grid_ref, slot_ref):
    synthesise(in_ref, ts_ref, slot_ref, grid_ref)
    syn = syn_ref[...]

    def row(q):
        out_ref[q] = (g_ref[q].astype(F32) + dot(syn, spectrum_at(q, grid_ref))).astype(BF16)

    repeat(g_ref.shape[0], row, 2)


def mix_body(layer, backward, idx_ref, in_ref, own_ref, far_ref, *rest):
    if backward:
        coef_ref, out_ref, grad_ref, w_ref, sem = rest
    else:
        out_ref, coef_ref, w_ref, sem = rest
    pairs = w_ref.shape[1]
    mine = idx_ref[1] == layer

    def fetch(source):
        return pltpu.make_async_copy(source, w_ref, sem)

    @pl.when(mine)
    def _():
        fetch(own_ref).start()

    @pl.when(jnp.logical_not(mine))
    def _():
        fetch(far_ref).start()

    contract = (((1,), (1 if backward else 0,)), ((), ()))
    rows = 2 * SLOTS
    index = lax.broadcasted_iota(jnp.int32, (rows, 256), 0)
    pos = jnp.where(index < SLOTS, index, index - SLOTS)
    stacks = []
    for rr in range(pairs // 2):
        span = slice(rr * rows, (rr + 1) * rows)
        blocks = [in_ref[b, span].astype(F32) for b in range(4)]
        a0, a1 = interleave(blocks[0], blocks[1])
        b0, b1 = interleave(blocks[2], blocks[3])
        real = jnp.concatenate([a0, b0], axis=1)
        imag = jnp.concatenate([a1, b1], axis=1)
        for i in range(2):
            part = slice(i * SLOTS, (i + 1) * SLOTS)
            stack = jnp.concatenate([real[part], imag[part]], axis=0)
            stacks.append(stack)
            if not backward:
                coef_ref[2 * rr + i] = stack.astype(BF16)
    fetch(own_ref).wait()
    for rr in range(pairs // 2):
        span = slice(rr * rows, (rr + 1) * rows)
        real, imag = [], []
        for r in (2 * rr, 2 * rr + 1):
            stack = stacks[r]
            narrow = stack.astype(BF16)
            lower = pos <= 16 * (r // 4) + r % 4 + 4 * idx_ref[0]
            one = lax.dot_general(narrow, w_ref[0, r], contract, preferred_element_type=F32)
            two = lax.dot_general(
                narrow, w_ref[1, pairs - 1 - r], contract, preferred_element_type=F32
            )
            mixed = jnp.where(lower, one, two)
            real.append(mixed[:SLOTS])
            imag.append(mixed[SLOTS:])
            if backward:
                over = (((0,), (0,)), ((), ()))
                first = jnp.where(lower, stack, 0.0).astype(BF16)
                second = jnp.where(lower, 0.0, stack).astype(BF16)
                for place, piece in ((r, first), (2 * pairs - 1 - r, second)):
                    grad = lax.dot_general(coef_ref[r], piece, over, preferred_element_type=F32)
                    grad_ref[place] = grad.astype(BF16)
        real = jnp.concatenate(real, axis=0)
        imag = jnp.concatenate(imag, axis=0)
        for t in range(2):
            lanes = slice(t * 128, (t + 1) * 128)
            left, right = interleave(real[:, lanes], imag[:, lanes])
            out_ref[2 * t, span] = left.astype(BF16)
            out_ref[2 * t + 1, span] = right.astype(BF16)


def local(ta, ts, fields_in, cotangent, weights):
    rows_all, lat_rows, longitudes, channels = fields_in.shape
    degrees = longitudes // 2
    samples = rows_all // 2
    section = lax.axis_index("section")
    x_at, z_at = lax.axis_index("x"), lax.axis_index("z")
    idx = jnp.stack([x_at, section]).astype(jnp.int32)
    syn_np = longitude_table(longitudes, degrees)
    syn = jnp.asarray(syn_np)
    ana = jnp.asarray(np.ascontiguousarray(syn_np.T))
    swap = [(0, 1), (1, 0)]
    pairs = degrees // 2
    q_rows = lat_rows // 2
    block_rows = pairs // 4 * SLOTS

    packed_block = pl.BlockSpec((4, q_rows, longitudes, 128), lambda s, i: (s, 0, 0, 0))
    packed_shape = jax.ShapeDtypeStruct((16, q_rows, longitudes, 128), BF16)
    grid_shape = jax.ShapeDtypeStruct((pairs, longitudes, 128), BF16)
    spec_shape = jax.ShapeDtypeStruct((4, block_rows, 128), BF16)

    def pack(field):
        block = (1, lat_rows, longitudes, channels)
        return pl.pallas_call(
            pack_body,
            grid_spec=pltpu.PrefetchScalarGridSpec(
                num_scalar_prefetch=1,
                grid=(samples,),
                in_specs=[pl.BlockSpec(block, lambda s, i: (s + i[1] * samples, 0, 0, 0))],
                out_specs=packed_block,
            ),
            out_shape=packed_shape,
            compiler_params=params(),
        )(idx, field)

    def unpack(own, far):
        block = (1, lat_rows, longitudes, channels)
        held = pl.BlockSpec(
            (4, q_rows, longitudes, 128), lambda s, i: (lax.rem(s, samples), 0, 0, 0)
        )
        return pl.pallas_call(
            unpack_body,
            grid_spec=pltpu.PrefetchScalarGridSpec(
                num_scalar_prefetch=1,
                grid=(rows_all,),
                in_specs=[held, held],
                out_specs=pl.BlockSpec(block, lambda s, i: (s, 0, 0, 0)),
            ),
            out_shape=jax.ShapeDtypeStruct(fields_in.shape, BF16),
            compiler_params=params(),
        )(idx, own, far)

    def to_local(field):
        return lax.all_to_all(pack(field), ("z", "x"), 0, 0, tiled=True).reshape(grid_shape.shape)

    def to_rows(value):
        return lax.all_to_all(value.reshape(packed_shape.shape), ("z", "x"), 0, 0, tiled=True)

    def turn(value):
        return lax.all_to_all(value, "x", 0, 0, tiled=True)

    tall = pltpu.VMEM((pairs * 128, 128), F32)
    slots = pltpu.VMEM((pairs * SLOTS, 128), F32)

    def grid_call(body, shapes, scratch, *args):
        return pl.pallas_call(
            body, out_shape=shapes, scratch_shapes=scratch, compiler_params=params()
        )(*args)

    vmem = pl.BlockSpec(memory_space=pltpu.VMEM)
    anywhere = pl.BlockSpec(memory_space=pl.ANY)
    coef_shape = jax.ShapeDtypeStruct((pairs // 4, 2 * SLOTS, channels), BF16)
    grad_shape = jax.ShapeDtypeStruct((degrees // 4, channels, channels), BF16)

    def mix_call(layer, value, own, far, coef=None):
        backward = coef is not None

        def body(*refs):
            mix_body(layer, backward, *refs)

        return pl.pallas_call(
            body,
            in_specs=[pl.BlockSpec(memory_space=pltpu.SMEM), vmem, anywhere, anywhere]
            + [vmem] * backward,
            out_specs=[vmem, vmem],
            out_shape=[spec_shape, grad_shape if backward else coef_shape],
            scratch_shapes=[
                pltpu.VMEM((2, pairs // 4, channels, channels), BF16),
                pltpu.SemaphoreType.DMA,
            ],
            compiler_params=params(),
        )(idx, value, own, far, *([coef] if backward else []))

    folded = weights[0].reshape(4, 4, 4, channels, channels)
    low = lax.dynamic_index_in_dim(folded[:2], x_at, 1, keepdims=False)
    high = lax.dynamic_index_in_dim(folded[2:], 3 - x_at, 1, keepdims=False)
    own = jnp.stack([low, high]).reshape(2, pairs // 4, channels, channels)
    far = lax.ppermute(own, "section", swap)

    front = section == 0

    def reduce_first(grad):
        halves = grad.reshape(degrees // 4, 2, channels // 2, channels)
        keep = lax.dynamic_index_in_dim(halves, section, 1, keepdims=False)
        give = lax.dynamic_index_in_dim(halves, 1 - section, 1, keepdims=False)
        got = lax.ppermute(give, "section", swap)
        both = (keep.astype(F32) + got.astype(F32)).astype(BF16)
        parts = lax.all_to_all(both, ("z", "dp"), 0, 0, tiled=True)
        return jnp.sum(parts.astype(F32), axis=0)

    field = to_local(fields_in)
    value = grid_call(first_body, spec_shape, [tall, slots], field, ana, ta)
    cot = to_local(cotangent)
    value, coef0 = mix_call(0, turn(value), own, far)
    h1, slope, value = grid_call(
        layer0_body, [grid_shape, grid_shape, spec_shape], [tall, tall, slots],
        turn(value), field, syn, ana, ts, ta,
    )
    value, coef1 = mix_call(1, turn(value), own, far)
    top, value = grid_call(
        layer1_body, [grid_shape, spec_shape], [tall, tall, slots],
        turn(value), h1, cot, syn, ana, ts, ta,
    )
    value, grad1 = mix_call(1, turn(value), own, far, coef1)
    g1, value = grid_call(
        back1_body, [grid_shape, spec_shape], [tall, tall, slots],
        turn(value), cot, slope, syn, ana, ts, ta,
    )
    value, grad0 = mix_call(0, turn(value), own, far, coef0)
    bottom = grid_call(
        back0_body, grid_shape, [tall, slots], turn(value), g1, syn, ts
    )
    top = to_rows(top)
    bottom = to_rows(bottom)
    passed = lax.ppermute(jnp.where(front, top, bottom), "section", swap)
    section_ends = unpack(jnp.where(front, bottom, top), passed)[None]

    sum1, sum0 = reduce_first(grad1), reduce_first(grad0)
    mine = jnp.where(front, sum0, sum1)
    other = lax.ppermute(jnp.where(front, sum1, sum0), "section", swap)
    total = jnp.concatenate([jnp.where(front, mine, other), jnp.where(front, other, mine)], axis=0)
    flipped = lax.ppermute(total, "x", [(i, 3 - i) for i in range(4)])
    total = jnp.where(z_at < 2, total, flipped)
    batch_count = rows_all * lax.axis_size("dp")
    return (section_ends, (total / batch_count)[None, None])


def solution(mesh):
    grid = Mesh(mesh.devices.reshape(2, 4, 4, 4), ("section", "z", "x", "dp"))
    rows = P("dp", ("z", "x"), None, None)
    in_specs = (rows, rows, P("section", None, None, None))
    out_specs = (
        P("section", "dp", ("z", "x"), None, None),
        P("section", ("z", "x", "dp"), None, None),
    )
    ta, ts = polar_tables(64, 4)

    def body(fields_in, cotangent, weights):
        return local(jnp.asarray(ta), jnp.asarray(ts), fields_in, cotangent, weights)

    return jax.shard_map(body, mesh=grid, in_specs=in_specs, out_specs=out_specs, check_vma=False)
```

time: 872 us -> 321 us (0.37); the launches traced: 859 us -> 320 us
  waiting for transfers between devices: 435 us -> 77.1 us
  matrix products: 189 us -> 0 us
  Pallas kernels: 0 us -> 81 us
  starting transfers between devices: 103 us -> 35.9 us
  blocking collectives: 42.8 us -> 83.8 us
  local copies, waits for them, and re-layouts: 68.2 us -> 29.3 us
  between operations: 15.5 us -> 0.98 us
    reduce_scatter x1 -> x0, waiting for transfers between devices: 357 us -> none  [local(): lax.psum_scatter(accumulated, ('sht', 'dp'), scatter_dimension=0, tiled=T...]
    dot_general x55 -> x0, matrix products: 189 us -> none  [the longest x5 66.6 us: degree_products(): jnp.einsum('mlspc,mlspd->lcd', left_side, right_side, preferred_element_t...]
    pallas_call x0 -> x12, Pallas kernels: none -> 81 us  [the longest x5 63.7 us: grid_call(): pl.pallas_call(body, out_shape=shapes, scratch_shapes=scratch, compiler_p...]
    all_to_all x17 -> x8, starting transfers between devices: 91.9 us -> 34.6 us  [the longest x3 11.8 us: turn(): return lax.all_to_all(value, 'x', 0, 0, tiled=True)]
    reshape x57 -> x0, local copies, waits for them, and re-layouts: 41.6 us -> none  [the longest x20 15.4 us: spectral_pass(): grid_part = grid_part.reshape(samples, latitudes, 2 * orders_here, channels)]
    all_to_all x3 -> x6, blocking collectives: 42.8 us -> 83.8 us  [the longest x5 58.2 us: turn(): return lax.all_to_all(value, 'x', 0, 0, tiled=True)]
    convert_element_type x20 -> x0, local copies, waits for them, and re-layouts: 17.8 us -> none  [the longest x10 11.3 us: spectral_pass(): spectral = jnp.einsum('sanc,nk->sakc', field_in, long_basis, preferred_el...]
    unnamed x28 -> x50, local copies, waits for them, and re-layouts: 3.01 us -> 16 us
  transfers between devices with their start and end apart: 26 -> 14, of which waited for: 15 -> 10; matrix products, arithmetic and copies ran while one was open for 18% -> 5% of each run, Pallas kernels for 0% -> 7%
where the time goes in v2:
time: 321 us; the launch traced here: 320 us
  blocking collectives  83.8 us (26%)
  Pallas kernels  81 us (25%)
  waiting for transfers between devices  77.1 us (24%)
  starting transfers between devices  35.9 us (11%)
  local copies, waits for them, and re-layouts  29.3 us (9%)
  other arithmetic  11.5 us (4%)
    pallas_call x5, Pallas kernels, grid_call(): pl.pallas_call(body, out_shape=shapes, scratch_shapes=scratch, compiler_p...  63.7 us
    all_to_all x5, blocking collectives, turn(): return lax.all_to_all(value, 'x', 0, 0, tiled=True)  58.2 us
    all_to_all x1, blocking collectives, to_local(): lax.all_to_all(pack(field), ('z', 'x'), 0, 0, tiled=True)  25.6 us
    all_to_all x3, waiting for transfers between devices, turn(): return lax.all_to_all(value, 'x', 0, 0, tiled=True)  21 us
    all_to_all x2, waiting for transfers between devices, to_rows(): lax.all_to_all(value.reshape(packed_shape.shape), ('z', 'x'), 0, 0, tiled...  19.3 us
    all_to_all x2, waiting for transfers between devices, reduce_first(): parts = lax.all_to_all(both, ('z', 'dp'), 0, 0, tiled=True)  16.8 us
    unnamed x50, local copies, waits for them, and re-layouts  16 us
    all_to_all x3, starting transfers between devices, turn(): return lax.all_to_all(value, 'x', 0, 0, tiled=True)  11.8 us
  transfers between devices with their start and end apart: 14, of which 10 were waited for; matrix products, arithmetic and copies ran while one was open for 5% of the time, Pallas kernels for 7%

profile of v2, /device:TPU:0, one launch (start us, length us, event | category | flops | bytes accessed | tf_op | source)
XLA Modules:
  0.0 319.6 jit_solution(5431163033079349764)
XLA Ops:
  0.6 6.0 %fusion.2 = (bf16[1,32,256,256]{3,2,1,0:T(8,128)(2,1)}, bf16[1,32,256,256]{3,2,1,0:T(8,128)(2,1)}) fusion(bf16[1,64,256,256]{3,2,1,0:T(8,128)(2,1)} %param.9), kind=kLoop, calls=%fused_computation.20 | loop fusion | bytes 16777216 | tf_op jit(solution)/shard_map/slice | solution.py:463
  12.3 25.6 %all_to_all.70 = bf16[16,2,128,128]{3,2,1,0:T(8,128)(2,1)S(1)} all-to-all(bf16[16,2,128,128]{3,2,1,0:T(8,128)(2,1)S(1)} %shard_map.86), channel_id=1, replica_groups=mesh['section'=2,'z'=4,'x'=4,'dp'=4] {'z','x'}, dimensions={0} | all-to-all | bytes 2097152 | tf_op jit(solution)/shard_map/all_to_all | solution.py:422
  38.0 5.9 %shard_map.87 = bf16[4,576,128]{2,1,0:T(8,128)(2,1)S(1)} custom-call(bf16[32,128,128]{2,1,0:T(8,128)(2,1)S(1)} %bitcast.29, bf16[128,128]{1,0:T(8,128)(2,1)S(1)} %copy-done.24, bf16[65,64,64]{2,1,0:T(8,128)(2,1)S(1)} %copy-done), custom_call_target="tpu_custom_call" | custom-call | tf_op jit(solution)/shard_map/pallas_call | solution.py:434
  43.8 12.2 %all_to_all.71.refs_1_ = bf16[4,576,128]{2,1,0:T(8,128)(2,1)S(1)} all-to-all(bf16[4,576,128]{2,1,0:T(8,128)(2,1)S(1)} %shard_map.87), channel_id=1, replica_groups=mesh['section'=2,'z'=4,'x'=4,'dp'=4] {'x'}, dimensions={0} | all-to-all | bytes 1179648 | tf_op jit(solution)/shard_map/all_to_all | solution.py:428
  58.5 12.5 %all_to_all.72.in_ref = bf16[4,576,128]{2,1,0:T(8,128)(2,1)S(1)} all-to-all(bf16[4,576,128]{2,1,0:T(8,128)(2,1)S(1)} %get-tuple-element.17), channel_id=1, replica_groups=mesh['section'=2,'z'=4,'x'=4,'dp'=4] {'x'}, dimensions={0} | all-to-all | bytes 1179648 | tf_op jit(solution)/shard_map/all_to_all | solution.py:428
  70.9 16.3 %shard_map.89 = (bf16[32,128,128]{2,1,0:T(8,128)(2,1)S(1)}, bf16[32,128,128]{2,1,0:T(8,128)(2,1)S(1)}, bf16[4,576,128]{2,1,0:T(8,128)(2,1)S(1)}) custom-call(bf16[4,576,128]{2,1,0:T(8,128)(2,1)S(1)} %all_to_all.72.in_ref, bf16[32,128,128]{2,1,0:T(8,128)(2,1)S(1)} %bitcast.30, bf16[128,128]{1,0:T(8,128)(2,1)S(1)} %copy-done.23, ...), custom_call_target="tpu_custom_call" | custom-call | tf_op jit(solution)/shard_map/pallas_call | solution.py:434
  98.0 5.2 %all-to-all-done.3.refs_1_ = bf16[4,576,128]{2,1,0:T(8,128)(2,1)} async-done(((bf16[4,576,128]{2,1,0:T(8,128)(2,1)}), bf16[4,576,128]{2,1,0:T(8,128)(2,1)}, u32[]{:S(2)}, u32[]{:S(2)}) %all-to-all-start.3) | async-done | bytes 589856 | tf_op jit(solution)/shard_map/all_to_all | solution.py:428
  103.1 4.3 %all-to-all-start.5 = ((bf16[16,2,128,128]{3,2,1,0:T(8,128)(2,1)}), bf16[16,2,128,128]{3,2,1,0:T(8,128)(2,1)}, u32[]{:S(2)}, u32[]{:S(2)}) async-start(bf16[16,2,128,128]{3,2,1,0:T(8,128)(2,1)} %copy-done.2), calls=%async_computation.5 | async-start | bytes 2097152 | tf_op jit(solution)/shard_map/all_to_all | solution.py:422
  112.4 10.2 %all-to-all-done.5 = bf16[16,2,128,128]{3,2,1,0:T(8,128)(2,1)} async-done(((bf16[16,2,128,128]{3,2,1,0:T(8,128)(2,1)}), bf16[16,2,128,128]{3,2,1,0:T(8,128)(2,1)}, u32[]{:S(2)}, u32[]{:S(2)}) %all-to-all-start.5) | async-done | bytes 1048608 | tf_op jit(solution)/shard_map/all_to_all | solution.py:422
  122.6 11.9 %all_to_all.73.in_ref = bf16[4,576,128]{2,1,0:T(8,128)(2,1)S(1)} all-to-all(bf16[4,576,128]{2,1,0:T(8,128)(2,1)} %copy-done.18), channel_id=1, replica_groups=mesh['section'=2,'z'=4,'x'=4,'dp'=4] {'x'}, dimensions={0} | all-to-all | bytes 1179648 | tf_op jit(solution)/shard_map/all_to_all | solution.py:428
  135.7 16.9 %shard_map.92 = (bf16[32,128,128]{2,1,0:T(8,128)(2,1)S(1)}, bf16[4,576,128]{2,1,0:T(8,128)(2,1)S(1)}) custom-call(bf16[4,576,128]{2,1,0:T(8,128)(2,1)S(1)} %all_to_all.73.in_ref, bf16[32,128,128]{2,1,0:T(8,128)(2,1)S(1)} %copy-done.13, bf16[32,128,128]{2,1,0:T(8,128)(2,1)} %bitcast.7.cot_ref, bf16[128,128]{1,0:T(8,128)(2,1)S(1)} %copy-done.23, ...), custom_call_target="tpu_custom_call" | custom-call | tf_op jit(solution)/shard_map/pallas_call | solution.py:434
  152.6 10.8 %all_to_all.74.refs_1_ = bf16[4,576,128]{2,1,0:T(8,128)(2,1)S(1)} all-to-all(bf16[4,576,128]{2,1,0:T(8,128)(2,1)S(1)} %get-tuple-element.21), channel_id=1, replica_groups=mesh['section'=2,'z'=4,'x'=4,'dp'=4] {'x'}, dimensions={0} | all-to-all | bytes 1179648 | tf_op jit(solution)/shard_map/all_to_all | solution.py:428
  168.2 10.8 %all_to_all.75.in_ref = bf16[4,576,128]{2,1,0:T(8,128)(2,1)S(1)} all-to-all(bf16[4,576,128]{2,1,0:T(8,128)(2,1)S(1)} %get-tuple-element.23), channel_id=1, replica_groups=mesh['section'=2,'z'=4,'x'=4,'dp'=4] {'x'}, dimensions={0} | all-to-all | bytes 1179648 | tf_op jit(solution)/shard_map/all_to_all | solution.py:428
  179.0 16.2 %shard_map.94 = (bf16[32,128,128]{2,1,0:T(8,128)(2,1)S(1)}, bf16[4,576,128]{2,1,0:T(8,128)(2,1)S(1)}) custom-call(bf16[4,576,128]{2,1,0:T(8,128)(2,1)S(1)} %all_to_all.75.in_ref, bf16[32,128,128]{2,1,0:T(8,128)(2,1)} %bitcast.7.cot_ref, bf16[32,128,128]{2,1,0:T(8,128)(2,1)S(1)} %copy-done.11, bf16[128,128]{1,0:T(8,128)(2,1)S(1)} %copy-done.23, ...), custom_call_target="tpu_custom_call" | custom-call | tf_op jit(solution)/shard_map/pallas_call | solution.py:434
  201.2 10.2 %all-to-all-done.8.refs_1_ = bf16[4,576,128]{2,1,0:T(8,128)(2,1)} async-done(((bf16[4,576,128]{2,1,0:T(8,128)(2,1)}), bf16[4,576,128]{2,1,0:T(8,128)(2,1)}, u32[]{:S(2)}, u32[]{:S(2)}) %all-to-all-start.8) | async-done | bytes 589856 | tf_op jit(solution)/shard_map/all_to_all | solution.py:428
  223.0 6.1 %all-to-all-done.11 = bf16[16,2,128,128]{3,2,1,0:T(8,128)(2,1)} async-done(((bf16[16,2,128,128]{3,2,1,0:T(8,128)(2,1)}), bf16[16,2,128,128]{3,2,1,0:T(8,128)(2,1)}, u32[]{:S(2)}, u32[]{:S(2)}) %all-to-all-start.11) | async-done | bytes 1048608 | tf_op jit(solution)/shard_map/all_to_all | solution.py:425
  235.5 5.5 %all-to-all-done.9.in_ref = bf16[4,576,128]{2,1,0:T(8,128)(2,1)S(1)} async-done(((bf16[4,576,128]{2,1,0:T(8,128)(2,1)}), bf16[4,576,128]{2,1,0:T(8,128)(2,1)S(1)}, u32[]{:S(2)}, u32[]{:S(2)}) %all-to-all-start.9) | async-done | bytes 589856 | tf_op jit(solution)/shard_map/all_to_all | solution.py:428
  241.0 5.6 %all-to-all-start.13 = ((bf16[16,128,256]{2,1,0:T(8,128)(2,1)}), bf16[16,128,256]{2,1,0:T(8,128)(2,1)}, u32[]{:S(2)}, u32[]{:S(2)}) async-start(bf16[16,128,256]{2,1,0:T(8,128)(2,1)} %fusion), calls=%async_computation.13 | async-start | bytes 2097152 | tf_op jit(solution)/shard_map/all_to_all | solution.py:476
  249.0 8.4 %shard_map.96 = bf16[32,128,128]{2,1,0:T(8,128)(2,1)} custom-call(bf16[4,576,128]{2,1,0:T(8,128)(2,1)S(1)} %all-to-all-done.9.in_ref, bf16[32,128,128]{2,1,0:T(8,128)(2,1)S(1)} %copy-done.9, bf16[128,128]{1,0:T(8,128)(2,1)S(1)} %copy-done.23, bf16[64,64,64]{2,1,0:T(8,128)(2,1)S(1)} %copy-done.1), custom_call_target="tpu_custom_call" | custom-call | tf_op jit(solution)/shard_map/pallas_call | solution.py:434
  257.5 4.4 %all-to-all-done.13 = bf16[16,128,256]{2,1,0:T(8,128)(2,1)} async-done(((bf16[16,128,256]{2,1,0:T(8,128)(2,1)}), bf16[16,128,256]{2,1,0:T(8,128)(2,1)}, u32[]{:S(2)}, u32[]{:S(2)}) %all-to-all-start.13) | async-done | bytes 1048608 | tf_op jit(solution)/shard_map/all_to_all | solution.py:476
  268.1 13.1 %all-to-all-done.10 = bf16[16,2,128,128]{3,2,1,0:T(8,128)(2,1)S(1)} async-done(((bf16[16,2,128,128]{3,2,1,0:T(8,128)(2,1)}), bf16[16,2,128,128]{3,2,1,0:T(8,128)(2,1)S(1)}, u32[]{:S(2)}, u32[]{:S(2)}) %all-to-all-start.10) | async-done | bytes 1048608 | tf_op jit(solution)/shard_map/all_to_all | solution.py:425
  281.2 4.9 %all-to-all-start.12 = ((bf16[16,128,256]{2,1,0:T(8,128)(2,1)}), bf16[16,128,256]{2,1,0:T(8,128)(2,1)}, u32[]{:S(2)}, u32[]{:S(2)}) async-start(bf16[16,128,256]{2,1,0:T(8,128)(2,1)} %fusion.1), calls=%async_computation.12 | async-start | bytes 2097152 | tf_op jit(solution)/shard_map/all_to_all | solution.py:476
  289.8 12.4 %all-to-all-done.12 = bf16[16,128,256]{2,1,0:T(8,128)(2,1)} async-done(((bf16[16,128,256]{2,1,0:T(8,128)(2,1)}), bf16[16,128,256]{2,1,0:T(8,128)(2,1)}, u32[]{:S(2)}, u32[]{:S(2)}) %all-to-all-start.12) | async-done | bytes 1048608 | tf_op jit(solution)/shard_map/all_to_all | solution.py:476
  306.2 8.5 %collective-permute-done.5 = f32[256,256]{1,0:T(8,128)S(1)} collective-permute-done((f32[256,256]{1,0:T(8,128)S(1)}, f32[256,256]{1,0:T(8,128)S(1)}, u32[]{:S(2)}, u32[]{:S(2)}) %collective-permute-start.5) | collective-permute-done | bytes 262176 | tf_op jit(solution)/shard_map/ppermute | solution.py:510
  (88 shorter events, 74.5 us)
Async XLA Ops:
  9.4 46.7 %collective-permute-start = (bf16[2,8,256,256]{3,2,1,0:T(8,128)(2,1)S(1)}, bf16[2,8,256,256]{3,2,1,0:T(8,128)(2,1)}, u32[]{:S(2)}, u32[]{:S(2)}) collective-permute-start(bf16[2,8,256,256]{3,2,1,0:T(8,128)(2,1)S(1)} %pad_maximum_fusion.refs_2_), channel_id=1, source_target_pairs={{0,64},{64,0},{1,65},{65,1},{2,66},{66,2},{3,67},{67,3},{4,68},{68... | collective-permute-start | bytes 6291464 | tf_op jit(solution)/shard_map/ppermute | solution.py:466
  11.2 26.8 %copy-start = (bf16[65,64,64]{2,1,0:T(8,128)(2,1)S(1)}, bf16[65,64,64]{2,1,0:T(8,128)(2,1)}, u32[]{:S(2)}) copy-start(bf16[65,64,64]{2,1,0:T(8,128)(2,1)} %constant.56.clone.ta_ref) | copy-start | bytes 1597444
  11.2 26.8 %copy-start.24 = (bf16[128,128]{1,0:T(8,128)(2,1)S(1)}, bf16[128,128]{1,0:T(8,128)(2,1)}, u32[]{:S(2)}) copy-start(bf16[128,128]{1,0:T(8,128)(2,1)} %constant.59.clone.ana_ref) | copy-start | bytes 98308
  56.0 14.9 %copy-start.1 = (bf16[64,64,64]{2,1,0:T(8,128)(2,1)S(1)}, bf16[64,64,64]{2,1,0:T(8,128)(2,1)}, u32[]{:S(2)}) copy-start(bf16[64,64,64]{2,1,0:T(8,128)(2,1)} %constant.57.clone.ts_ref) | copy-start | bytes 1572868
  56.0 14.9 %copy-start.23 = (bf16[128,128]{1,0:T(8,128)(2,1)S(1)}, bf16[128,128]{1,0:T(8,128)(2,1)}, u32[]{:S(2)}) copy-start(bf16[128,128]{1,0:T(8,128)(2,1)} %constant.58.clone.syn_ref) | copy-start | bytes 98308
  90.0 13.1 %all-to-all-start.3 = ((bf16[4,576,128]{2,1,0:T(8,128)(2,1)}), bf16[4,576,128]{2,1,0:T(8,128)(2,1)}, u32[]{:S(2)}, u32[]{:S(2)}) async-start(bf16[4,576,128]{2,1,0:T(8,128)(2,1)} %copy-done.17), calls=%async_computation.3 | async-start | bytes 1179648 | tf_op jit(solution)/shard_map/all_to_all | solution.py:428
  103.1 19.5 %all-to-all-start.5 = ((bf16[16,2,128,128]{3,2,1,0:T(8,128)(2,1)}), bf16[16,2,128,128]{3,2,1,0:T(8,128)(2,1)}, u32[]{:S(2)}, u32[]{:S(2)}) async-start(bf16[16,2,128,128]{3,2,1,0:T(8,128)(2,1)} %copy-done.2), calls=%async_computation.5 | async-start | bytes 2097152 | tf_op jit(solution)/shard_map/all_to_all | solution.py:422
  135.7 27.7 %copy-start.22 = (bf16[8,144,256]{2,1,0:T(8,128)(2,1)S(1)}, bf16[8,144,256]{2,1,0:T(8,128)(2,1)}, u32[]{:S(2)}) copy-start(bf16[8,144,256]{2,1,0:T(8,128)(2,1)} %copy-done.21) | copy-start | bytes 1769476
  152.6 10.8 %copy-start.14 = (bf16[32,128,128]{2,1,0:T(8,128)(2,1)}, bf16[32,128,128]{2,1,0:T(8,128)(2,1)S(1)}, u32[]{:S(2)}) copy-start(bf16[32,128,128]{2,1,0:T(8,128)(2,1)S(1)} %get-tuple-element.29) | copy-start | bytes 3145732
  163.4 15.6 %copy-start.11 = (bf16[32,128,128]{2,1,0:T(8,128)(2,1)S(1)}, bf16[32,128,128]{2,1,0:T(8,128)(2,1)}, u32[]{:S(2)}) copy-start(bf16[32,128,128]{2,1,0:T(8,128)(2,1)} %copy-done.10) | copy-start | bytes 3145732
  197.0 14.4 %all-to-all-start.8 = ((bf16[4,576,128]{2,1,0:T(8,128)(2,1)}), bf16[4,576,128]{2,1,0:T(8,128)(2,1)}, u32[]{:S(2)}, u32[]{:S(2)}) async-start(bf16[4,576,128]{2,1,0:T(8,128)(2,1)} %copy-done.16), calls=%async_computation.8 | async-start | bytes 1179648 | tf_op jit(solution)/shard_map/all_to_all | solution.py:428
  211.5 17.7 %all-to-all-start.11 = ((bf16[16,2,128,128]{3,2,1,0:T(8,128)(2,1)}), bf16[16,2,128,128]{3,2,1,0:T(8,128)(2,1)}, u32[]{:S(2)}, u32[]{:S(2)}) async-start(bf16[16,2,128,128]{3,2,1,0:T(8,128)(2,1)} %bitcast.35), calls=%async_computation.11 | async-start | bytes 2097152 | tf_op jit(solution)/shard_map/all_to_all | solution.py:425
  215.8 2.4 copy-start.20
  218.2 14.5 %collective-permute-start.3 = (bf16[16,128,256]{2,1,0:T(8,128)(2,1)}, bf16[16,128,256]{2,1,0:T(8,128)(2,1)}, u32[]{:S(2)}, u32[]{:S(2)}) collective-permute-start(bf16[16,128,256]{2,1,0:T(8,128)(2,1)} %dynamic-slice_bitcast_fusion), channel_id=1, source_target_pairs={{0,64},{64,0},{1,65},{65,1},{2,66},{66,2},{3,67},{67,3},{4,68},{68... | collective-permute-start | bytes 3145736 | tf_op jit(solution)/shard_map/ppermute | solution.py:474
  229.1 11.9 %all-to-all-start.9 = ((bf16[4,576,128]{2,1,0:T(8,128)(2,1)}), bf16[4,576,128]{2,1,0:T(8,128)(2,1)S(1)}, u32[]{:S(2)}, u32[]{:S(2)}) async-start(bf16[4,576,128]{2,1,0:T(8,128)(2,1)} %copy-done.15), calls=%async_computation.9 | async-start | bytes 1179648 | tf_op jit(solution)/shard_map/all_to_all | solution.py:428
  235.5 13.5 %copy-start.9 = (bf16[32,128,128]{2,1,0:T(8,128)(2,1)S(1)}, bf16[32,128,128]{2,1,0:T(8,128)(2,1)}, u32[]{:S(2)}) copy-start(bf16[32,128,128]{2,1,0:T(8,128)(2,1)} %copy-done.8) | copy-start | bytes 3145732
  241.0 20.8 %all-to-all-start.13 = ((bf16[16,128,256]{2,1,0:T(8,128)(2,1)}), bf16[16,128,256]{2,1,0:T(8,128)(2,1)}, u32[]{:S(2)}, u32[]{:S(2)}) async-start(bf16[16,128,256]{2,1,0:T(8,128)(2,1)} %fusion), calls=%async_computation.13 | async-start | bytes 2097152 | tf_op jit(solution)/shard_map/all_to_all | solution.py:476
  249.0 16.5 %collective-permute-start.2 = (bf16[16,128,256]{2,1,0:T(8,128)(2,1)}, bf16[16,128,256]{2,1,0:T(8,128)(2,1)}, u32[]{:S(2)}, u32[]{:S(2)}) collective-permute-start(bf16[16,128,256]{2,1,0:T(8,128)(2,1)} %dynamic-slice_bitcast_fusion.1), channel_id=1, source_target_pairs={{0,64},{64,0},{1,65},{65,1},{2,66},{66,2},{3,67},{67,3},{4,68},{68... | collective-permute-start | bytes 3145736 | tf_op jit(solution)/shard_map/ppermute | solution.py:474
  257.5 8.1 %copy-start.5 = (bf16[16,256,256]{2,1,0:T(8,128)(2,1)S(1)}, bf16[16,256,256]{2,1,0:T(8,128)(2,1)}, u32[]{:S(2)}) copy-start(bf16[16,256,256]{2,1,0:T(8,128)(2,1)} %copy-done.4) | copy-start | bytes 6291460
  261.9 19.3 %all-to-all-start.10 = ((bf16[16,2,128,128]{3,2,1,0:T(8,128)(2,1)}), bf16[16,2,128,128]{3,2,1,0:T(8,128)(2,1)S(1)}, u32[]{:S(2)}, u32[]{:S(2)}) async-start(bf16[16,2,128,128]{3,2,1,0:T(8,128)(2,1)} %bitcast.8), calls=%async_computation.10 | async-start | bytes 2097152 | tf_op jit(solution)/shard_map/all_to_all | solution.py:425
  281.2 21.0 %all-to-all-start.12 = ((bf16[16,128,256]{2,1,0:T(8,128)(2,1)}), bf16[16,128,256]{2,1,0:T(8,128)(2,1)}, u32[]{:S(2)}, u32[]{:S(2)}) async-start(bf16[16,128,256]{2,1,0:T(8,128)(2,1)} %fusion.1), calls=%async_computation.12 | async-start | bytes 2097152 | tf_op jit(solution)/shard_map/all_to_all | solution.py:476
  289.8 25.7 %collective-permute-start.1 = (bf16[16,2,128,128]{3,2,1,0:T(8,128)(2,1)}, bf16[16,2,128,128]{3,2,1,0:T(8,128)(2,1)S(1)}, u32[]{:S(2)}, u32[]{:S(2)}) collective-permute-start(bf16[16,2,128,128]{3,2,1,0:T(8,128)(2,1)} %get-tuple-element.34), channel_id=1, source_target_pairs={{0,64},{64,0},{1,65},{65,1},{2,66},{66,2},{3,67},{67,3},{4,68},{68... | collective-permute-start | bytes 3145736 | tf_op jit(solution)/shard_map/ppermute | solution.py:503
  303.6 1.4 collective-permute-start.4
  305.1 9.6 %collective-permute-start.5 = (f32[256,256]{1,0:T(8,128)S(1)}, f32[256,256]{1,0:T(8,128)S(1)}, u32[]{:S(2)}, u32[]{:S(2)}) collective-permute-start(f32[256,256]{1,0:T(8,128)S(1)} %pad_maximum_fusion.1), channel_id=1, source_target_pairs={{0,12},{4,8},{8,4},{12,0},{1,13},{5,9},{9,5},{13,1},{2,14},{6,10},... | collective-permute-start | bytes 786440 | tf_op jit(solution)/shard_map/ppermute | solution.py:510
  (15 other events, 16.0 us)

commit v3 on v2

v3 whole, which is shorter than its diff:
```python
import math

import jax
import jax.numpy as jnp
import ml_dtypes
import numpy as np
from jax import lax
from jax.experimental import pallas as pl
from jax.experimental.pallas import tpu as pltpu
from jax.sharding import Mesh
from jax.sharding import PartitionSpec as P

BF16 = jnp.bfloat16
F32 = jnp.float32


def gauss_nodes(resolution):
    counter = np.arange(resolution) * 1.0
    guesses = np.cos(math.pi * (counter + 0.75) / (resolution + 0.5))
    for sweep in range(100):
        current = np.ones(resolution)
        previous = np.zeros(resolution)
        for degree in range(1, resolution + 1):
            following = (
                (2.0 * degree - 1.0) * guesses * current - (degree - 1.0) * previous
            ) / degree
            previous = current
            current = following
        slope_val = resolution * (guesses * current - previous) / (guesses * guesses - 1.0)
        guesses = guesses - current / slope_val
    current = np.ones(resolution)
    previous = np.zeros(resolution)
    for degree in range(1, resolution + 1):
        following = ((2.0 * degree - 1.0) * guesses * current - (degree - 1.0) * previous) / degree
        previous = current
        current = following
    slope_val = resolution * (guesses * current - previous) / (guesses * guesses - 1.0)
    weights_q = 2.0 / ((1.0 - guesses * guesses) * slope_val * slope_val)
    return (guesses[::-1].copy(), weights_q[::-1].copy())


def legendre_table(resolution):
    points, quadrature = gauss_nodes(resolution)
    sine_row = np.sqrt(1.0 - points * points)
    basis = np.zeros((resolution, resolution, resolution))
    diagonal = np.full(resolution, math.sqrt(1.0 / (4.0 * math.pi)))
    for harmonic in range(resolution):
        if harmonic > 0:
            diagonal = diagonal * sine_row * math.sqrt((2.0 * harmonic + 1.0) / (2.0 * harmonic))
        basis[harmonic, harmonic] = diagonal
        if harmonic + 1 < resolution:
            basis[harmonic, harmonic + 1] = points * math.sqrt(2.0 * harmonic + 3.0) * diagonal
        for degree in range(harmonic + 2, resolution):
            alpha_coef = math.sqrt(
                (4.0 * degree * degree - 1.0) / (degree * degree - harmonic * harmonic)
            )
            beta_coef = math.sqrt(
                ((degree - 1.0) ** 2 - harmonic * harmonic) / (4.0 * (degree - 1.0) ** 2 - 1.0)
            )
            basis[harmonic, degree] = alpha_coef * (
                points * basis[harmonic, degree - 1] - beta_coef * basis[harmonic, degree - 2]
            )
    return basis * np.sqrt(2.0 * math.pi * quadrature)[None, None, :]


def longitude_table(longitudes, degrees):
    column = np.arange(2 * degrees)
    harmonic, parity = column // 2, column % 2
    phase = (np.arange(longitudes)[:, None] * harmonic[None, :]) % longitudes
    angles = phase.astype(np.float32) * np.float32(2.0 * math.pi / longitudes)
    scales = np.where(harmonic == 0, 1.0 / math.sqrt(longitudes), math.sqrt(2.0 / longitudes))
    basis = np.where(parity[None, :] == 0, np.cos(angles), -np.sin(angles))
    return (basis * scales[None, :].astype(np.float32)).astype(ml_dtypes.bfloat16)


SLOTS = 72


def pair_degrees(degrees, blocks):
    quarter = degrees // 16
    return np.array(
        [
            16 * (r // quarter) + quarter * x + r % quarter
            for x in range(blocks)
            for r in range(degrees // 2 // blocks)
        ]
    )


def polar_tables(degrees, blocks):
    leg = legendre_table(degrees).astype(np.float32).astype(ml_dtypes.bfloat16)
    low = pair_degrees(degrees, blocks)
    pairs = degrees // 2
    ana = np.zeros((degrees + 1, 2, pairs, 2, pairs), ml_dtypes.bfloat16)
    syn = np.zeros((degrees, 2, pairs, 2, pairs), ml_dtypes.bfloat16)
    for half in range(2):
        for g, l in enumerate(low):
            for pos in range(degrees + 1):
                if l >= pos:
                    ana[pos, half, g, 1] = leg[pos, l, half::2]
                else:
                    ana[pos, half, g, 0] = leg[degrees - pos, degrees - 1 - l, half::2]
            for m in range(degrees):
                if l >= m:
                    syn[m, half, :, 1, g] = leg[m, l, half::2]
                if degrees - 1 - l >= m:
                    syn[m, half, :, 0, g] = leg[m, degrees - 1 - l, half::2]
    size = (2 * pairs, 2 * pairs)
    return ana.reshape((degrees + 1,) + size), syn.reshape((degrees,) + size)


def params(megabytes=16):
    return pltpu.CompilerParams(vmem_limit_bytes=megabytes * 2**20)


def cost(microseconds):
    return pl.CostEstimate(
        flops=int(microseconds * 1.1e9), bytes_accessed=1 << 20, transcendentals=0
    )


def dot(left, right):
    return jnp.dot(left, right, preferred_element_type=F32)


def normal_cdf(values):
    return 0.5 * (1.0 + lax.erf(values * (1.0 / math.sqrt(2.0))))


def low_lanes(shape):
    return lax.broadcasted_iota(jnp.int32, shape, len(shape) - 1) < shape[-1] // 2


def turned(value):
    return pltpu.roll(value, value.shape[-1] // 2, value.ndim - 1)


def interleave(first, second):
    low = low_lanes(first.shape)
    return jnp.where(low, first, turned(second)), jnp.where(low, turned(first), second)


def begin(source, target, sem):
    copy = pltpu.make_async_copy(source, target, sem)
    copy.start()
    return copy


def pack_body(idx_ref, field_hbm, cot_hbm, out_ref, field_ref, cot_ref, sem):
    samples, rows, _, channels = field_ref.shape
    loads = []
    for s in range(samples):
        at = s + samples * idx_ref[1]
        loads.append(begin(field_hbm.at[at], field_ref.at[s], sem.at[s]))
        loads.append(begin(cot_hbm.at[at], cot_ref.at[s], sem.at[samples + s]))
    for s in range(samples):
        for i, ref in enumerate((field_ref, cot_ref)):
            loads[2 * s + i].wait()
            for q in range(rows // 2):
                for t in range(channels // 128):
                    span = slice(t * 128, (t + 1) * 128)
                    one, two = ref[s, 2 * q, :, span], ref[s, 2 * q + 1, :, span]
                    left, right = interleave(one.astype(F32), two.astype(F32))
                    out_ref[4 * s + 2 * t, i, q] = left.astype(BF16)
                    out_ref[4 * s + 2 * t + 1, i, q] = right.astype(BF16)


def unpack_body(in_ref, out_hbm, out_ref, sem):
    samples, rows, _, channels = out_ref.shape
    saves = []
    for s in range(samples):
        for q in range(rows // 2):
            for t in range(channels // 128):
                span = slice(t * 128, (t + 1) * 128)
                one, two = in_ref[4 * s + 2 * t, q], in_ref[4 * s + 2 * t + 1, q]
                one, two = interleave(one.astype(F32), two.astype(F32))
                out_ref[s, 2 * q, :, span] = one.astype(BF16)
                out_ref[s, 2 * q + 1, :, span] = two.astype(BF16)
        saves.append(begin(out_ref.at[s], out_hbm.at[s], sem.at[s]))
    for save in saves:
        save.wait()


def select_body(idx_ref, weight_ref, out_ref, sem):
    quarter = out_ref.shape[1] // 2
    copies = []
    for z in range(4):
        at = 4 * quarter * z + quarter * (idx_ref[0] if z < 2 else 3 - idx_ref[0])
        target = out_ref.at[z // 2, pl.ds((z % 2) * quarter, quarter)]
        copies.append(begin(weight_ref.at[0, pl.ds(at, quarter)], target, sem.at[z]))
    for copy in copies:
        copy.wait()


def prepare_body(idx_ref, own_ref, far_ref, ta_hbm, ts_hbm, w0_ref, w1_ref, ta_ref, ts_ref, sem):
    def fetch(source, target, at):
        return pltpu.make_async_copy(source, target, sem.at[at])

    tables = [begin(ta_hbm, ta_ref, sem.at[2]), begin(ts_hbm, ts_ref, sem.at[3])]

    @pl.when(idx_ref[1] == 0)
    def _():
        fetch(own_ref, w0_ref, 0).start()
        fetch(far_ref, w1_ref, 1).start()

    @pl.when(idx_ref[1] == 1)
    def _():
        fetch(far_ref, w0_ref, 0).start()
        fetch(own_ref, w1_ref, 1).start()

    fetch(own_ref, w0_ref, 0).wait()
    fetch(own_ref, w1_ref, 1).wait()
    for table in tables:
        table.wait()


def store_spectrum(q, value, spec_ref):
    spec_ref[pl.ds(q, 128, stride=32), :] = value


def spectrum_at(q, grid_ref):
    return grid_ref[q * 128 : (q + 1) * 128, :].astype(BF16)


def analyse(spec_ref, table_ref, slot_ref, out_ref):
    degrees = table_ref.shape[0] - 1
    pairs = degrees // 2

    low = low_lanes((pairs, 128))

    def order(m):
        rows = spec_ref[m * 2 * pairs : (m + 1) * 2 * pairs, :].astype(BF16)
        return jnp.concatenate([rows[:pairs], rows[pairs:]], axis=1)

    for pos in range(degrees + 1):
        right, left = order(min(degrees - pos, degrees - 1)), table_ref[pos]
        if pos < pairs:
            right = jnp.concatenate([right, order(pos)], axis=0)
        else:
            left = left[:, :pairs]
        both = dot(left, right)
        even, odd = both[:pairs], both[pairs:]
        value = jnp.where(low, even[:, :128], odd[:, 128:]) + turned(
            jnp.where(low, even[:, 128:], odd[:, :128])
        )
        slot_ref[pl.ds(pos, pairs, stride=SLOTS), :] = value
    for pos in range(degrees + 1, SLOTS):
        slot_ref[pl.ds(pos, pairs, stride=SLOTS), :] = jnp.zeros((pairs, 128), F32)
    blocks, rows, _ = out_ref.shape
    for b in range(blocks):
        out_ref[b] = slot_ref[b * rows : (b + 1) * rows, :].astype(BF16)


def synthesise(in_ref, table_ref, slot_ref, grid_ref):
    degrees = table_ref.shape[0]
    pairs = degrees // 2
    blocks, rows, _ = in_ref.shape
    for b in range(blocks):
        slot_ref[b * rows : (b + 1) * rows, :] = in_ref[b].astype(F32)

    for m in range(degrees):
        right = slot_ref[pl.ds(degrees - m, pairs, stride=SLOTS), :]
        left = table_ref[m]
        if m < pairs:
            low = slot_ref[pl.ds(m, pairs, stride=SLOTS), :]
            right = jnp.concatenate([right, low], axis=0)
        else:
            left = left[:, :pairs]
        both = dot(left, right.astype(BF16))
        real, imag = interleave(both[:pairs], both[pairs:])
        grid_ref[pl.ds(2 * m, pairs, stride=2 * degrees), :] = real
        grid_ref[pl.ds(2 * m + 1, pairs, stride=2 * degrees), :] = imag


def gelu_parts(pre):
    cdf = normal_cdf(pre)
    density = jnp.exp(-0.5 * pre * pre) * (1.0 / math.sqrt(2.0 * math.pi))
    return pre * cdf, cdf + pre * density


def first_body(recv_ref, ana_ref, ta_ref, out_ref, spec_ref, slot_ref):
    basis = ana_ref[...]
    for d in range(recv_ref.shape[0]):
        for q in range(2):
            store_spectrum(2 * d + q, dot(basis, recv_ref[d, 0, q]), spec_ref)
    analyse(spec_ref, ta_ref, slot_ref, out_ref)


def layer0_body(in_ref, recv_ref, syn_ref, ana_ref, ts_ref, ta_ref, h_ref, slope_ref, out_ref,
                spec_ref, grid_ref, slot_ref):
    synthesise(in_ref, ts_ref, slot_ref, grid_ref)
    syn, ana = syn_ref[...], ana_ref[...]
    for d in range(recv_ref.shape[0]):
        for q in range(2):
            value, slope = gelu_parts(dot(syn, spectrum_at(2 * d + q, grid_ref)))
            slope_ref[d, q] = slope.astype(BF16)
            h = (recv_ref[d, 0, q].astype(F32) + value).astype(BF16)
            h_ref[d, q] = h
            store_spectrum(2 * d + q, dot(ana, h), spec_ref)
    analyse(spec_ref, ta_ref, slot_ref, out_ref)


def layer1_body(in_ref, recv_ref, h_ref, syn_ref, ana_ref, ts_ref, ta_ref, top_ref, out_ref,
                spec_ref, grid_ref, slot_ref):
    synthesise(in_ref, ts_ref, slot_ref, grid_ref)
    syn, ana = syn_ref[...], ana_ref[...]
    for d in range(recv_ref.shape[0]):
        for q in range(2):
            value, slope = gelu_parts(dot(syn, spectrum_at(2 * d + q, grid_ref)))
            top_ref[d, q] = (h_ref[d, q].astype(F32) + value).astype(BF16)
            gpre = (recv_ref[d, 1, q].astype(F32) * slope).astype(BF16)
            store_spectrum(2 * d + q, dot(ana, gpre), spec_ref)
    analyse(spec_ref, ta_ref, slot_ref, out_ref)


def back1_body(in_ref, recv_ref, slope_ref, syn_ref, ana_ref, ts_ref, ta_ref, g_ref, out_ref,
               spec_ref, grid_ref, slot_ref):
    synthesise(in_ref, ts_ref, slot_ref, grid_ref)
    syn, ana = syn_ref[...], ana_ref[...]
    for d in range(recv_ref.shape[0]):
        for q in range(2):
            back = dot(syn, spectrum_at(2 * d + q, grid_ref))
            g = (recv_ref[d, 1, q].astype(F32) + back).astype(BF16)
            g_ref[d, q] = g
            gpre = (g.astype(F32) * slope_ref[d, q].astype(F32)).astype(BF16)
            store_spectrum(2 * d + q, dot(ana, gpre), spec_ref)
    analyse(spec_ref, ta_ref, slot_ref, out_ref)


def back0_body(in_ref, g_ref, top_ref, syn_ref, ts_ref, ends_ref, grid_ref, slot_ref, sem):
    move = begin(top_ref, ends_ref.at[1], sem.at[0])
    synthesise(in_ref, ts_ref, slot_ref, grid_ref)
    syn = syn_ref[...]
    for d in range(g_ref.shape[0]):
        for q in range(2):
            back = dot(syn, spectrum_at(2 * d + q, grid_ref))
            ends_ref[0, d, q] = (g_ref[d, q].astype(F32) + back).astype(BF16)
    move.wait()


def lower_rows(x_at, r):
    index = lax.broadcasted_iota(jnp.int32, (2 * SLOTS, 256), 0)
    pos = jnp.where(index < SLOTS, index, index - SLOTS)
    return pos <= 16 * (r // 4) + r % 4 + 4 * x_at


def mix_body(backward, idx_ref, in_ref, w_ref, out_ref, coef_ref):
    pairs = w_ref.shape[1]
    contract = (((1,), (1 if backward else 0,)), ((), ()))
    rows = 2 * SLOTS
    for rr in range(pairs // 2):
        span = slice(rr * rows, (rr + 1) * rows)
        blocks = [in_ref[b, span].astype(F32) for b in range(4)]
        a0, a1 = interleave(blocks[0], blocks[1])
        b0, b1 = interleave(blocks[2], blocks[3])
        real = jnp.concatenate([a0, b0], axis=1)
        imag = jnp.concatenate([a1, b1], axis=1)
        reals, imags = [], []
        for r in (2 * rr, 2 * rr + 1):
            part = slice((r % 2) * SLOTS, (r % 2 + 1) * SLOTS)
            stack = jnp.concatenate([real[part], imag[part]], axis=0).astype(BF16)
            coef_ref[r] = stack
            one = lax.dot_general(stack, w_ref[0, r], contract, preferred_element_type=F32)
            two = lax.dot_general(
                stack, w_ref[1, pairs - 1 - r], contract, preferred_element_type=F32
            )
            mixed = jnp.where(lower_rows(idx_ref[0], r), one, two)
            reals.append(mixed[:SLOTS])
            imags.append(mixed[SLOTS:])
        real = jnp.concatenate(reals, axis=0)
        imag = jnp.concatenate(imags, axis=0)
        for t in range(2):
            lanes = slice(t * 128, (t + 1) * 128)
            left, right = interleave(real[:, lanes], imag[:, lanes])
            out_ref[2 * t, span] = left.astype(BF16)
            out_ref[2 * t + 1, span] = right.astype(BF16)


def grad_body(flip, idx_ref, coef0_ref, coef1_ref, grad0_ref, grad1_ref, out_ref):
    pairs = coef0_ref.shape[0]
    over = (((0,), (0,)), ((), ()))
    first = idx_ref[1] == (1 if flip else 0)
    for r in range(pairs):
        coef = jnp.where(first, coef0_ref[r].astype(F32), coef1_ref[r].astype(F32)).astype(BF16)
        grad = jnp.where(first, grad0_ref[r].astype(F32), grad1_ref[r].astype(F32))
        lower = lower_rows(idx_ref[0], r)
        pieces = (jnp.where(lower, grad, 0.0), jnp.where(lower, 0.0, grad))
        for at, piece in zip((r, 2 * pairs - 1 - r), pieces):
            place = 4 * ((at % 4 + 4 - idx_ref[2]) % 4) + (at // 4 + 4 - idx_ref[3]) % 4
            made = lax.dot_general(coef, piece.astype(BF16), over, preferred_element_type=F32)
            out_ref[place] = made.astype(BF16)


def local(ta, ts, fields_in, cotangent, weights):
    rows_all, lat_rows, longitudes, channels = fields_in.shape
    degrees = longitudes // 2
    samples = rows_all // 2
    section = lax.axis_index("section")
    x_at, z_at, y_at = lax.axis_index("x"), lax.axis_index("z"), lax.axis_index("dp")
    idx = jnp.stack([x_at, section, y_at, z_at]).astype(jnp.int32)
    syn_np = longitude_table(longitudes, degrees)
    syn = jnp.asarray(syn_np)
    ana = jnp.asarray(np.ascontiguousarray(syn_np.T))
    swap = [(0, 1), (1, 0)]
    pairs = degrees // 2
    q_rows = lat_rows // 2

    vmem = pl.BlockSpec(memory_space=pltpu.VMEM)
    smem = pl.BlockSpec(memory_space=pltpu.SMEM)
    hbm = pl.BlockSpec(memory_space=pltpu.HBM)
    half_shape = (16, q_rows, longitudes, 128)
    half = pltpu.VMEM(half_shape, BF16)
    spec = pltpu.VMEM((4, pairs // 4 * SLOTS, 128), BF16)
    coef = pltpu.VMEM((pairs // 4, 2 * SLOTS, channels), BF16)
    product = pltpu.VMEM((degrees // 4, channels, channels), BF16)
    chosen = pltpu.VMEM((2, pairs // 4, channels, channels), BF16)
    tall = pltpu.VMEM((pairs * 128, 128), F32)
    slots = pltpu.VMEM((pairs * SLOTS, 128), F32)

    def far_away(array):
        return pltpu.with_memory_space_constraint(array, pltpu.HBM)

    def near(array):
        return pltpu.with_memory_space_constraint(array, pltpu.VMEM)

    def call(time, body, ins, shapes, scratches, *args, sems=0, outs=None):
        many = isinstance(shapes, list)
        return pl.pallas_call(
            body,
            in_specs=ins,
            out_specs=outs or ([vmem] * len(shapes) if many else vmem),
            out_shape=shapes,
            scratch_shapes=scratches + [pltpu.SemaphoreType.DMA((sems,))] * (sems > 0),
            cost_estimate=cost(time),
            compiler_params=params(),
        )(*args)

    quarter_field = pltpu.VMEM((samples, lat_rows, longitudes, channels), BF16)
    packed = call(
        3, pack_body, [smem, hbm, hbm], pltpu.VMEM((16, 2) + half_shape[1:], BF16),
        [quarter_field] * 2, idx, far_away(fields_in), far_away(cotangent), sems=2 * samples,
    )
    own = call(2, select_body, [smem, hbm], chosen, [], idx, far_away(weights), sems=4)
    far = lax.ppermute(own, "section", swap)
    w0, w1, ta, ts = call(
        2, prepare_body, [smem, vmem, vmem, hbm, hbm],
        [chosen, chosen, pltpu.VMEM(ta.shape, BF16), pltpu.VMEM(ts.shape, BF16)], [],
        idx, near(own), near(far), far_away(ta), far_away(ts), sems=4,
    )
    recv = near(lax.all_to_all(packed, ("z", "x"), 0, 0, tiled=True))

    def turn(value):
        return near(lax.all_to_all(value, "x", 0, 0, tiled=True))

    def mix_call(value, weight, backward):
        def body(*refs):
            mix_body(backward, *refs)

        return call(2, body, [smem, vmem, vmem], [spec, coef], [], idx, value, weight)

    value = call(3, first_body, [vmem] * 3, spec, [tall, slots], recv, ana, ta)
    value, coef0 = mix_call(turn(value), w0, False)
    h1, slope, value = call(
        6, layer0_body, [vmem] * 6, [half, half, spec], [tall, tall, slots],
        turn(value), recv, syn, ana, ts, ta,
    )
    value, coef1 = mix_call(turn(value), w1, False)
    top, value = call(
        6, layer1_body, [vmem] * 7, [half, spec], [tall, tall, slots],
        turn(value), recv, h1, syn, ana, ts, ta,
    )
    value, grad1 = mix_call(turn(value), w1, True)
    g1, value = call(
        5, back1_body, [vmem] * 7, [half, spec], [tall, tall, slots],
        turn(value), recv, slope, syn, ana, ts, ta,
    )
    value, grad0 = mix_call(turn(value), w0, True)
    ends = call(
        4, back0_body, [vmem] * 5, pltpu.VMEM((2,) + half_shape, BF16), [tall, slots],
        turn(value), g1, top, syn, ts, sems=1,
    )
    ends = ends.reshape((32,) + half_shape[1:])
    ends = near(lax.all_to_all(ends, ("section", "z", "x"), 0, 0, tiled=True))
    section_ends = call(
        3, unpack_body, [vmem], pltpu.HBM(fields_in.shape, BF16),
        [pltpu.VMEM(fields_in.shape, BF16)], ends, sems=rows_all, outs=hbm,
    )[None]

    def grad_call(flip):
        def body(*refs):
            grad_body(flip, *refs)

        return call(
            3, body, [smem] + [vmem] * 4, product, [], idx, coef0, coef1, grad0, grad1
        )

    got = lax.ppermute(grad_call(True), "section", swap)
    both = (grad_call(False).astype(F32) + got.astype(F32)).astype(BF16)

    def fold(value, axes, routes):
        step = value.shape[0] // 4
        total = 0.0
        for k, route in enumerate(routes):
            block = value[k * step : (k + 1) * step]
            if route is not None:
                block = lax.ppermute(block, axes, route)
            total += block.astype(F32)
        return total

    along = [None] + [[(i, (i + k) % 4) for i in range(4)] for k in range(1, 4)]
    across = []
    for k in range(4):
        across.append([])
        for z in range(4):
            for x in range(4):
                there = (z + k) % 4
                across[k].append((4 * z + x, 4 * there + (x if there < 2 else 3 - x)))
    total = fold(fold(both, "dp", along).astype(BF16), ("z", "x"), across)
    batch_count = rows_all * lax.axis_size("dp")
    return (section_ends, (total / batch_count)[None])


def solution(mesh):
    grid = Mesh(mesh.devices.reshape(2, 4, 4, 4), ("section", "z", "x", "dp"))
    rows = P("dp", ("z", "x"), None, None)
    in_specs = (rows, rows, P("section", None, None, None))
    out_specs = (
        P("section", "dp", ("z", "x"), None, None),
        P("section", ("z", "x", "dp"), None, None),
    )
    ta, ts = polar_tables(64, 4)

    def body(fields_in, cotangent, weights):
        return local(jnp.asarray(ta), jnp.asarray(ts), fields_in, cotangent, weights)

    return jax.shard_map(body, mesh=grid, in_specs=in_specs, out_specs=out_specs, check_vma=False)
```

time: 321 us -> 228 us (0.71)
  Pallas kernels: 81 us -> 42.9 us
  waiting for transfers between devices: 77.1 us -> 53 us
  local copies, waits for them, and re-layouts: 29.3 us -> 7.27 us
  other arithmetic: 11.5 us -> 3.33 us
  blocking collectives: 83.8 us -> 91.2 us
  starting transfers between devices: 35.9 us -> 28.9 us
    all_to_all x8 -> x2, waiting for transfers between devices: 67.3 us -> 26.7 us  [the longest x1 26.7 us: local(): recv = near(lax.all_to_all(packed, ('z', 'x'), 0, 0, tiled=True))]
    pallas_call x12 -> x15, Pallas kernels: 81 us -> 42.9 us  [call(): pl.pallas_call(body, in_specs=ins, out_specs=outs or ([vmem] * len(shapes...]
    all_to_all x8 -> x2, starting transfers between devices: 34.6 us -> 12.1 us  [the longest x1 7.96 us: local(): recv = near(lax.all_to_all(packed, ('z', 'x'), 0, 0, tiled=True))]
    ppermute x5 -> x8, waiting for transfers between devices: 9.85 us -> 26.3 us  [the longest x7 26.3 us: fold(): block = lax.ppermute(block, axes, route)]
    ppermute x5 -> x8, starting transfers between devices: 1.23 us -> 16.7 us  [the longest x7 16.7 us: fold(): block = lax.ppermute(block, axes, route)]
    unnamed x50 -> x34, local copies, waits for them, and re-layouts: 16 us -> 7.12 us
    all_to_all x6 -> x8, blocking collectives: 83.8 us -> 91.2 us  [turn(): return near(lax.all_to_all(value, 'x', 0, 0, tiled=True))]
    slice x1 -> x2, local copies, waits for them, and re-layouts: 5.95 us -> 0.14 us  [fold(): block = value[k * step:(k + 1) * step]]
  transfers between devices with their start and end apart: 14 -> 11, of which waited for: 10 -> 5; matrix products, arithmetic and copies ran while one was open for 5% -> 1% of each run, Pallas kernels for 7% -> 6%
where the time goes in v3:
time: 228 us
  blocking collectives  91.2 us (40%)
  waiting for transfers between devices  53 us (23%)
  Pallas kernels  42.9 us (19%)
  starting transfers between devices  28.9 us (13%)
  local copies, waits for them, and re-layouts  7.27 us (3%)
  other arithmetic  3.33 us (1%)
    all_to_all x8, blocking collectives, turn(): return near(lax.all_to_all(value, 'x', 0, 0, tiled=True))  91.2 us
    pallas_call x15, Pallas kernels, call(): pl.pallas_call(body, in_specs=ins, out_specs=outs or ([vmem] * len(shapes...  42.9 us
    all_to_all x1, waiting for transfers between devices, local(): recv = near(lax.all_to_all(packed, ('z', 'x'), 0, 0, tiled=True))  26.7 us
    ppermute x7, waiting for transfers between devices, fold(): block = lax.ppermute(block, axes, route)  26.3 us
    ppermute x7, starting transfers between devices, fold(): block = lax.ppermute(block, axes, route)  16.7 us
    all_to_all x1, starting transfers between devices, local(): recv = near(lax.all_to_all(packed, ('z', 'x'), 0, 0, tiled=True))  7.96 us
    unnamed x34, local copies, waits for them, and re-layouts  7.12 us
  transfers between devices with their start and end apart: 11, of which 5 were waited for; matrix products, arithmetic and copies ran while one was open for 1% of the time, Pallas kernels for 6%

profile of v3, /device:TPU:0, one launch (start us, length us, event | category | flops | bytes accessed | tf_op | source)
XLA Modules:
  0.0 227.7 jit_solution(15865396204090487110)
XLA Ops:
  0.7 3.5 %shard_map.87.own_ref = bf16[2,8,256,256]{3,2,1,0:T(8,128)(2,1)} custom-call(s32[4]{0:T(128)S(1)} %pad_add_fusion.idx_ref.refs_0_, bf16[1,64,256,256]{3,2,1,0:T(8,128)(2,1)} %weight_ref.1), custom_call_target="tpu_custom_call" | custom-call | flops 2200000000 | bytes 1048576 | tf_op jit(solution)/shard_map/pallas_call | solution.py:428
  4.3 2.7 %shard_map.86 = bf16[16,2,2,128,128]{4,3,2,1,0:T(8,128)(2,1)S(1)} custom-call(s32[4]{0:T(128)S(1)} %pad_add_fusion.idx_ref.refs_0_, bf16[8,4,128,256]{3,2,1,0:T(8,128)(2,1)} %field_hbm.1, bf16[8,4,128,256]{3,2,1,0:T(8,128)(2,1)} %cot_hbm.1), custom_call_target="tpu_custom_call" | custom-call | flops 3300000000 | bytes 1048576 | tf_op jit(solution)/shard_map/pallas_call | solution.py:428
  8.3 8.0 %all-to-all-start = ((bf16[16,2,2,128,128]{4,3,2,1,0:T(8,128)(2,1)}), bf16[16,2,2,128,128]{4,3,2,1,0:T(8,128)(2,1)S(1)}, u32[]{:S(2)}, u32[]{:S(2)}) async-start(bf16[16,2,2,128,128]{4,3,2,1,0:T(8,128)(2,1)} %copy-done), calls=%async_computation | async-start | bytes 4194304 | tf_op jit(solution)/shard_map/all_to_all | solution.py:450
  16.3 3.8 %shard_map.88 = (bf16[2,8,256,256]{3,2,1,0:T(8,128)(2,1)S(1)}, bf16[2,8,256,256]{3,2,1,0:T(8,128)(2,1)S(1)}, bf16[65,64,64]{2,1,0:T(8,128)(2,1)S(1)}, bf16[64,64,64]{2,1,0:T(8,128)(2,1)S(1)}) custom-call(s32[4]{0:T(128)S(1)} %pad_add_fusion.idx_ref.refs_0_, bf16[2,8,256,256]{3,2,1,0:T(8,128)(2,1)} %shard_map.87.own_ref, ...), custom_call_target="tpu_custom_call" | custom-call | flops 2200000000 | bytes 1048576 | tf_op jit(solution)/shard_map/pallas_call | solution.py:428
  23.8 26.7 %all-to-all-done.recv_ref = bf16[16,2,2,128,128]{4,3,2,1,0:T(8,128)(2,1)S(1)} async-done(((bf16[16,2,2,128,128]{4,3,2,1,0:T(8,128)(2,1)}), bf16[16,2,2,128,128]{4,3,2,1,0:T(8,128)(2,1)S(1)}, u32[]{:S(2)}, u32[]{:S(2)}) %all-to-all-start) | async-done | bytes 2097184 | tf_op jit(solution)/shard_map/all_to_all | solution.py:450
  53.0 12.4 %all_to_all.50.refs_1_ = bf16[4,576,128]{2,1,0:T(8,128)(2,1)S(1)} all-to-all(bf16[4,576,128]{2,1,0:T(8,128)(2,1)S(1)} %shard_map.89), channel_id=1, replica_groups=mesh['section'=2,'z'=4,'x'=4,'dp'=4] {'x'}, dimensions={0} | all-to-all | bytes 1179648 | tf_op jit(solution)/shard_map/all_to_all | solution.py:453
  66.6 11.2 %all_to_all.51.in_ref = bf16[4,576,128]{2,1,0:T(8,128)(2,1)S(1)} all-to-all(bf16[4,576,128]{2,1,0:T(8,128)(2,1)S(1)} %get-tuple-element.23), channel_id=1, replica_groups=mesh['section'=2,'z'=4,'x'=4,'dp'=4] {'x'}, dimensions={0} | all-to-all | bytes 1179648 | tf_op jit(solution)/shard_map/all_to_all | solution.py:453
  77.8 5.4 %shard_map.91 = (bf16[16,2,128,128]{3,2,1,0:T(8,128)(2,1)S(1)}, bf16[16,2,128,128]{3,2,1,0:T(8,128)(2,1)S(1)}, bf16[4,576,128]{2,1,0:T(8,128)(2,1)S(1)}) custom-call(bf16[4,576,128]{2,1,0:T(8,128)(2,1)S(1)} %all_to_all.51.in_ref, bf16[16,2,2,128,128]{4,3,2,1,0:T(8,128)(2,1)S(1)} %all-to-all-done.recv_ref, bf16[128,128]{1,0:T(8,128)(2,1)S(1)} %copy-done.1, ...), custom_call_target="tpu_custom_call" | custom-call | flops 6600000000 | bytes 1048576 | tf_op jit(solution)/shard_map/pallas_call | solution.py:428
  83.3 10.8 %all_to_all.52.refs_1_ = bf16[4,576,128]{2,1,0:T(8,128)(2,1)S(1)} all-to-all(bf16[4,576,128]{2,1,0:T(8,128)(2,1)S(1)} %get-tuple-element.25), channel_id=1, replica_groups=mesh['section'=2,'z'=4,'x'=4,'dp'=4] {'x'}, dimensions={0} | all-to-all | bytes 1179648 | tf_op jit(solution)/shard_map/all_to_all | solution.py:453
  95.3 10.8 %all_to_all.53.in_ref = bf16[4,576,128]{2,1,0:T(8,128)(2,1)S(1)} all-to-all(bf16[4,576,128]{2,1,0:T(8,128)(2,1)S(1)} %get-tuple-element.27), channel_id=1, replica_groups=mesh['section'=2,'z'=4,'x'=4,'dp'=4] {'x'}, dimensions={0} | all-to-all | bytes 1179648 | tf_op jit(solution)/shard_map/all_to_all | solution.py:453
  106.1 5.5 %shard_map.93 = (bf16[16,2,128,128]{3,2,1,0:T(8,128)(2,1)S(1)}, bf16[4,576,128]{2,1,0:T(8,128)(2,1)S(1)}) custom-call(bf16[4,576,128]{2,1,0:T(8,128)(2,1)S(1)} %all_to_all.53.in_ref, bf16[16,2,2,128,128]{4,3,2,1,0:T(8,128)(2,1)S(1)} %all-to-all-done.recv_ref, bf16[16,2,128,128]{3,2,1,0:T(8,128)(2,1)S(1)} %get-tuple-element.28.h_ref, ...), custom_call_target="tpu_custom_call" | custom-call | flops 6600000000 | bytes 1048576 | tf_op jit(solution)/shard_map/pallas_call | solution.py:428
  111.6 10.8 %all_to_all.54.refs_1_ = bf16[4,576,128]{2,1,0:T(8,128)(2,1)S(1)} all-to-all(bf16[4,576,128]{2,1,0:T(8,128)(2,1)S(1)} %get-tuple-element.29), channel_id=1, replica_groups=mesh['section'=2,'z'=4,'x'=4,'dp'=4] {'x'}, dimensions={0} | all-to-all | bytes 1179648 | tf_op jit(solution)/shard_map/all_to_all | solution.py:453
  123.9 10.8 %all_to_all.55.in_ref = bf16[4,576,128]{2,1,0:T(8,128)(2,1)S(1)} all-to-all(bf16[4,576,128]{2,1,0:T(8,128)(2,1)S(1)} %get-tuple-element.30), channel_id=1, replica_groups=mesh['section'=2,'z'=4,'x'=4,'dp'=4] {'x'}, dimensions={0} | all-to-all | bytes 1179648 | tf_op jit(solution)/shard_map/all_to_all | solution.py:453
  134.8 4.8 %shard_map.95 = (bf16[16,2,128,128]{3,2,1,0:T(8,128)(2,1)S(1)}, bf16[4,576,128]{2,1,0:T(8,128)(2,1)S(1)}) custom-call(bf16[4,576,128]{2,1,0:T(8,128)(2,1)S(1)} %all_to_all.55.in_ref, bf16[16,2,2,128,128]{4,3,2,1,0:T(8,128)(2,1)S(1)} %all-to-all-done.recv_ref, bf16[16,2,128,128]{3,2,1,0:T(8,128)(2,1)S(1)} %get-tuple-element.31.slope_ref, ...), custom_call_target="tpu_custom_call" | custom-call | flops 5500000256 | bytes 1048576 | tf_op jit(solution)/shard_map/pallas_call | solution.py:428
  139.6 10.8 %all_to_all.56.refs_1_ = bf16[4,576,128]{2,1,0:T(8,128)(2,1)S(1)} all-to-all(bf16[4,576,128]{2,1,0:T(8,128)(2,1)S(1)} %get-tuple-element.32), channel_id=1, replica_groups=mesh['section'=2,'z'=4,'x'=4,'dp'=4] {'x'}, dimensions={0} | all-to-all | bytes 1179648 | tf_op jit(solution)/shard_map/all_to_all | solution.py:453
  151.9 2.6 %shard_map.100 = bf16[16,256,256]{2,1,0:T(8,128)(2,1)} custom-call(s32[4]{0:T(128)S(1)} %pad_add_fusion.idx_ref.refs_0_, bf16[8,144,256]{2,1,0:T(8,128)(2,1)S(1)} %get-tuple-element.36.refs_1_, bf16[8,144,256]{2,1,0:T(8,128)(2,1)S(1)} %get-tuple-element.37.refs_2_, bf16[8,144,256]{2,1,0:T(8,128)(2,1)S(1)} %get-tuple-element.38.refs_3_, ...), custom_call_target="tpu_custom_call" | custom-call | flops 3300000000 | bytes 1048576 | tf_op jit(solution)/shard_map/pallas_call | solution.py:428
  154.6 13.5 %all_to_all.57.in_ref = bf16[4,576,128]{2,1,0:T(8,128)(2,1)S(1)} all-to-all(bf16[4,576,128]{2,1,0:T(8,128)(2,1)S(1)} %get-tuple-element.33), channel_id=1, replica_groups=mesh['section'=2,'z'=4,'x'=4,'dp'=4] {'x'}, dimensions={0} | all-to-all | bytes 1179648 | tf_op jit(solution)/shard_map/all_to_all | solution.py:453
  168.1 3.8 %shard_map.97 = bf16[2,16,2,128,128]{4,3,2,1,0:T(8,128)(2,1)} custom-call(bf16[4,576,128]{2,1,0:T(8,128)(2,1)S(1)} %all_to_all.57.in_ref, bf16[16,2,128,128]{3,2,1,0:T(8,128)(2,1)S(1)} %get-tuple-element.34.g_ref, bf16[16,2,128,128]{3,2,1,0:T(8,128)(2,1)S(1)} %get-tuple-element.35.top_ref, bf16[128,128]{1,0:T(8,128)(2,1)S(1)} %copy-done.1, ...), custom_call_target="tpu_custom_call" | custom-call | flops 4400000000 | bytes 1048576 | tf_op jit(solution)/shard_map/pallas_call | solution.py:428
  171.9 4.2 %all-to-all-start.9 = ((bf16[32,2,128,128]{3,2,1,0:T(8,128)(2,1)}), bf16[32,2,128,128]{3,2,1,0:T(8,128)(2,1)S(1)}, u32[]{:S(2)}, u32[]{:S(2)}) async-start(bf16[32,2,128,128]{3,2,1,0:T(8,128)(2,1)} %bitcast.4), calls=%async_computation.9 | async-start | bytes 4194304 | tf_op jit(solution)/shard_map/all_to_all | solution.py:483
  187.2 10.1 %collective-permute-done.2 = bf16[4,256,256]{2,1,0:T(8,128)(2,1)S(1)} collective-permute-done((bf16[4,256,256]{2,1,0:T(8,128)(2,1)S(1)}, bf16[4,256,256]{2,1,0:T(8,128)(2,1)S(1)}, u32[]{:S(2)}, u32[]{:S(2)}) %collective-permute-start.2) | collective-permute-done | bytes 524320 | tf_op jit(solution)/shard_map/ppermute | solution.py:506
  197.3 10.6 %collective-permute-done.4 = bf16[4,256,256]{2,1,0:T(8,128)(2,1)S(1)} collective-permute-done((bf16[4,256,256]{2,1,0:T(8,128)(2,1)S(1)}, bf16[4,256,256]{2,1,0:T(8,128)(2,1)S(1)}, u32[]{:S(2)}, u32[]{:S(2)}) %collective-permute-start.4) | collective-permute-done | bytes 524320 | tf_op jit(solution)/shard_map/ppermute | solution.py:506
  210.7 6.9 %collective-permute-start.8 = (bf16[1,256,256]{2,1,0:T(8,128)(2,1)S(1)}, bf16[1,256,256]{2,1,0:T(8,128)(2,1)S(1)}, u32[]{:S(2)}, u32[]{:S(2)}) collective-permute-start(bf16[1,256,256]{2,1,0:T(8,128)(2,1)S(1)} %get-tuple-element.44), channel_id=1, source_target_pairs={{0,60},{4,56},{8,52},{12,48},{16,0},{20,4},{24,8},{28,12},{32,16},... | collective-permute-start | bytes 393224 | tf_op jit(solution)/shard_map/ppermute | solution.py:506
  218.0 3.5 %collective-permute-start.6 = (bf16[1,256,256]{2,1,0:T(8,128)(2,1)S(1)}, bf16[1,256,256]{2,1,0:T(8,128)(2,1)S(1)}, u32[]{:S(2)}, u32[]{:S(2)}) collective-permute-start(bf16[1,256,256]{2,1,0:T(8,128)(2,1)S(1)} %get-tuple-element.46), channel_id=1, source_target_pairs={{0,16},{4,20},{8,24},{12,28},{16,44},{20,40},{24,36},{28,32},{32,6... | collective-permute-start | bytes 393224 | tf_op jit(solution)/shard_map/ppermute | solution.py:506
  223.1 3.8 %collective-permute-done.7 = bf16[1,256,256]{2,1,0:T(8,128)(2,1)S(1)} collective-permute-done((bf16[1,256,256]{2,1,0:T(8,128)(2,1)S(1)}, bf16[1,256,256]{2,1,0:T(8,128)(2,1)S(1)}, u32[]{:S(2)}, u32[]{:S(2)}) %collective-permute-start.7) | collective-permute-done | bytes 131104 | tf_op jit(solution)/shard_map/ppermute | solution.py:506
  (61 shorter events, 29.6 us)
Async XLA Ops:
  4.2 12.1 %collective-permute-start = (bf16[2,8,256,256]{3,2,1,0:T(8,128)(2,1)}, bf16[2,8,256,256]{3,2,1,0:T(8,128)(2,1)}, u32[]{:S(2)}, u32[]{:S(2)}) collective-permute-start(bf16[2,8,256,256]{3,2,1,0:T(8,128)(2,1)} %shard_map.87.own_ref), channel_id=1, source_target_pairs={{0,64},{64,0},{1,65},{65,1},{2,66},{66,2},{3,67},{67,3},{4,68},{68... | collective-permute-start | bytes 6291464 | tf_op jit(solution)/shard_map/ppermute | solution.py:444
  7.0 1.3 copy-start
  8.3 42.2 %all-to-all-start = ((bf16[16,2,2,128,128]{4,3,2,1,0:T(8,128)(2,1)}), bf16[16,2,2,128,128]{4,3,2,1,0:T(8,128)(2,1)S(1)}, u32[]{:S(2)}, u32[]{:S(2)}) async-start(bf16[16,2,2,128,128]{4,3,2,1,0:T(8,128)(2,1)} %copy-done), calls=%async_computation | async-start | bytes 4194304 | tf_op jit(solution)/shard_map/all_to_all | solution.py:450
  16.3 34.2 %copy-start.2 = (bf16[128,128]{1,0:T(8,128)(2,1)S(1)}, bf16[128,128]{1,0:T(8,128)(2,1)}, u32[]{:S(2)}) copy-start(bf16[128,128]{1,0:T(8,128)(2,1)} %constant.31.clone.ana_ref) | copy-start | bytes 98308
  20.1 1.3 copy-start.3
  50.5 14.9 %copy-start.4 = (bf16[2,8,256,256]{3,2,1,0:T(8,128)(2,1)S(1)}, bf16[2,8,256,256]{3,2,1,0:T(8,128)(2,1)}, u32[]{:S(2)}) copy-start(bf16[2,8,256,256]{3,2,1,0:T(8,128)(2,1)} %copy-done.3) | copy-start | bytes 6291460
  65.4 12.5 %copy-start.1 = (bf16[128,128]{1,0:T(8,128)(2,1)S(1)}, bf16[128,128]{1,0:T(8,128)(2,1)}, u32[]{:S(2)}) copy-start(bf16[128,128]{1,0:T(8,128)(2,1)} %constant.30.clone.syn_ref) | copy-start | bytes 98308
  65.4 12.5 %copy-start.8 = (bf16[64,64,64]{2,1,0:T(8,128)(2,1)S(1)}, bf16[64,64,64]{2,1,0:T(8,128)(2,1)}, u32[]{:S(2)}) copy-start(bf16[64,64,64]{2,1,0:T(8,128)(2,1)} %copy-done.7) | copy-start | bytes 1572868
  66.6 85.3 %copy-start.9 = (bf16[8,144,256]{2,1,0:T(8,128)(2,1)}, bf16[8,144,256]{2,1,0:T(8,128)(2,1)S(1)}, u32[]{:S(2)}) copy-start(bf16[8,144,256]{2,1,0:T(8,128)(2,1)S(1)} %get-tuple-element.36.refs_1_) | copy-start | bytes 1769476
  77.8 16.3 %copy-start.6 = (bf16[2,8,256,256]{3,2,1,0:T(8,128)(2,1)S(1)}, bf16[2,8,256,256]{3,2,1,0:T(8,128)(2,1)}, u32[]{:S(2)}) copy-start(bf16[2,8,256,256]{3,2,1,0:T(8,128)(2,1)} %copy-done.5) | copy-start | bytes 6291460
  95.3 56.6 %copy-start.11 = (bf16[8,144,256]{2,1,0:T(8,128)(2,1)}, bf16[8,144,256]{2,1,0:T(8,128)(2,1)S(1)}, u32[]{:S(2)}) copy-start(bf16[8,144,256]{2,1,0:T(8,128)(2,1)S(1)} %get-tuple-element.37.refs_2_) | copy-start | bytes 1769476
  123.9 28.0 %copy-start.13 = (bf16[8,144,256]{2,1,0:T(8,128)(2,1)}, bf16[8,144,256]{2,1,0:T(8,128)(2,1)S(1)}, u32[]{:S(2)}) copy-start(bf16[8,144,256]{2,1,0:T(8,128)(2,1)S(1)} %get-tuple-element.39.refs_4_) | copy-start | bytes 1769476
  151.9 2.7 %copy-start.15 = (bf16[8,144,256]{2,1,0:T(8,128)(2,1)}, bf16[8,144,256]{2,1,0:T(8,128)(2,1)S(1)}, u32[]{:S(2)}) copy-start(bf16[8,144,256]{2,1,0:T(8,128)(2,1)S(1)} %get-tuple-element.38.refs_3_) | copy-start | bytes 1769476
  154.6 25.0 %collective-permute-start.1 = (bf16[16,256,256]{2,1,0:T(8,128)(2,1)}, bf16[16,256,256]{2,1,0:T(8,128)(2,1)}, u32[]{:S(2)}, u32[]{:S(2)}) collective-permute-start(bf16[16,256,256]{2,1,0:T(8,128)(2,1)} %shard_map.100), channel_id=1, source_target_pairs={{0,64},{64,0},{1,65},{65,1},{2,66},{66,2},{3,67},{67,3},{4,68},{68... | collective-permute-start | bytes 6291464 | tf_op jit(solution)/shard_map/ppermute | solution.py:497
  171.9 4.2 %copy-start.10 = (bf16[8,144,256]{2,1,0:T(8,128)(2,1)S(1)}, bf16[8,144,256]{2,1,0:T(8,128)(2,1)}, u32[]{:S(2)}) copy-start(bf16[8,144,256]{2,1,0:T(8,128)(2,1)} %copy-done.9) | copy-start | bytes 1769476
  171.9 4.2 %copy-start.12 = (bf16[8,144,256]{2,1,0:T(8,128)(2,1)S(1)}, bf16[8,144,256]{2,1,0:T(8,128)(2,1)}, u32[]{:S(2)}) copy-start(bf16[8,144,256]{2,1,0:T(8,128)(2,1)} %copy-done.11) | copy-start | bytes 1769476
  171.9 49.6 %all-to-all-start.9 = ((bf16[32,2,128,128]{3,2,1,0:T(8,128)(2,1)}), bf16[32,2,128,128]{3,2,1,0:T(8,128)(2,1)S(1)}, u32[]{:S(2)}, u32[]{:S(2)}) async-start(bf16[32,2,128,128]{3,2,1,0:T(8,128)(2,1)} %bitcast.4), calls=%async_computation.9 | async-start | bytes 4194304 | tf_op jit(solution)/shard_map/all_to_all | solution.py:483
  181.9 15.4 %collective-permute-start.2 = (bf16[4,256,256]{2,1,0:T(8,128)(2,1)S(1)}, bf16[4,256,256]{2,1,0:T(8,128)(2,1)S(1)}, u32[]{:S(2)}, u32[]{:S(2)}) collective-permute-start(bf16[4,256,256]{2,1,0:T(8,128)(2,1)S(1)} %get-tuple-element.40), channel_id=1, source_target_pairs={{0,1},{1,2},{2,3},{3,0},{4,5},{5,6},{6,7},{7,4},{8,9},{9,10},{10,1... | collective-permute-start | bytes 1572872 | tf_op jit(solution)/shard_map/ppermute | solution.py:506
  183.6 24.4 %collective-permute-start.4 = (bf16[4,256,256]{2,1,0:T(8,128)(2,1)S(1)}, bf16[4,256,256]{2,1,0:T(8,128)(2,1)S(1)}, u32[]{:S(2)}, u32[]{:S(2)}) collective-permute-start(bf16[4,256,256]{2,1,0:T(8,128)(2,1)S(1)} %get-tuple-element.41), channel_id=1, source_target_pairs={{0,3},{1,0},{2,1},{3,2},{4,7},{5,4},{6,5},{7,6},{8,11},{9,8},{10,9... | collective-permute-start | bytes 1572872 | tf_op jit(solution)/shard_map/ppermute | solution.py:506
  185.2 24.5 %collective-permute-start.3 = (bf16[4,256,256]{2,1,0:T(8,128)(2,1)S(1)}, bf16[4,256,256]{2,1,0:T(8,128)(2,1)S(1)}, u32[]{:S(2)}, u32[]{:S(2)}) collective-permute-start(bf16[4,256,256]{2,1,0:T(8,128)(2,1)S(1)} %get-tuple-element.42), channel_id=1, source_target_pairs={{0,2},{1,3},{2,0},{3,1},{4,6},{5,7},{6,4},{7,5},{8,10},{9,11},{10,... | collective-permute-start | bytes 1572872 | tf_op jit(solution)/shard_map/ppermute | solution.py:506
  210.1 13.1 %collective-permute-start.5 = (bf16[1,256,256]{2,1,0:T(8,128)(2,1)S(1)}, bf16[1,256,256]{2,1,0:T(8,128)(2,1)S(1)}, u32[]{:S(2)}, u32[]{:S(2)}) collective-permute-start(bf16[1,256,256]{2,1,0:T(8,128)(2,1)S(1)} %get-tuple-element.43), channel_id=1, source_target_pairs={{0,0},{4,4},{8,8},{12,12},{16,16},{20,20},{24,24},{28,28},{32,44},... | collective-permute-start | bytes 393224 | tf_op jit(solution)/shard_map/ppermute | solution.py:506
  210.7 12.4 %collective-permute-start.8 = (bf16[1,256,256]{2,1,0:T(8,128)(2,1)S(1)}, bf16[1,256,256]{2,1,0:T(8,128)(2,1)S(1)}, u32[]{:S(2)}, u32[]{:S(2)}) collective-permute-start(bf16[1,256,256]{2,1,0:T(8,128)(2,1)S(1)} %get-tuple-element.44), channel_id=1, source_target_pairs={{0,60},{4,56},{8,52},{12,48},{16,0},{20,4},{24,8},{28,12},{32,16},... | collective-permute-start | bytes 393224 | tf_op jit(solution)/shard_map/ppermute | solution.py:506
  217.6 9.3 %collective-permute-start.7 = (bf16[1,256,256]{2,1,0:T(8,128)(2,1)S(1)}, bf16[1,256,256]{2,1,0:T(8,128)(2,1)S(1)}, u32[]{:S(2)}, u32[]{:S(2)}) collective-permute-start(bf16[1,256,256]{2,1,0:T(8,128)(2,1)S(1)} %get-tuple-element.45), channel_id=1, source_target_pairs={{0,44},{4,40},{8,36},{12,32},{16,60},{20,56},{24,52},{28,48},{32,0... | collective-permute-start | bytes 393224 | tf_op jit(solution)/shard_map/ppermute | solution.py:506
  218.0 8.9 %collective-permute-start.6 = (bf16[1,256,256]{2,1,0:T(8,128)(2,1)S(1)}, bf16[1,256,256]{2,1,0:T(8,128)(2,1)S(1)}, u32[]{:S(2)}, u32[]{:S(2)}) collective-permute-start(bf16[1,256,256]{2,1,0:T(8,128)(2,1)S(1)} %get-tuple-element.46), channel_id=1, source_target_pairs={{0,16},{4,20},{8,24},{12,28},{16,44},{20,40},{24,36},{28,32},{32,6... | collective-permute-start | bytes 393224 | tf_op jit(solution)/shard_map/ppermute | solution.py:506
  (4 other events, 4.4 us)

commit v4 on v3

--- a/solution.py
+++ b/solution.py
@@ -146,9 +146,9 @@
     return copy
 
 
-def pack_body(idx_ref, field_hbm, cot_hbm, out_ref, field_ref, cot_ref, sem):
+def pack_body(idx_ref, field_hbm, cot_hbm, out_hbm, field_ref, cot_ref, out_ref, sem):
     samples, rows, _, channels = field_ref.shape
-    loads = []
+    loads, saves = [], []
     for s in range(samples):
         at = s + samples * idx_ref[1]
         loads.append(begin(field_hbm.at[at], field_ref.at[s], sem.at[s]))
@@ -163,6 +163,10 @@
                     left, right = interleave(one.astype(F32), two.astype(F32))
                     out_ref[4 * s + 2 * t, i, q] = left.astype(BF16)
                     out_ref[4 * s + 2 * t + 1, i, q] = right.astype(BF16)
+        span = pl.ds(4 * s, 4)
+        saves.append(begin(out_ref.at[span], out_hbm.at[span], sem.at[2 * samples + s]))
+    for save in saves:
+        save.wait()
 
 
 def unpack_body(in_ref, out_hbm, out_ref, sem):
@@ -181,37 +185,33 @@
         save.wait()
 
 
-def select_body(idx_ref, weight_ref, out_ref, sem):
-    quarter = out_ref.shape[1] // 2
-    copies = []
-    for z in range(4):
-        at = 4 * quarter * z + quarter * (idx_ref[0] if z < 2 else 3 - idx_ref[0])
-        target = out_ref.at[z // 2, pl.ds((z % 2) * quarter, quarter)]
-        copies.append(begin(weight_ref.at[0, pl.ds(at, quarter)], target, sem.at[z]))
-    for copy in copies:
+def prepare_body(idx_ref, own_hbm, far_hbm, ta_hbm, ts_hbm, w0_ref, w1_ref, ta_ref, ts_ref, sem):
+    quarter = w0_ref.shape[1] // 2
+
+    def fetch(source, target, layer):
+        copies = []
+        for z in range(4):
+            at = 4 * quarter * z + quarter * (idx_ref[0] if z < 2 else 3 - idx_ref[0])
+            part = target.at[z // 2, pl.ds((z % 2) * quarter, quarter)]
+            origin = source.at[0, pl.ds(at, quarter)]
+            copies.append(pltpu.make_async_copy(origin, part, sem.at[4 * layer + z]))
+        return copies
+
+    tables = [begin(ta_hbm, ta_ref, sem.at[8]), begin(ts_hbm, ts_ref, sem.at[9])]
+    front = idx_ref[1] == 0
+
+    @pl.when(front)
+    def _():
+        for copy in fetch(own_hbm, w0_ref, 0) + fetch(far_hbm, w1_ref, 1):
+            copy.start()
+
+    @pl.when(jnp.logical_not(front))
+    def _():
+        for copy in fetch(far_hbm, w0_ref, 0) + fetch(own_hbm, w1_ref, 1):
+            copy.start()
+
+    for copy in fetch(own_hbm, w0_ref, 0) + fetch(own_hbm, w1_ref, 1) + tables:
         copy.wait()
-
-
-def prepare_body(idx_ref, own_ref, far_ref, ta_hbm, ts_hbm, w0_ref, w1_ref, ta_ref, ts_ref, sem):
-    def fetch(source, target, at):
-        return pltpu.make_async_copy(source, target, sem.at[at])
-
-    tables = [begin(ta_hbm, ta_ref, sem.at[2]), begin(ts_hbm, ts_ref, sem.at[3])]
-
-    @pl.when(idx_ref[1] == 0)
-    def _():
-        fetch(own_ref, w0_ref, 0).start()
-        fetch(far_ref, w1_ref, 1).start()
-
-    @pl.when(idx_ref[1] == 1)
-    def _():
-        fetch(far_ref, w0_ref, 0).start()
-        fetch(own_ref, w1_ref, 1).start()
-
-    fetch(own_ref, w0_ref, 0).wait()
-    fetch(own_ref, w1_ref, 1).wait()
-    for table in tables:
-        table.wait()
 
 
 def store_spectrum(q, value, spec_ref):
@@ -278,11 +278,24 @@
     return pre * cdf, cdf + pre * density
 
 
+def beside(first, second):
+    return jnp.concatenate([first, second], axis=1)
+
+
+def spectra_at(d, grid_ref):
+    return beside(spectrum_at(2 * d, grid_ref), spectrum_at(2 * d + 1, grid_ref))
+
+
+def store_spectra(d, value, spec_ref):
+    for q in range(2):
+        store_spectrum(2 * d + q, value[:, q * 128 : (q + 1) * 128], spec_ref)
+
+
 def first_body(recv_ref, ana_ref, ta_ref, out_ref, spec_ref, slot_ref):
     basis = ana_ref[...]
     for d in range(recv_ref.shape[0]):
-        for q in range(2):
-            store_spectrum(2 * d + q, dot(basis, recv_ref[d, 0, q]), spec_ref)
+        field = beside(recv_ref[d, 0, 0], recv_ref[d, 0, 1])
+        store_spectra(d, dot(basis, field), spec_ref)
     analyse(spec_ref, ta_ref, slot_ref, out_ref)
 
 
@@ -291,12 +304,15 @@
     synthesise(in_ref, ts_ref, slot_ref, grid_ref)
     syn, ana = syn_ref[...], ana_ref[...]
     for d in range(recv_ref.shape[0]):
+        pre = dot(syn, spectra_at(d, grid_ref))
+        made = []
         for q in range(2):
-            value, slope = gelu_parts(dot(syn, spectrum_at(2 * d + q, grid_ref)))
+            value, slope = gelu_parts(pre[:, q * 128 : (q + 1) * 128])
             slope_ref[d, q] = slope.astype(BF16)
             h = (recv_ref[d, 0, q].astype(F32) + value).astype(BF16)
             h_ref[d, q] = h
-            store_spectrum(2 * d + q, dot(ana, h), spec_ref)
+            made.append(h)
+        store_spectra(d, dot(ana, beside(*made)), spec_ref)
     analyse(spec_ref, ta_ref, slot_ref, out_ref)
 
 
@@ -305,11 +321,13 @@
     synthesise(in_ref, ts_ref, slot_ref, grid_ref)
     syn, ana = syn_ref[...], ana_ref[...]
     for d in range(recv_ref.shape[0]):
+        pre = dot(syn, spectra_at(d, grid_ref))
+        made = []
         for q in range(2):
-            value, slope = gelu_parts(dot(syn, spectrum_at(2 * d + q, grid_ref)))
+            value, slope = gelu_parts(pre[:, q * 128 : (q + 1) * 128])
             top_ref[d, q] = (h_ref[d, q].astype(F32) + value).astype(BF16)
-            gpre = (recv_ref[d, 1, q].astype(F32) * slope).astype(BF16)
-            store_spectrum(2 * d + q, dot(ana, gpre), spec_ref)
+            made.append((recv_ref[d, 1, q].astype(F32) * slope).astype(BF16))
+        store_spectra(d, dot(ana, beside(*made)), spec_ref)
     analyse(spec_ref, ta_ref, slot_ref, out_ref)
 
 
@@ -318,12 +336,13 @@
     synthesise(in_ref, ts_ref, slot_ref, grid_ref)
     syn, ana = syn_ref[...], ana_ref[...]
     for d in range(recv_ref.shape[0]):
+        back = dot(syn, spectra_at(d, grid_ref))
+        made = []
         for q in range(2):
-            back = dot(syn, spectrum_at(2 * d + q, grid_ref))
-            g = (recv_ref[d, 1, q].astype(F32) + back).astype(BF16)
+            g = (recv_ref[d, 1, q].astype(F32) + back[:, q * 128 : (q + 1) * 128]).astype(BF16)
             g_ref[d, q] = g
-            gpre = (g.astype(F32) * slope_ref[d, q].astype(F32)).astype(BF16)
-            store_spectrum(2 * d + q, dot(ana, gpre), spec_ref)
+            made.append((g.astype(F32) * slope_ref[d, q].astype(F32)).astype(BF16))
+        store_spectra(d, dot(ana, beside(*made)), spec_ref)
     analyse(spec_ref, ta_ref, slot_ref, out_ref)
 
 
@@ -332,9 +351,10 @@
     synthesise(in_ref, ts_ref, slot_ref, grid_ref)
     syn = syn_ref[...]
     for d in range(g_ref.shape[0]):
+        back = dot(syn, spectra_at(d, grid_ref))
         for q in range(2):
-            back = dot(syn, spectrum_at(2 * d + q, grid_ref))
-            ends_ref[0, d, q] = (g_ref[d, q].astype(F32) + back).astype(BF16)
+            part = back[:, q * 128 : (q + 1) * 128]
+            ends_ref[0, d, q] = (g_ref[d, q].astype(F32) + part).astype(BF16)
     move.wait()
 
 
@@ -376,19 +396,49 @@
             out_ref[2 * t + 1, span] = right.astype(BF16)
 
 
-def grad_body(flip, idx_ref, coef0_ref, coef1_ref, grad0_ref, grad1_ref, out_ref):
-    pairs = coef0_ref.shape[0]
+def grad_body(idx_ref, coef_ref, grad_ref, out_ref):
+    pairs = coef_ref.shape[0]
     over = (((0,), (0,)), ((), ()))
-    first = idx_ref[1] == (1 if flip else 0)
     for r in range(pairs):
-        coef = jnp.where(first, coef0_ref[r].astype(F32), coef1_ref[r].astype(F32)).astype(BF16)
-        grad = jnp.where(first, grad0_ref[r].astype(F32), grad1_ref[r].astype(F32))
+        grad = grad_ref[r].astype(F32)
         lower = lower_rows(idx_ref[0], r)
         pieces = (jnp.where(lower, grad, 0.0), jnp.where(lower, 0.0, grad))
         for at, piece in zip((r, 2 * pairs - 1 - r), pieces):
             place = 4 * ((at % 4 + 4 - idx_ref[2]) % 4) + (at // 4 + 4 - idx_ref[3]) % 4
-            made = lax.dot_general(coef, piece.astype(BF16), over, preferred_element_type=F32)
+            made = lax.dot_general(
+                coef_ref[r], piece.astype(BF16), over, preferred_element_type=F32
+            )
             out_ref[place] = made.astype(BF16)
+
+
+def add_body(first_ref, second_ref, *parts):
+    for k, part_ref in enumerate(parts):
+        for i in range(4):
+            total = first_ref[4 * k + i].astype(F32) + second_ref[4 * k + i].astype(F32)
+            part_ref[i] = total.astype(BF16)
+
+
+def fold_body(idx_ref, *refs):
+    parts = refs[8:]
+
+    def write(first, second, third, fourth):
+        for k, part_ref in enumerate(parts):
+            total = first[k].astype(F32) + second[k].astype(F32)
+            part_ref[0] = (total + third[k].astype(F32) + fourth[k].astype(F32)).astype(BF16)
+
+    @pl.when(idx_ref[1] == 0)
+    def _():
+        write(*refs[:4])
+
+    @pl.when(idx_ref[1] == 1)
+    def _():
+        write(*refs[4:8])
+
+
+def mean_body(count, first, second, third, fourth, out_ref):
+    total = first[...].astype(F32) + second[...].astype(F32)
+    total += third[...].astype(F32) + fourth[...].astype(F32)
+    out_ref[...] = total / count
 
 
 def local(ta, ts, fields_in, cotangent, weights):
@@ -437,15 +487,15 @@
 
     quarter_field = pltpu.VMEM((samples, lat_rows, longitudes, channels), BF16)
     packed = call(
-        3, pack_body, [smem, hbm, hbm], pltpu.VMEM((16, 2) + half_shape[1:], BF16),
-        [quarter_field] * 2, idx, far_away(fields_in), far_away(cotangent), sems=2 * samples,
-    )
-    own = call(2, select_body, [smem, hbm], chosen, [], idx, far_away(weights), sems=4)
-    far = lax.ppermute(own, "section", swap)
+        3, pack_body, [smem, hbm, hbm], pltpu.HBM((16, 2) + half_shape[1:], BF16),
+        [quarter_field] * 2 + [pltpu.VMEM((16, 2) + half_shape[1:], BF16)],
+        idx, far_away(fields_in), far_away(cotangent), sems=3 * samples, outs=hbm,
+    )
+    far = lax.ppermute(weights, "section", swap)
     w0, w1, ta, ts = call(
-        2, prepare_body, [smem, vmem, vmem, hbm, hbm],
+        2, prepare_body, [smem] + [hbm] * 4,
         [chosen, chosen, pltpu.VMEM(ta.shape, BF16), pltpu.VMEM(ts.shape, BF16)], [],
-        idx, near(own), near(far), far_away(ta), far_away(ts), sems=4,
+        idx, far_away(weights), far_away(far), far_away(ta), far_away(ts), sems=10,
     )
     recv = near(lax.all_to_all(packed, ("z", "x"), 0, 0, tiled=True))
 
@@ -457,6 +507,28 @@
             mix_body(backward, *refs)
 
         return call(2, body, [smem, vmem, vmem], [spec, coef], [], idx, value, weight)
+
+    row = pltpu.VMEM((4, channels, channels), BF16)
+    single = pltpu.VMEM((1, channels, channels), BF16)
+
+    def exchange(parts, axes, routes):
+        return [
+            part if route is None else near(lax.ppermute(part, axes, route))
+            for part, route in zip(parts, routes)
+        ]
+
+    def along_dp(first, second, layer):
+        made = call(3, grad_body, [smem, vmem, vmem], product, [], idx, first, second)
+        got = near(lax.ppermute(made, "section", [(1 - layer, layer)]))
+        parts = call(2, add_body, [vmem] * 2, [row] * 4, [], made, got)
+        routes = [None]
+        for k in range(1, 4):
+            routes.append([(4 * layer + i, 4 * layer + (i + k) % 4) for i in range(4)])
+        return exchange(parts, ("section", "dp"), routes)
+
+    def together(value, others):
+        value, *others = lax.optimization_barrier((value, *others))
+        return near(value), [near(other) for other in others]
 
     value = call(3, first_body, [vmem] * 3, spec, [tall, slots], recv, ana, ta)
     value, coef0 = mix_call(turn(value), w0, False)
@@ -475,9 +547,11 @@
         turn(value), recv, slope, syn, ana, ts, ta,
     )
     value, grad0 = mix_call(turn(value), w0, True)
+    grad0, parts1 = together(grad0, along_dp(coef1, grad1, 1))
+    value = turn(value)
     ends = call(
         4, back0_body, [vmem] * 5, pltpu.VMEM((2,) + half_shape, BF16), [tall, slots],
-        turn(value), g1, top, syn, ts, sems=1,
+        value, g1, top, syn, ts, sems=1,
     )
     ends = ends.reshape((32,) + half_shape[1:])
     ends = near(lax.all_to_all(ends, ("section", "z", "x"), 0, 0, tiled=True))
@@ -486,28 +560,6 @@
         [pltpu.VMEM(fields_in.shape, BF16)], ends, sems=rows_all, outs=hbm,
     )[None]
 
-    def grad_call(flip):
-        def body(*refs):
-            grad_body(flip, *refs)
-
-        return call(
-            3, body, [smem] + [vmem] * 4, product, [], idx, coef0, coef1, grad0, grad1
-        )
-
-    got = lax.ppermute(grad_call(True), "section", swap)
-    both = (grad_call(False).astype(F32) + got.astype(F32)).astype(BF16)
-
-    def fold(value, axes, routes):
-        step = value.shape[0] // 4
-        total = 0.0
-        for k, route in enumerate(routes):
-            block = value[k * step : (k + 1) * step]
-            if route is not None:
-                block = lax.ppermute(block, axes, route)
-            total += block.astype(F32)
-        return total
-
-    along = [None] + [[(i, (i + k) % 4) for i in range(4)] for k in range(1, 4)]
     across = []
     for k in range(4):
         across.append([])
@@ -515,9 +567,16 @@
             for x in range(4):
                 there = (z + k) % 4
                 across[k].append((4 * z + x, 4 * there + (x if there < 2 else 3 - x)))
-    total = fold(fold(both, "dp", along).astype(BF16), ("z", "x"), across)
+    parts0 = along_dp(coef0, grad0, 0)
+    parts = call(2, fold_body, [smem] + [vmem] * 8, [single] * 4, [], idx, *parts0, *parts1)
+    parts = exchange(parts, ("z", "x"), across)
     batch_count = rows_all * lax.axis_size("dp")
-    return (section_ends, (total / batch_count)[None])
+
+    def mean(*refs):
+        mean_body(batch_count, *refs)
+
+    total = call(1, mean, [vmem] * 4, jax.ShapeDtypeStruct(single.shape, F32), [], *parts)
+    return (section_ends, total[None])
 
 
 def solution(mesh):

time: 228 us -> 223 us (0.978); the launches traced: 228 us -> 220 us
  starting transfers between devices: 28.9 us -> 46.5 us
  waiting for transfers between devices: 53 us -> 39.4 us
  blocking collectives: 91.2 us -> 78 us
  Pallas kernels: 42.9 us -> 48.4 us
  other arithmetic: 3.33 us -> 0.08 us
    ppermute x9 -> x13, waiting for transfers between devices: 26.3 us -> 12.2 us  [the longest x10 10.4 us: exchange(): lax.ppermute(part, axes, route)]
    all_to_all x8 -> x7, blocking collectives: 91.2 us -> 78 us  [turn(): return near(lax.all_to_all(value, 'x', 0, 0, tiled=True))]
    ppermute x9 -> x13, starting transfers between devices: 16.8 us -> 26.4 us  [the longest x10 22.5 us: exchange(): lax.ppermute(part, axes, route)]
    pallas_call x15 -> x18, Pallas kernels: 42.9 us -> 48.4 us  [call(): pl.pallas_call(body, in_specs=ins, out_specs=outs or ([vmem] * len(shapes...]
    all_to_all x1, starting transfers between devices: 4.16 us -> 8.59 us  [local(): ends = near(lax.all_to_all(ends, ('section', 'z', 'x'), 0, 0, tiled=True))]
    all_to_all x0 -> x1, starting transfers between devices: none -> 3.48 us  [turn(): return near(lax.all_to_all(value, 'x', 0, 0, tiled=True))]
    convert_element_type x2 -> x0, other arithmetic: 2.48 us -> none  [the longest x1 2.22 us: local(): both = (grad_call(False).astype(F32) + got.astype(F32)).astype(BF16)]
    unnamed x34 -> x40, local copies, waits for them, and re-layouts: 7.12 us -> 7.08 us
  transfers between devices with their start and end apart: 11 -> 16, of which waited for: 5 -> 8; matrix products, arithmetic and copies ran while one was open for 1% -> 0% of each run, Pallas kernels for 6% -> 12%
where the time goes in v4:
time: 223 us; the launch traced here: 220 us
  blocking collectives  78 us (35%)
  Pallas kernels  48.4 us (22%)
  starting transfers between devices  46.5 us (21%)
  waiting for transfers between devices  39.4 us (18%)
  local copies, waits for them, and re-layouts  7.08 us (3%)
    all_to_all x7, blocking collectives, turn(): return near(lax.all_to_all(value, 'x', 0, 0, tiled=True))  78 us
    pallas_call x18, Pallas kernels, call(): pl.pallas_call(body, in_specs=ins, out_specs=outs or ([vmem] * len(shapes...  48.4 us
    all_to_all x1, waiting for transfers between devices, local(): recv = near(lax.all_to_all(packed, ('z', 'x'), 0, 0, tiled=True))  25.2 us
    ppermute x10, starting transfers between devices, exchange(): lax.ppermute(part, axes, route)  22.5 us
    ppermute x10, waiting for transfers between devices, exchange(): lax.ppermute(part, axes, route)  10.4 us
    all_to_all x1, starting transfers between devices, local(): ends = near(lax.all_to_all(ends, ('section', 'z', 'x'), 0, 0, tiled=True))  8.59 us
    all_to_all x1, starting transfers between devices, local(): recv = near(lax.all_to_all(packed, ('z', 'x'), 0, 0, tiled=True))  7.97 us
    unnamed x40, local copies, waits for them, and re-layouts  7.08 us
  transfers between devices with their start and end apart: 16, of which 8 were waited for; matrix products, arithmetic and copies ran while one was open for 0% of the time, Pallas kernels for 12%

profile of v4, /device:TPU:0, one launch (start us, length us, event | category | flops | bytes accessed | tf_op | source)
XLA Modules:
  0.0 220.4 jit_solution(18142775501134087737)
XLA Ops:
  0.8 3.5 %shard_map.86 = bf16[16,2,2,128,128]{4,3,2,1,0:T(8,128)(2,1)} custom-call(s32[4]{0:T(128)S(1)} %pad_add_fusion.idx_ref.refs_0_, bf16[8,4,128,256]{3,2,1,0:T(8,128)(2,1)} %field_hbm.1, bf16[8,4,128,256]{3,2,1,0:T(8,128)(2,1)} %cot_hbm.1), custom_call_target="tpu_custom_call" | custom-call | flops 3300000000 | bytes 1048576 | tf_op jit(solution)/shard_map/pallas_call | solution.py:478
  4.3 8.0 %all-to-all-start = ((bf16[16,2,2,128,128]{4,3,2,1,0:T(8,128)(2,1)}), bf16[16,2,2,128,128]{4,3,2,1,0:T(8,128)(2,1)S(1)}, u32[]{:S(2)}, u32[]{:S(2)}) async-start(bf16[16,2,2,128,128]{4,3,2,1,0:T(8,128)(2,1)} %shard_map.86), calls=%async_computation | async-start | bytes 4194304 | tf_op jit(solution)/shard_map/all_to_all | solution.py:500
  14.2 3.4 %shard_map.87 = (bf16[2,8,256,256]{3,2,1,0:T(8,128)(2,1)S(1)}, bf16[2,8,256,256]{3,2,1,0:T(8,128)(2,1)S(1)}, bf16[65,64,64]{2,1,0:T(8,128)(2,1)S(1)}, bf16[64,64,64]{2,1,0:T(8,128)(2,1)S(1)}) custom-call(s32[4]{0:T(128)S(1)} %pad_add_fusion.idx_ref.refs_0_, bf16[1,64,256,256]{3,2,1,0:T(8,128)(2,1)} %own_hbm.1, ...), custom_call_target="tpu_custom_call" | custom-call | flops 2200000000 | bytes 1048576 | tf_op jit(solution)/shard_map/pallas_call | solution.py:478
  21.3 25.2 %all-to-all-done.recv_ref = bf16[16,2,2,128,128]{4,3,2,1,0:T(8,128)(2,1)S(1)} async-done(((bf16[16,2,2,128,128]{4,3,2,1,0:T(8,128)(2,1)}), bf16[16,2,2,128,128]{4,3,2,1,0:T(8,128)(2,1)S(1)}, u32[]{:S(2)}, u32[]{:S(2)}) %all-to-all-start) | async-done | bytes 2097184 | tf_op jit(solution)/shard_map/all_to_all | solution.py:500
  48.7 12.4 %all_to_all.50.refs_1_ = bf16[4,576,128]{2,1,0:T(8,128)(2,1)S(1)} all-to-all(bf16[4,576,128]{2,1,0:T(8,128)(2,1)S(1)} %shard_map.88), channel_id=1, replica_groups=mesh['section'=2,'z'=4,'x'=4,'dp'=4] {'x'}, dimensions={0} | all-to-all | bytes 1179648 | tf_op jit(solution)/shard_map/all_to_all | solution.py:503
  62.3 11.3 %all_to_all.51.in_ref = bf16[4,576,128]{2,1,0:T(8,128)(2,1)S(1)} all-to-all(bf16[4,576,128]{2,1,0:T(8,128)(2,1)S(1)} %get-tuple-element.40), channel_id=1, replica_groups=mesh['section'=2,'z'=4,'x'=4,'dp'=4] {'x'}, dimensions={0} | all-to-all | bytes 1179648 | tf_op jit(solution)/shard_map/all_to_all | solution.py:503
  73.6 4.8 %shard_map.90 = (bf16[16,2,128,128]{3,2,1,0:T(8,128)(2,1)S(1)}, bf16[16,2,128,128]{3,2,1,0:T(8,128)(2,1)S(1)}, bf16[4,576,128]{2,1,0:T(8,128)(2,1)S(1)}) custom-call(bf16[4,576,128]{2,1,0:T(8,128)(2,1)S(1)} %all_to_all.51.in_ref, bf16[16,2,2,128,128]{4,3,2,1,0:T(8,128)(2,1)S(1)} %all-to-all-done.recv_ref, bf16[128,128]{1,0:T(8,128)(2,1)S(1)} %copy-done.10, ...), custom_call_target="tpu_custom_call" | custom-call | flops 6600000000 | bytes 1048576 | tf_op jit(solution)/shard_map/pallas_call | solution.py:478
  78.4 10.8 %all_to_all.52.refs_1_ = bf16[4,576,128]{2,1,0:T(8,128)(2,1)S(1)} all-to-all(bf16[4,576,128]{2,1,0:T(8,128)(2,1)S(1)} %get-tuple-element.42), channel_id=1, replica_groups=mesh['section'=2,'z'=4,'x'=4,'dp'=4] {'x'}, dimensions={0} | all-to-all | bytes 1179648 | tf_op jit(solution)/shard_map/all_to_all | solution.py:503
  90.4 10.8 %all_to_all.53.in_ref = bf16[4,576,128]{2,1,0:T(8,128)(2,1)S(1)} all-to-all(bf16[4,576,128]{2,1,0:T(8,128)(2,1)S(1)} %get-tuple-element.44), channel_id=1, replica_groups=mesh['section'=2,'z'=4,'x'=4,'dp'=4] {'x'}, dimensions={0} | all-to-all | bytes 1179648 | tf_op jit(solution)/shard_map/all_to_all | solution.py:503
  101.2 4.9 %shard_map.92 = (bf16[16,2,128,128]{3,2,1,0:T(8,128)(2,1)S(1)}, bf16[4,576,128]{2,1,0:T(8,128)(2,1)S(1)}) custom-call(bf16[4,576,128]{2,1,0:T(8,128)(2,1)S(1)} %all_to_all.53.in_ref, bf16[16,2,2,128,128]{4,3,2,1,0:T(8,128)(2,1)S(1)} %all-to-all-done.recv_ref, bf16[16,2,128,128]{3,2,1,0:T(8,128)(2,1)S(1)} %get-tuple-element.45.h_ref, ...), custom_call_target="tpu_custom_call" | custom-call | flops 6600000000 | bytes 1048576 | tf_op jit(solution)/shard_map/pallas_call | solution.py:478
  106.1 10.8 %all_to_all.54.refs_1_ = bf16[4,576,128]{2,1,0:T(8,128)(2,1)S(1)} all-to-all(bf16[4,576,128]{2,1,0:T(8,128)(2,1)S(1)} %get-tuple-element.46), channel_id=1, replica_groups=mesh['section'=2,'z'=4,'x'=4,'dp'=4] {'x'}, dimensions={0} | all-to-all | bytes 1179648 | tf_op jit(solution)/shard_map/all_to_all | solution.py:503
  123.7 10.8 %all_to_all.55.in_ref = bf16[4,576,128]{2,1,0:T(8,128)(2,1)S(1)} all-to-all(bf16[4,576,128]{2,1,0:T(8,128)(2,1)S(1)} %get-tuple-element.47), channel_id=1, replica_groups=mesh['section'=2,'z'=4,'x'=4,'dp'=4] {'x'}, dimensions={0} | all-to-all | bytes 1179648 | tf_op jit(solution)/shard_map/all_to_all | solution.py:503
  134.5 5.1 %shard_map.94 = (bf16[16,2,128,128]{3,2,1,0:T(8,128)(2,1)S(1)}, bf16[4,576,128]{2,1,0:T(8,128)(2,1)}) custom-call(bf16[4,576,128]{2,1,0:T(8,128)(2,1)S(1)} %all_to_all.55.in_ref, bf16[16,2,2,128,128]{4,3,2,1,0:T(8,128)(2,1)S(1)} %all-to-all-done.recv_ref, bf16[16,2,128,128]{3,2,1,0:T(8,128)(2,1)S(1)} %get-tuple-element.48.slope_ref, ...), custom_call_target="tpu_custom_call" | custom-call | flops 5500000256 | bytes 1048576 | tf_op jit(solution)/shard_map/pallas_call | solution.py:478
  140.7 3.5 %all-to-all-start.7 = ((bf16[4,576,128]{2,1,0:T(8,128)(2,1)}), bf16[4,576,128]{2,1,0:T(8,128)(2,1)S(1)}, u32[]{:S(2)}, u32[]{:S(2)}) async-start(bf16[4,576,128]{2,1,0:T(8,128)(2,1)} %get-tuple-element.49), calls=%async_computation.7 | async-start | bytes 1179648 | tf_op jit(solution)/shard_map/all_to_all | solution.py:503
  144.1 3.3 %shard_map.99 = (bf16[4,256,256]{2,1,0:T(8,128)(2,1)S(1)}, bf16[4,256,256]{2,1,0:T(8,128)(2,1)}, bf16[4,256,256]{2,1,0:T(8,128)(2,1)}, bf16[4,256,256]{2,1,0:T(8,128)(2,1)S(1)}) custom-call(bf16[16,256,256]{2,1,0:T(8,128)(2,1)} %shard_map.98.first_ref, bf16[16,256,256]{2,1,0:T(8,128)(2,1)} %collective-permute-done.1.second_ref), custom_call_target="tpu_custom_call" | custom-call | flops 2200000000 | bytes 1048576 | tf_op jit(solution)/shard_map/pallas_call | solution.py:478
  159.7 11.1 %all_to_all.56.in_ref = bf16[4,576,128]{2,1,0:T(8,128)(2,1)S(1)} all-to-all(bf16[4,576,128]{2,1,0:T(8,128)(2,1)S(1)} %get-tuple-element.50), channel_id=1, replica_groups=mesh['section'=2,'z'=4,'x'=4,'dp'=4] {'x'}, dimensions={0} | all-to-all | bytes 1179648 | tf_op jit(solution)/shard_map/all_to_all | solution.py:503
  170.7 3.7 %shard_map.96 = bf16[2,16,2,128,128]{4,3,2,1,0:T(8,128)(2,1)} custom-call(bf16[4,576,128]{2,1,0:T(8,128)(2,1)S(1)} %all_to_all.56.in_ref, bf16[16,2,128,128]{3,2,1,0:T(8,128)(2,1)S(1)} %copy-done.19, bf16[16,2,128,128]{3,2,1,0:T(8,128)(2,1)S(1)} %copy-done.17, bf16[128,128]{1,0:T(8,128)(2,1)S(1)} %copy-done.10, bf16[64,64,64]{2,1,0:T(8,128)(2,1)S(1)} %copy-done.7), custom_call_target="tpu_custom_call" | custom-call | flops 4400000000 | bytes 1048576 | tf_op jit(solution)/shard_map/pallas_call | solution.py:478
  174.5 8.6 %all-to-all-start.9 = ((bf16[32,2,128,128]{3,2,1,0:T(8,128)(2,1)}), bf16[32,2,128,128]{3,2,1,0:T(8,128)(2,1)S(1)}, u32[]{:S(2)}, u32[]{:S(2)}) async-start(bf16[32,2,128,128]{3,2,1,0:T(8,128)(2,1)} %bitcast.4), calls=%async_computation.9 | async-start | bytes 4194304 | tf_op jit(solution)/shard_map/all_to_all | solution.py:557
  183.1 2.8 %shard_map.101 = (bf16[4,256,256]{2,1,0:T(8,128)(2,1)S(1)}, bf16[4,256,256]{2,1,0:T(8,128)(2,1)S(1)}, bf16[4,256,256]{2,1,0:T(8,128)(2,1)S(1)}, bf16[4,256,256]{2,1,0:T(8,128)(2,1)S(1)}) custom-call(bf16[16,256,256]{2,1,0:T(8,128)(2,1)} %shard_map.100.first_ref, bf16[16,256,256]{2,1,0:T(8,128)(2,1)} %collective-permute-done.5.second_ref), custom_call_target="tpu_custom_call" | custom-call | flops 2200000000 | bytes 1048576 | tf_op jit(solution)/shard_map/pallas_call | solution.py:478
  185.9 4.4 %collective-permute-start.6 = (bf16[4,256,256]{2,1,0:T(8,128)(2,1)S(1)}, bf16[4,256,256]{2,1,0:T(8,128)(2,1)S(1)}, u32[]{:S(2)}, u32[]{:S(2)}) collective-permute-start(bf16[4,256,256]{2,1,0:T(8,128)(2,1)S(1)} %get-tuple-element.63), channel_id=1, source_target_pairs={{0,1},{1,2},{2,3},{3,0},{4,5},{5,6},{6,7},{7,4},{8,9},{9,10},{10,1... | collective-permute-start | bytes 1572872 | tf_op jit(solution)/shard_map/ppermute | solution.py:516
  190.3 3.5 %collective-permute-start.7 = (bf16[4,256,256]{2,1,0:T(8,128)(2,1)S(1)}, bf16[4,256,256]{2,1,0:T(8,128)(2,1)S(1)}, u32[]{:S(2)}, u32[]{:S(2)}) collective-permute-start(bf16[4,256,256]{2,1,0:T(8,128)(2,1)S(1)} %get-tuple-element.64), channel_id=1, source_target_pairs={{0,2},{1,3},{2,0},{3,1},{4,6},{5,7},{6,4},{7,5},{8,10},{9,11},{10,... | collective-permute-start | bytes 1572872 | tf_op jit(solution)/shard_map/ppermute | solution.py:516
  193.8 3.6 %collective-permute-start.8 = (bf16[4,256,256]{2,1,0:T(8,128)(2,1)S(1)}, bf16[4,256,256]{2,1,0:T(8,128)(2,1)S(1)}, u32[]{:S(2)}, u32[]{:S(2)}) collective-permute-start(bf16[4,256,256]{2,1,0:T(8,128)(2,1)S(1)} %get-tuple-element.65), channel_id=1, source_target_pairs={{0,3},{1,0},{2,1},{3,2},{4,7},{5,4},{6,5},{7,6},{8,11},{9,8},{10,9... | collective-permute-start | bytes 1572872 | tf_op jit(solution)/shard_map/ppermute | solution.py:516
  198.2 6.5 %collective-permute-done.7.refs_2_ = bf16[4,256,256]{2,1,0:T(8,128)(2,1)S(1)} collective-permute-done((bf16[4,256,256]{2,1,0:T(8,128)(2,1)S(1)}, bf16[4,256,256]{2,1,0:T(8,128)(2,1)S(1)}, u32[]{:S(2)}, u32[]{:S(2)}) %collective-permute-start.7) | collective-permute-done | bytes 524320 | tf_op jit(solution)/shard_map/ppermute | solution.py:516
  209.8 4.8 %collective-permute-start.11 = (bf16[1,256,256]{2,1,0:T(8,128)(2,1)S(1)}, bf16[1,256,256]{2,1,0:T(8,128)(2,1)S(1)}, u32[]{:S(2)}, u32[]{:S(2)}) collective-permute-start(bf16[1,256,256]{2,1,0:T(8,128)(2,1)S(1)} %get-tuple-element.72), channel_id=1, source_target_pairs={{0,44},{4,40},{8,36},{12,32},{16,60},{20,56},{24,52},{28,48},{32,0... | collective-permute-start | bytes 393224 | tf_op jit(solution)/shard_map/ppermute | solution.py:516
  (74 shorter events, 41.9 us)
Async XLA Ops:
  0.6 13.6 %collective-permute-start = (bf16[1,64,256,256]{3,2,1,0:T(8,128)(2,1)}, bf16[1,64,256,256]{3,2,1,0:T(8,128)(2,1)}, u32[]{:S(2)}, u32[]{:S(2)}) collective-permute-start(bf16[1,64,256,256]{3,2,1,0:T(8,128)(2,1)} %own_hbm.1), channel_id=1, source_target_pairs={{0,64},{64,0},{1,65},{65,1},{2,66},{66,2},{3,67},{67,3},{4,68},{68... | collective-permute-start | bytes 25165832 | tf_op jit(solution)/shard_map/ppermute | solution.py:494
  4.3 42.1 %all-to-all-start = ((bf16[16,2,2,128,128]{4,3,2,1,0:T(8,128)(2,1)}), bf16[16,2,2,128,128]{4,3,2,1,0:T(8,128)(2,1)S(1)}, u32[]{:S(2)}, u32[]{:S(2)}) async-start(bf16[16,2,2,128,128]{4,3,2,1,0:T(8,128)(2,1)} %shard_map.86), calls=%async_computation | async-start | bytes 4194304 | tf_op jit(solution)/shard_map/all_to_all | solution.py:500
  12.3 34.2 %copy-start.11 = (bf16[128,128]{1,0:T(8,128)(2,1)S(1)}, bf16[128,128]{1,0:T(8,128)(2,1)}, u32[]{:S(2)}) copy-start(bf16[128,128]{1,0:T(8,128)(2,1)} %constant.28.clone.ana_ref) | copy-start | bytes 98308
  62.3 16.1 %copy-start.14 = (bf16[8,144,256]{2,1,0:T(8,128)(2,1)}, bf16[8,144,256]{2,1,0:T(8,128)(2,1)S(1)}, u32[]{:S(2)}) copy-start(bf16[8,144,256]{2,1,0:T(8,128)(2,1)S(1)} %get-tuple-element.53.coef_ref) | copy-start | bytes 1769476
  73.6 15.6 %copy-start.4 = (bf16[2,8,256,256]{3,2,1,0:T(8,128)(2,1)S(1)}, bf16[2,8,256,256]{3,2,1,0:T(8,128)(2,1)}, u32[]{:S(2)}) copy-start(bf16[2,8,256,256]{3,2,1,0:T(8,128)(2,1)} %copy-done.3) | copy-start | bytes 6291460
  121.1 23.0 %collective-permute-start.1 = (bf16[16,256,256]{2,1,0:T(8,128)(2,1)}, bf16[16,256,256]{2,1,0:T(8,128)(2,1)}, u32[]{:S(2)}, u32[]{:S(2)}) collective-permute-start(bf16[16,256,256]{2,1,0:T(8,128)(2,1)} %shard_map.98.first_ref), channel_id=1, source_target_pairs={{0,64},{1,65},{2,66},{3,67},{4,68},{5,69},{6,70},{7,71},{8,72},{9,... | collective-permute-start | bytes 6291464 | tf_op jit(solution)/shard_map/ppermute | solution.py:522
  140.7 11.9 %all-to-all-start.7 = ((bf16[4,576,128]{2,1,0:T(8,128)(2,1)}), bf16[4,576,128]{2,1,0:T(8,128)(2,1)S(1)}, u32[]{:S(2)}, u32[]{:S(2)}) async-start(bf16[4,576,128]{2,1,0:T(8,128)(2,1)} %get-tuple-element.49), calls=%async_computation.7 | async-start | bytes 1179648 | tf_op jit(solution)/shard_map/all_to_all | solution.py:503
  148.3 7.3 %collective-permute-start.2 = (bf16[4,256,256]{2,1,0:T(8,128)(2,1)}, bf16[4,256,256]{2,1,0:T(8,128)(2,1)S(1)}, u32[]{:S(2)}, u32[]{:S(2)}) collective-permute-start(bf16[4,256,256]{2,1,0:T(8,128)(2,1)} %get-tuple-element.58), channel_id=1, source_target_pairs={{64,65},{65,66},{66,67},{67,64},{68,69},{69,70},{70,71},{71,68},{7... | collective-permute-start | bytes 1572872 | tf_op jit(solution)/shard_map/ppermute | solution.py:516
  149.0 6.6 %collective-permute-start.3 = (bf16[4,256,256]{2,1,0:T(8,128)(2,1)}, bf16[4,256,256]{2,1,0:T(8,128)(2,1)S(1)}, u32[]{:S(2)}, u32[]{:S(2)}) collective-permute-start(bf16[4,256,256]{2,1,0:T(8,128)(2,1)} %get-tuple-element.59), channel_id=1, source_target_pairs={{64,66},{65,67},{66,64},{67,65},{68,70},{69,71},{70,68},{71,69},{7... | collective-permute-start | bytes 1572872 | tf_op jit(solution)/shard_map/ppermute | solution.py:516
  149.7 5.9 %collective-permute-start.4 = (bf16[4,256,256]{2,1,0:T(8,128)(2,1)S(1)}, bf16[4,256,256]{2,1,0:T(8,128)(2,1)S(1)}, u32[]{:S(2)}, u32[]{:S(2)}) collective-permute-start(bf16[4,256,256]{2,1,0:T(8,128)(2,1)S(1)} %get-tuple-element.60), channel_id=1, source_target_pairs={{64,67},{65,64},{66,65},{67,66},{68,71},{69,68},{70,69},{71,70},{7... | collective-permute-start | bytes 1572872 | tf_op jit(solution)/shard_map/ppermute | solution.py:516
  155.6 15.1 %copy-start.7 = (bf16[64,64,64]{2,1,0:T(8,128)(2,1)S(1)}, bf16[64,64,64]{2,1,0:T(8,128)(2,1)}, u32[]{:S(2)}) copy-start(bf16[64,64,64]{2,1,0:T(8,128)(2,1)} %copy-done.5) | copy-start | bytes 1572868
  155.7 15.1 %copy-start.17 = (bf16[16,2,128,128]{3,2,1,0:T(8,128)(2,1)S(1)}, bf16[16,2,128,128]{3,2,1,0:T(8,128)(2,1)}, u32[]{:S(2)}) copy-start(bf16[16,2,128,128]{3,2,1,0:T(8,128)(2,1)} %copy-done.16) | copy-start | bytes 3145732
  155.7 15.1 %copy-start.19 = (bf16[16,2,128,128]{3,2,1,0:T(8,128)(2,1)S(1)}, bf16[16,2,128,128]{3,2,1,0:T(8,128)(2,1)}, u32[]{:S(2)}) copy-start(bf16[16,2,128,128]{3,2,1,0:T(8,128)(2,1)} %copy-done.18) | copy-start | bytes 3145732
  158.4 24.7 %collective-permute-start.5 = (bf16[16,256,256]{2,1,0:T(8,128)(2,1)}, bf16[16,256,256]{2,1,0:T(8,128)(2,1)}, u32[]{:S(2)}, u32[]{:S(2)}) collective-permute-start(bf16[16,256,256]{2,1,0:T(8,128)(2,1)} %shard_map.100.first_ref), channel_id=1, source_target_pairs={{64,0},{65,1},{66,2},{67,3},{68,4},{69,5},{70,6},{71,7},{72,8},{73... | collective-permute-start | bytes 6291464 | tf_op jit(solution)/shard_map/ppermute | solution.py:522
  174.5 42.3 %all-to-all-start.9 = ((bf16[32,2,128,128]{3,2,1,0:T(8,128)(2,1)}), bf16[32,2,128,128]{3,2,1,0:T(8,128)(2,1)S(1)}, u32[]{:S(2)}, u32[]{:S(2)}) async-start(bf16[32,2,128,128]{3,2,1,0:T(8,128)(2,1)} %bitcast.4), calls=%async_computation.9 | async-start | bytes 4194304 | tf_op jit(solution)/shard_map/all_to_all | solution.py:557
  183.1 23.5 %copy-start.9 = (bf16[4,256,256]{2,1,0:T(8,128)(2,1)S(1)}, bf16[4,256,256]{2,1,0:T(8,128)(2,1)}, u32[]{:S(2)}) copy-start(bf16[4,256,256]{2,1,0:T(8,128)(2,1)} %copy-done.8) | copy-start | bytes 1572868
  183.1 23.5 %copy-start.13 = (bf16[4,256,256]{2,1,0:T(8,128)(2,1)S(1)}, bf16[4,256,256]{2,1,0:T(8,128)(2,1)}, u32[]{:S(2)}) copy-start(bf16[4,256,256]{2,1,0:T(8,128)(2,1)} %copy-done.12) | copy-start | bytes 1572868
  185.9 12.3 %collective-permute-start.6 = (bf16[4,256,256]{2,1,0:T(8,128)(2,1)S(1)}, bf16[4,256,256]{2,1,0:T(8,128)(2,1)S(1)}, u32[]{:S(2)}, u32[]{:S(2)}) collective-permute-start(bf16[4,256,256]{2,1,0:T(8,128)(2,1)S(1)} %get-tuple-element.63), channel_id=1, source_target_pairs={{0,1},{1,2},{2,3},{3,0},{4,5},{5,6},{6,7},{7,4},{8,9},{9,10},{10,1... | collective-permute-start | bytes 1572872 | tf_op jit(solution)/shard_map/ppermute | solution.py:516
  190.3 14.4 %collective-permute-start.7 = (bf16[4,256,256]{2,1,0:T(8,128)(2,1)S(1)}, bf16[4,256,256]{2,1,0:T(8,128)(2,1)S(1)}, u32[]{:S(2)}, u32[]{:S(2)}) collective-permute-start(bf16[4,256,256]{2,1,0:T(8,128)(2,1)S(1)} %get-tuple-element.64), channel_id=1, source_target_pairs={{0,2},{1,3},{2,0},{3,1},{4,6},{5,7},{6,4},{7,5},{8,10},{9,11},{10,... | collective-permute-start | bytes 1572872 | tf_op jit(solution)/shard_map/ppermute | solution.py:516
  193.8 12.8 %collective-permute-start.8 = (bf16[4,256,256]{2,1,0:T(8,128)(2,1)S(1)}, bf16[4,256,256]{2,1,0:T(8,128)(2,1)S(1)}, u32[]{:S(2)}, u32[]{:S(2)}) collective-permute-start(bf16[4,256,256]{2,1,0:T(8,128)(2,1)S(1)} %get-tuple-element.65), channel_id=1, source_target_pairs={{0,3},{1,0},{2,1},{3,2},{4,7},{5,4},{6,5},{7,6},{8,11},{9,8},{10,9... | collective-permute-start | bytes 1572872 | tf_op jit(solution)/shard_map/ppermute | solution.py:516
  208.1 10.4 %collective-permute-start.10 = (bf16[1,256,256]{2,1,0:T(8,128)(2,1)}, bf16[1,256,256]{2,1,0:T(8,128)(2,1)S(1)}, u32[]{:S(2)}, u32[]{:S(2)}) collective-permute-start(bf16[1,256,256]{2,1,0:T(8,128)(2,1)} %get-tuple-element.71), channel_id=1, source_target_pairs={{0,16},{4,20},{8,24},{12,28},{16,44},{20,40},{24,36},{28,32},{32,6... | collective-permute-start | bytes 393224 | tf_op jit(solution)/shard_map/ppermute | solution.py:516
  209.8 9.1 %collective-permute-start.11 = (bf16[1,256,256]{2,1,0:T(8,128)(2,1)S(1)}, bf16[1,256,256]{2,1,0:T(8,128)(2,1)S(1)}, u32[]{:S(2)}, u32[]{:S(2)}) collective-permute-start(bf16[1,256,256]{2,1,0:T(8,128)(2,1)S(1)} %get-tuple-element.72), channel_id=1, source_target_pairs={{0,44},{4,40},{8,36},{12,32},{16,60},{20,56},{24,52},{28,48},{32,0... | collective-permute-start | bytes 393224 | tf_op jit(solution)/shard_map/ppermute | solution.py:516
  214.6 5.0 %collective-permute-start.12 = (bf16[1,256,256]{2,1,0:T(8,128)(2,1)S(1)}, bf16[1,256,256]{2,1,0:T(8,128)(2,1)S(1)}, u32[]{:S(2)}, u32[]{:S(2)}) collective-permute-start(bf16[1,256,256]{2,1,0:T(8,128)(2,1)S(1)} %get-tuple-element.73), channel_id=1, source_target_pairs={{0,60},{4,56},{8,52},{12,48},{16,0},{20,4},{24,8},{28,12},{32,16},... | collective-permute-start | bytes 393224 | tf_op jit(solution)/shard_map/ppermute | solution.py:516
  216.1 3.5 %collective-permute-start.9 = (bf16[1,256,256]{2,1,0:T(8,128)(2,1)S(1)}, bf16[1,256,256]{2,1,0:T(8,128)(2,1)S(1)}, u32[]{:S(2)}, u32[]{:S(2)}) collective-permute-start(bf16[1,256,256]{2,1,0:T(8,128)(2,1)S(1)} %get-tuple-element.70), channel_id=1, source_target_pairs={{0,0},{4,4},{8,8},{12,12},{16,16},{20,20},{24,24},{28,28},{32,44},... | collective-permute-start | bytes 393224 | tf_op jit(solution)/shard_map/ppermute | solution.py:516
  (12 other events, 63.2 us)

commit v5 on v4

--- a/solution.py
+++ b/solution.py
@@ -547,7 +547,9 @@
         turn(value), recv, slope, syn, ana, ts, ta,
     )
     value, grad0 = mix_call(turn(value), w0, True)
-    grad0, parts1 = together(grad0, along_dp(coef1, grad1, 1))
+    parts1 = along_dp(coef1, grad1, 1)
+    grad0, early = together(grad0, [parts1[k] for k in (0, 1, 3)])
+    parts1 = [early[0], early[1], parts1[2], early[2]]
     value = turn(value)
     ends = call(
         4, back0_body, [vmem] * 5, pltpu.VMEM((2,) + half_shape, BF16), [tall, slots],

time: 223 us -> 222 us (level)
  starting transfers between devices: 46.5 us -> 42.9 us
    all_to_all x1, starting transfers between devices: 8.59 us -> 4.8 us  [local(): ends = near(lax.all_to_all(ends, ('section', 'z', 'x'), 0, 0, tiled=True))]
    unnamed x40 -> x38, local copies, waits for them, and re-layouts: 7.08 us -> 7.86 us
where the time goes in v5:
time: 222 us; the launch traced here: 219 us
  blocking collectives  79.3 us (36%)
  Pallas kernels  47.7 us (21%)
  starting transfers between devices  42.9 us (19%)
  waiting for transfers between devices  39.8 us (18%)
  local copies, waits for them, and re-layouts  7.86 us (4%)
    all_to_all x7, blocking collectives, turn(): return near(lax.all_to_all(value, 'x', 0, 0, tiled=True))  79.3 us
    pallas_call x18, Pallas kernels, call(): pl.pallas_call(body, in_specs=ins, out_specs=outs or ([vmem] * len(shapes...  47.7 us
    all_to_all x1, waiting for transfers between devices, local(): recv = near(lax.all_to_all(packed, ('z', 'x'), 0, 0, tiled=True))  25.2 us
    ppermute x10, starting transfers between devices, exchange(): lax.ppermute(part, axes, route)  22.7 us
    ppermute x10, waiting for transfers between devices, exchange(): lax.ppermute(part, axes, route)  10.3 us
    all_to_all x1, starting transfers between devices, local(): recv = near(lax.all_to_all(packed, ('z', 'x'), 0, 0, tiled=True))  7.97 us
    unnamed x38, local copies, waits for them, and re-layouts  7.86 us
    all_to_all x1, starting transfers between devices, local(): ends = near(lax.all_to_all(ends, ('section', 'z', 'x'), 0, 0, tiled=True))  4.8 us
  transfers between devices with their start and end apart: 16, of which 8 were waited for; matrix products, arithmetic and copies ran while one was open for 0% of the time, Pallas kernels for 12%

profile of v5, /device:TPU:0, one launch (start us, length us, event | category | flops | bytes accessed | tf_op | source)
XLA Modules:
  0.0 218.7 jit_solution(7038027474372444786)
XLA Ops:
  0.8 3.5 %shard_map.86 = bf16[16,2,2,128,128]{4,3,2,1,0:T(8,128)(2,1)} custom-call(s32[4]{0:T(128)S(1)} %pad_add_fusion.idx_ref.refs_0_, bf16[8,4,128,256]{3,2,1,0:T(8,128)(2,1)} %field_hbm.1, bf16[8,4,128,256]{3,2,1,0:T(8,128)(2,1)} %cot_hbm.1), custom_call_target="tpu_custom_call" | custom-call | flops 3300000000 | bytes 1048576 | tf_op jit(solution)/shard_map/pallas_call | solution.py:478
  4.3 8.0 %all-to-all-start = ((bf16[16,2,2,128,128]{4,3,2,1,0:T(8,128)(2,1)}), bf16[16,2,2,128,128]{4,3,2,1,0:T(8,128)(2,1)S(1)}, u32[]{:S(2)}, u32[]{:S(2)}) async-start(bf16[16,2,2,128,128]{4,3,2,1,0:T(8,128)(2,1)} %shard_map.86), calls=%async_computation | async-start | bytes 4194304 | tf_op jit(solution)/shard_map/all_to_all | solution.py:500
  14.2 3.4 %shard_map.87 = (bf16[2,8,256,256]{3,2,1,0:T(8,128)(2,1)S(1)}, bf16[2,8,256,256]{3,2,1,0:T(8,128)(2,1)S(1)}, bf16[65,64,64]{2,1,0:T(8,128)(2,1)S(1)}, bf16[64,64,64]{2,1,0:T(8,128)(2,1)S(1)}) custom-call(s32[4]{0:T(128)S(1)} %pad_add_fusion.idx_ref.refs_0_, bf16[1,64,256,256]{3,2,1,0:T(8,128)(2,1)} %own_hbm.1, ...), custom_call_target="tpu_custom_call" | custom-call | flops 2200000000 | bytes 1048576 | tf_op jit(solution)/shard_map/pallas_call | solution.py:478
  21.3 25.2 %all-to-all-done.recv_ref = bf16[16,2,2,128,128]{4,3,2,1,0:T(8,128)(2,1)S(1)} async-done(((bf16[16,2,2,128,128]{4,3,2,1,0:T(8,128)(2,1)}), bf16[16,2,2,128,128]{4,3,2,1,0:T(8,128)(2,1)S(1)}, u32[]{:S(2)}, u32[]{:S(2)}) %all-to-all-start) | async-done | bytes 2097184 | tf_op jit(solution)/shard_map/all_to_all | solution.py:500
  48.7 12.4 %all_to_all.50.refs_1_ = bf16[4,576,128]{2,1,0:T(8,128)(2,1)S(1)} all-to-all(bf16[4,576,128]{2,1,0:T(8,128)(2,1)S(1)} %shard_map.88), channel_id=1, replica_groups=mesh['section'=2,'z'=4,'x'=4,'dp'=4] {'x'}, dimensions={0} | all-to-all | bytes 1179648 | tf_op jit(solution)/shard_map/all_to_all | solution.py:503
  62.3 11.3 %all_to_all.51.in_ref = bf16[4,576,128]{2,1,0:T(8,128)(2,1)S(1)} all-to-all(bf16[4,576,128]{2,1,0:T(8,128)(2,1)S(1)} %get-tuple-element.39), channel_id=1, replica_groups=mesh['section'=2,'z'=4,'x'=4,'dp'=4] {'x'}, dimensions={0} | all-to-all | bytes 1179648 | tf_op jit(solution)/shard_map/all_to_all | solution.py:503
  73.6 4.8 %shard_map.90 = (bf16[16,2,128,128]{3,2,1,0:T(8,128)(2,1)S(1)}, bf16[16,2,128,128]{3,2,1,0:T(8,128)(2,1)S(1)}, bf16[4,576,128]{2,1,0:T(8,128)(2,1)S(1)}) custom-call(bf16[4,576,128]{2,1,0:T(8,128)(2,1)S(1)} %all_to_all.51.in_ref, bf16[16,2,2,128,128]{4,3,2,1,0:T(8,128)(2,1)S(1)} %all-to-all-done.recv_ref, bf16[128,128]{1,0:T(8,128)(2,1)S(1)} %copy-done.9, ...), custom_call_target="tpu_custom_call" | custom-call | flops 6600000000 | bytes 1048576 | tf_op jit(solution)/shard_map/pallas_call | solution.py:478
  78.4 10.8 %all_to_all.52.refs_1_ = bf16[4,576,128]{2,1,0:T(8,128)(2,1)S(1)} all-to-all(bf16[4,576,128]{2,1,0:T(8,128)(2,1)S(1)} %get-tuple-element.41), channel_id=1, replica_groups=mesh['section'=2,'z'=4,'x'=4,'dp'=4] {'x'}, dimensions={0} | all-to-all | bytes 1179648 | tf_op jit(solution)/shard_map/all_to_all | solution.py:503
  90.4 10.8 %all_to_all.53.in_ref = bf16[4,576,128]{2,1,0:T(8,128)(2,1)S(1)} all-to-all(bf16[4,576,128]{2,1,0:T(8,128)(2,1)S(1)} %get-tuple-element.43), channel_id=1, replica_groups=mesh['section'=2,'z'=4,'x'=4,'dp'=4] {'x'}, dimensions={0} | all-to-all | bytes 1179648 | tf_op jit(solution)/shard_map/all_to_all | solution.py:503
  101.2 4.9 %shard_map.92 = (bf16[16,2,128,128]{3,2,1,0:T(8,128)(2,1)S(1)}, bf16[4,576,128]{2,1,0:T(8,128)(2,1)S(1)}) custom-call(bf16[4,576,128]{2,1,0:T(8,128)(2,1)S(1)} %all_to_all.53.in_ref, bf16[16,2,2,128,128]{4,3,2,1,0:T(8,128)(2,1)S(1)} %all-to-all-done.recv_ref, bf16[16,2,128,128]{3,2,1,0:T(8,128)(2,1)S(1)} %get-tuple-element.44.h_ref, ...), custom_call_target="tpu_custom_call" | custom-call | flops 6600000000 | bytes 1048576 | tf_op jit(solution)/shard_map/pallas_call | solution.py:478
  106.1 10.8 %all_to_all.54.refs_1_ = bf16[4,576,128]{2,1,0:T(8,128)(2,1)S(1)} all-to-all(bf16[4,576,128]{2,1,0:T(8,128)(2,1)S(1)} %get-tuple-element.45), channel_id=1, replica_groups=mesh['section'=2,'z'=4,'x'=4,'dp'=4] {'x'}, dimensions={0} | all-to-all | bytes 1179648 | tf_op jit(solution)/shard_map/all_to_all | solution.py:503
  123.7 10.8 %all_to_all.55.in_ref = bf16[4,576,128]{2,1,0:T(8,128)(2,1)S(1)} all-to-all(bf16[4,576,128]{2,1,0:T(8,128)(2,1)S(1)} %get-tuple-element.46), channel_id=1, replica_groups=mesh['section'=2,'z'=4,'x'=4,'dp'=4] {'x'}, dimensions={0} | all-to-all | bytes 1179648 | tf_op jit(solution)/shard_map/all_to_all | solution.py:503
  134.5 5.2 %shard_map.94 = (bf16[16,2,128,128]{3,2,1,0:T(8,128)(2,1)S(1)}, bf16[4,576,128]{2,1,0:T(8,128)(2,1)}) custom-call(bf16[4,576,128]{2,1,0:T(8,128)(2,1)S(1)} %all_to_all.55.in_ref, bf16[16,2,2,128,128]{4,3,2,1,0:T(8,128)(2,1)S(1)} %all-to-all-done.recv_ref, bf16[16,2,128,128]{3,2,1,0:T(8,128)(2,1)S(1)} %get-tuple-element.47.slope_ref, ...), custom_call_target="tpu_custom_call" | custom-call | flops 5500000256 | bytes 1048576 | tf_op jit(solution)/shard_map/pallas_call | solution.py:478
  140.6 3.5 %all-to-all-start.7 = ((bf16[4,576,128]{2,1,0:T(8,128)(2,1)}), bf16[4,576,128]{2,1,0:T(8,128)(2,1)S(1)}, u32[]{:S(2)}, u32[]{:S(2)}) async-start(bf16[4,576,128]{2,1,0:T(8,128)(2,1)} %get-tuple-element.48), calls=%async_computation.7 | async-start | bytes 1179648 | tf_op jit(solution)/shard_map/all_to_all | solution.py:503
  144.1 2.7 %shard_map.99 = (bf16[4,256,256]{2,1,0:T(8,128)(2,1)S(1)}, bf16[4,256,256]{2,1,0:T(8,128)(2,1)S(1)}, bf16[4,256,256]{2,1,0:T(8,128)(2,1)S(1)}, bf16[4,256,256]{2,1,0:T(8,128)(2,1)S(1)}) custom-call(bf16[16,256,256]{2,1,0:T(8,128)(2,1)} %shard_map.98.first_ref, bf16[16,256,256]{2,1,0:T(8,128)(2,1)} %collective-permute-done.1.second_ref), custom_call_target="tpu_custom_call" | custom-call | flops 2200000000 | bytes 1048576 | tf_op jit(solution)/shard_map/pallas_call | solution.py:478
  159.6 12.4 %all_to_all.56.in_ref = bf16[4,576,128]{2,1,0:T(8,128)(2,1)S(1)} all-to-all(bf16[4,576,128]{2,1,0:T(8,128)(2,1)S(1)} %get-tuple-element.49), channel_id=1, replica_groups=mesh['section'=2,'z'=4,'x'=4,'dp'=4] {'x'}, dimensions={0} | all-to-all | bytes 1179648 | tf_op jit(solution)/shard_map/all_to_all | solution.py:503
  172.1 3.8 %shard_map.96 = bf16[2,16,2,128,128]{4,3,2,1,0:T(8,128)(2,1)} custom-call(bf16[4,576,128]{2,1,0:T(8,128)(2,1)S(1)} %all_to_all.56.in_ref, bf16[16,2,128,128]{3,2,1,0:T(8,128)(2,1)S(1)} %copy-done.18, bf16[16,2,128,128]{3,2,1,0:T(8,128)(2,1)S(1)} %copy-done.16, bf16[128,128]{1,0:T(8,128)(2,1)S(1)} %copy-done.9, bf16[64,64,64]{2,1,0:T(8,128)(2,1)S(1)} %copy-done.7), custom_call_target="tpu_custom_call" | custom-call | flops 4400000000 | bytes 1048576 | tf_op jit(solution)/shard_map/pallas_call | solution.py:478
  175.8 4.8 %all-to-all-start.9 = ((bf16[32,2,128,128]{3,2,1,0:T(8,128)(2,1)}), bf16[32,2,128,128]{3,2,1,0:T(8,128)(2,1)S(1)}, u32[]{:S(2)}, u32[]{:S(2)}) async-start(bf16[32,2,128,128]{3,2,1,0:T(8,128)(2,1)} %bitcast.4), calls=%async_computation.9 | async-start | bytes 4194304 | tf_op jit(solution)/shard_map/all_to_all | solution.py:559
  184.2 3.5 %collective-permute-start.5 = (bf16[4,256,256]{2,1,0:T(8,128)(2,1)S(1)}, bf16[4,256,256]{2,1,0:T(8,128)(2,1)S(1)}, u32[]{:S(2)}, u32[]{:S(2)}) collective-permute-start(bf16[4,256,256]{2,1,0:T(8,128)(2,1)S(1)} %get-tuple-element.61), channel_id=1, source_target_pairs={{0,1},{1,2},{2,3},{3,0},{4,5},{5,6},{6,7},{7,4},{8,9},{9,10},{10,1... | collective-permute-start | bytes 1572872 | tf_op jit(solution)/shard_map/ppermute | solution.py:516
  187.7 4.8 %collective-permute-start.6 = (bf16[4,256,256]{2,1,0:T(8,128)(2,1)S(1)}, bf16[4,256,256]{2,1,0:T(8,128)(2,1)S(1)}, u32[]{:S(2)}, u32[]{:S(2)}) collective-permute-start(bf16[4,256,256]{2,1,0:T(8,128)(2,1)S(1)} %get-tuple-element.62), channel_id=1, source_target_pairs={{0,2},{1,3},{2,0},{3,1},{4,6},{5,7},{6,4},{7,5},{8,10},{9,11},{10,... | collective-permute-start | bytes 1572872 | tf_op jit(solution)/shard_map/ppermute | solution.py:516
  192.5 3.3 %collective-permute-start.7 = (bf16[4,256,256]{2,1,0:T(8,128)(2,1)S(1)}, bf16[4,256,256]{2,1,0:T(8,128)(2,1)S(1)}, u32[]{:S(2)}, u32[]{:S(2)}) collective-permute-start(bf16[4,256,256]{2,1,0:T(8,128)(2,1)S(1)} %get-tuple-element.63), channel_id=1, source_target_pairs={{0,3},{1,0},{2,1},{3,2},{4,7},{5,4},{6,5},{7,6},{8,11},{9,8},{10,9... | collective-permute-start | bytes 1572872 | tf_op jit(solution)/shard_map/ppermute | solution.py:516
  195.8 2.8 %collective-permute-done.5.refs_1_ = bf16[4,256,256]{2,1,0:T(8,128)(2,1)S(1)} collective-permute-done((bf16[4,256,256]{2,1,0:T(8,128)(2,1)S(1)}, bf16[4,256,256]{2,1,0:T(8,128)(2,1)S(1)}, u32[]{:S(2)}, u32[]{:S(2)}) %collective-permute-start.5) | collective-permute-done | bytes 524320 | tf_op jit(solution)/shard_map/ppermute | solution.py:516
  198.6 5.6 %collective-permute-done.6.refs_2_ = bf16[4,256,256]{2,1,0:T(8,128)(2,1)S(1)} collective-permute-done((bf16[4,256,256]{2,1,0:T(8,128)(2,1)S(1)}, bf16[4,256,256]{2,1,0:T(8,128)(2,1)S(1)}, u32[]{:S(2)}, u32[]{:S(2)}) %collective-permute-start.6) | collective-permute-done | bytes 524320 | tf_op jit(solution)/shard_map/ppermute | solution.py:516
  208.1 4.8 %collective-permute-start.11 = (bf16[1,256,256]{2,1,0:T(8,128)(2,1)S(1)}, bf16[1,256,256]{2,1,0:T(8,128)(2,1)S(1)}, u32[]{:S(2)}, u32[]{:S(2)}) collective-permute-start(bf16[1,256,256]{2,1,0:T(8,128)(2,1)S(1)} %get-tuple-element.70), channel_id=1, source_target_pairs={{0,44},{4,40},{8,36},{12,32},{16,60},{20,56},{24,52},{28,48},{32,0... | collective-permute-start | bytes 393224 | tf_op jit(solution)/shard_map/ppermute | solution.py:516
  (72 shorter events, 43.9 us)
Async XLA Ops:
  0.6 13.6 %collective-permute-start = (bf16[1,64,256,256]{3,2,1,0:T(8,128)(2,1)}, bf16[1,64,256,256]{3,2,1,0:T(8,128)(2,1)}, u32[]{:S(2)}, u32[]{:S(2)}) collective-permute-start(bf16[1,64,256,256]{3,2,1,0:T(8,128)(2,1)} %own_hbm.1), channel_id=1, source_target_pairs={{0,64},{64,0},{1,65},{65,1},{2,66},{66,2},{3,67},{67,3},{4,68},{68... | collective-permute-start | bytes 25165832 | tf_op jit(solution)/shard_map/ppermute | solution.py:494
  4.3 42.1 %all-to-all-start = ((bf16[16,2,2,128,128]{4,3,2,1,0:T(8,128)(2,1)}), bf16[16,2,2,128,128]{4,3,2,1,0:T(8,128)(2,1)S(1)}, u32[]{:S(2)}, u32[]{:S(2)}) async-start(bf16[16,2,2,128,128]{4,3,2,1,0:T(8,128)(2,1)} %shard_map.86), calls=%async_computation | async-start | bytes 4194304 | tf_op jit(solution)/shard_map/all_to_all | solution.py:500
  12.3 34.2 %copy-start.10 = (bf16[128,128]{1,0:T(8,128)(2,1)S(1)}, bf16[128,128]{1,0:T(8,128)(2,1)}, u32[]{:S(2)}) copy-start(bf16[128,128]{1,0:T(8,128)(2,1)} %constant.28.clone.ana_ref) | copy-start | bytes 98308
  46.5 14.6 %copy-start.1 = (bf16[2,8,256,256]{3,2,1,0:T(8,128)(2,1)S(1)}, bf16[2,8,256,256]{3,2,1,0:T(8,128)(2,1)}, u32[]{:S(2)}) copy-start(bf16[2,8,256,256]{3,2,1,0:T(8,128)(2,1)} %copy-done) | copy-start | bytes 6291460
  61.1 12.5 %copy-start.9 = (bf16[128,128]{1,0:T(8,128)(2,1)S(1)}, bf16[128,128]{1,0:T(8,128)(2,1)}, u32[]{:S(2)}) copy-start(bf16[128,128]{1,0:T(8,128)(2,1)} %constant.27.clone.syn_ref) | copy-start | bytes 98308
  73.6 15.6 %copy-start.4 = (bf16[2,8,256,256]{3,2,1,0:T(8,128)(2,1)S(1)}, bf16[2,8,256,256]{3,2,1,0:T(8,128)(2,1)}, u32[]{:S(2)}) copy-start(bf16[2,8,256,256]{3,2,1,0:T(8,128)(2,1)} %copy-done.3) | copy-start | bytes 6291460
  121.1 23.1 %collective-permute-start.1 = (bf16[16,256,256]{2,1,0:T(8,128)(2,1)}, bf16[16,256,256]{2,1,0:T(8,128)(2,1)}, u32[]{:S(2)}, u32[]{:S(2)}) collective-permute-start(bf16[16,256,256]{2,1,0:T(8,128)(2,1)} %shard_map.98.first_ref), channel_id=1, source_target_pairs={{0,64},{1,65},{2,66},{3,67},{4,68},{5,69},{6,70},{7,71},{8,72},{9,... | collective-permute-start | bytes 6291464 | tf_op jit(solution)/shard_map/ppermute | solution.py:522
  140.6 11.9 %all-to-all-start.7 = ((bf16[4,576,128]{2,1,0:T(8,128)(2,1)}), bf16[4,576,128]{2,1,0:T(8,128)(2,1)S(1)}, u32[]{:S(2)}, u32[]{:S(2)}) async-start(bf16[4,576,128]{2,1,0:T(8,128)(2,1)} %get-tuple-element.48), calls=%async_computation.7 | async-start | bytes 1179648 | tf_op jit(solution)/shard_map/all_to_all | solution.py:503
  148.4 7.2 %collective-permute-start.2 = (bf16[4,256,256]{2,1,0:T(8,128)(2,1)S(1)}, bf16[4,256,256]{2,1,0:T(8,128)(2,1)S(1)}, u32[]{:S(2)}, u32[]{:S(2)}) collective-permute-start(bf16[4,256,256]{2,1,0:T(8,128)(2,1)S(1)} %get-tuple-element.57), channel_id=1, source_target_pairs={{64,65},{65,66},{66,67},{67,64},{68,69},{69,70},{70,71},{71,68},{7... | collective-permute-start | bytes 1572872 | tf_op jit(solution)/shard_map/ppermute | solution.py:516
  149.1 6.5 %collective-permute-start.3 = (bf16[4,256,256]{2,1,0:T(8,128)(2,1)S(1)}, bf16[4,256,256]{2,1,0:T(8,128)(2,1)S(1)}, u32[]{:S(2)}, u32[]{:S(2)}) collective-permute-start(bf16[4,256,256]{2,1,0:T(8,128)(2,1)S(1)} %get-tuple-element.58), channel_id=1, source_target_pairs={{64,67},{65,64},{66,65},{67,66},{68,71},{69,68},{70,69},{71,70},{7... | collective-permute-start | bytes 1572872 | tf_op jit(solution)/shard_map/ppermute | solution.py:516
  155.6 16.4 %copy-start.7 = (bf16[64,64,64]{2,1,0:T(8,128)(2,1)S(1)}, bf16[64,64,64]{2,1,0:T(8,128)(2,1)}, u32[]{:S(2)}) copy-start(bf16[64,64,64]{2,1,0:T(8,128)(2,1)} %copy-done.5) | copy-start | bytes 1572868
  155.6 16.4 %copy-start.16 = (bf16[16,2,128,128]{3,2,1,0:T(8,128)(2,1)S(1)}, bf16[16,2,128,128]{3,2,1,0:T(8,128)(2,1)}, u32[]{:S(2)}) copy-start(bf16[16,2,128,128]{3,2,1,0:T(8,128)(2,1)} %copy-done.15) | copy-start | bytes 3145732
  155.6 16.4 %copy-start.18 = (bf16[16,2,128,128]{3,2,1,0:T(8,128)(2,1)S(1)}, bf16[16,2,128,128]{3,2,1,0:T(8,128)(2,1)}, u32[]{:S(2)}) copy-start(bf16[16,2,128,128]{3,2,1,0:T(8,128)(2,1)} %copy-done.17) | copy-start | bytes 3145732
  158.3 23.1 %collective-permute-start.4 = (bf16[16,256,256]{2,1,0:T(8,128)(2,1)}, bf16[16,256,256]{2,1,0:T(8,128)(2,1)}, u32[]{:S(2)}, u32[]{:S(2)}) collective-permute-start(bf16[16,256,256]{2,1,0:T(8,128)(2,1)} %shard_map.100.first_ref), channel_id=1, source_target_pairs={{64,0},{65,1},{66,2},{67,3},{68,4},{69,5},{70,6},{71,7},{72,8},{73... | collective-permute-start | bytes 6291464 | tf_op jit(solution)/shard_map/ppermute | solution.py:522
  175.8 39.2 %all-to-all-start.9 = ((bf16[32,2,128,128]{3,2,1,0:T(8,128)(2,1)}), bf16[32,2,128,128]{3,2,1,0:T(8,128)(2,1)S(1)}, u32[]{:S(2)}, u32[]{:S(2)}) async-start(bf16[32,2,128,128]{3,2,1,0:T(8,128)(2,1)} %bitcast.4), calls=%async_computation.9 | async-start | bytes 4194304 | tf_op jit(solution)/shard_map/all_to_all | solution.py:559
  180.6 24.2 %copy-start.12 = (bf16[4,256,256]{2,1,0:T(8,128)(2,1)S(1)}, bf16[4,256,256]{2,1,0:T(8,128)(2,1)}, u32[]{:S(2)}) copy-start(bf16[4,256,256]{2,1,0:T(8,128)(2,1)} %copy-done.11) | copy-start | bytes 1572868
  180.7 15.1 %collective-permute-start.8 = (bf16[4,256,256]{2,1,0:T(8,128)(2,1)}, bf16[4,256,256]{2,1,0:T(8,128)(2,1)S(1)}, u32[]{:S(2)}, u32[]{:S(2)}) collective-permute-start(bf16[4,256,256]{2,1,0:T(8,128)(2,1)} %copy-done.8), channel_id=1, source_target_pairs={{64,66},{65,67},{66,64},{67,65},{68,70},{69,71},{70,68},{71,69},{7... | collective-permute-start | bytes 1572872 | tf_op jit(solution)/shard_map/ppermute | solution.py:516
  184.2 14.4 %collective-permute-start.5 = (bf16[4,256,256]{2,1,0:T(8,128)(2,1)S(1)}, bf16[4,256,256]{2,1,0:T(8,128)(2,1)S(1)}, u32[]{:S(2)}, u32[]{:S(2)}) collective-permute-start(bf16[4,256,256]{2,1,0:T(8,128)(2,1)S(1)} %get-tuple-element.61), channel_id=1, source_target_pairs={{0,1},{1,2},{2,3},{3,0},{4,5},{5,6},{6,7},{7,4},{8,9},{9,10},{10,1... | collective-permute-start | bytes 1572872 | tf_op jit(solution)/shard_map/ppermute | solution.py:516
  187.7 16.5 %collective-permute-start.6 = (bf16[4,256,256]{2,1,0:T(8,128)(2,1)S(1)}, bf16[4,256,256]{2,1,0:T(8,128)(2,1)S(1)}, u32[]{:S(2)}, u32[]{:S(2)}) collective-permute-start(bf16[4,256,256]{2,1,0:T(8,128)(2,1)S(1)} %get-tuple-element.62), channel_id=1, source_target_pairs={{0,2},{1,3},{2,0},{3,1},{4,6},{5,7},{6,4},{7,5},{8,10},{9,11},{10,... | collective-permute-start | bytes 1572872 | tf_op jit(solution)/shard_map/ppermute | solution.py:516
  192.5 12.4 %collective-permute-start.7 = (bf16[4,256,256]{2,1,0:T(8,128)(2,1)S(1)}, bf16[4,256,256]{2,1,0:T(8,128)(2,1)S(1)}, u32[]{:S(2)}, u32[]{:S(2)}) collective-permute-start(bf16[4,256,256]{2,1,0:T(8,128)(2,1)S(1)} %get-tuple-element.63), channel_id=1, source_target_pairs={{0,3},{1,0},{2,1},{3,2},{4,7},{5,4},{6,5},{7,6},{8,11},{9,8},{10,9... | collective-permute-start | bytes 1572872 | tf_op jit(solution)/shard_map/ppermute | solution.py:516
  206.3 10.4 %collective-permute-start.10 = (bf16[1,256,256]{2,1,0:T(8,128)(2,1)}, bf16[1,256,256]{2,1,0:T(8,128)(2,1)S(1)}, u32[]{:S(2)}, u32[]{:S(2)}) collective-permute-start(bf16[1,256,256]{2,1,0:T(8,128)(2,1)} %get-tuple-element.69), channel_id=1, source_target_pairs={{0,16},{4,20},{8,24},{12,28},{16,44},{20,40},{24,36},{28,32},{32,6... | collective-permute-start | bytes 393224 | tf_op jit(solution)/shard_map/ppermute | solution.py:516
  208.1 9.1 %collective-permute-start.11 = (bf16[1,256,256]{2,1,0:T(8,128)(2,1)S(1)}, bf16[1,256,256]{2,1,0:T(8,128)(2,1)S(1)}, u32[]{:S(2)}, u32[]{:S(2)}) collective-permute-start(bf16[1,256,256]{2,1,0:T(8,128)(2,1)S(1)} %get-tuple-element.70), channel_id=1, source_target_pairs={{0,44},{4,40},{8,36},{12,32},{16,60},{20,56},{24,52},{28,48},{32,0... | collective-permute-start | bytes 393224 | tf_op jit(solution)/shard_map/ppermute | solution.py:516
  212.9 5.0 %collective-permute-start.12 = (bf16[1,256,256]{2,1,0:T(8,128)(2,1)S(1)}, bf16[1,256,256]{2,1,0:T(8,128)(2,1)S(1)}, u32[]{:S(2)}, u32[]{:S(2)}) collective-permute-start(bf16[1,256,256]{2,1,0:T(8,128)(2,1)S(1)} %get-tuple-element.71), channel_id=1, source_target_pairs={{0,60},{4,56},{8,52},{12,48},{16,0},{20,4},{24,8},{28,12},{32,16},... | collective-permute-start | bytes 393224 | tf_op jit(solution)/shard_map/ppermute | solution.py:516
  214.4 3.5 %collective-permute-start.9 = (bf16[1,256,256]{2,1,0:T(8,128)(2,1)S(1)}, bf16[1,256,256]{2,1,0:T(8,128)(2,1)S(1)}, u32[]{:S(2)}, u32[]{:S(2)}) collective-permute-start(bf16[1,256,256]{2,1,0:T(8,128)(2,1)S(1)} %get-tuple-element.68), channel_id=1, source_target_pairs={{0,0},{4,4},{8,8},{12,12},{16,16},{20,20},{24,24},{28,28},{32,44},... | collective-permute-start | bytes 393224 | tf_op jit(solution)/shard_map/ppermute | solution.py:516
  (11 other events, 45.4 us)

commit v6 on v5

--- a/solution.py
+++ b/solution.py
@@ -411,11 +411,22 @@
             out_ref[place] = made.astype(BF16)
 
 
-def add_body(first_ref, second_ref, *parts):
-    for k, part_ref in enumerate(parts):
-        for i in range(4):
-            total = first_ref[4 * k + i].astype(F32) + second_ref[4 * k + i].astype(F32)
-            part_ref[i] = total.astype(BF16)
+def add_body(layer, idx_ref, first_any, second_any, *rest):
+    parts, (first_ref, second_ref, sem) = rest[:4], rest[4:]
+
+    @pl.when(idx_ref[1] == layer)
+    def _():
+        loads = []
+        for k in range(4):
+            span = pl.ds(4 * k, 4)
+            loads.append(begin(first_any.at[span], first_ref.at[span], sem.at[2 * k]))
+            loads.append(begin(second_any.at[span], second_ref.at[span], sem.at[2 * k + 1]))
+        for k, part_ref in enumerate(parts):
+            loads[2 * k].wait()
+            loads[2 * k + 1].wait()
+            for i in range(4):
+                total = first_ref[4 * k + i].astype(F32) + second_ref[4 * k + i].astype(F32)
+                part_ref[i] = total.astype(BF16)
 
 
 def fold_body(idx_ref, *refs):
@@ -519,8 +530,15 @@
 
     def along_dp(first, second, layer):
         made = call(3, grad_body, [smem, vmem, vmem], product, [], idx, first, second)
-        got = near(lax.ppermute(made, "section", [(1 - layer, layer)]))
-        parts = call(2, add_body, [vmem] * 2, [row] * 4, [], made, got)
+        got = lax.ppermute(made, "section", [(1 - layer, layer)])
+        anywhere = pl.BlockSpec(memory_space=pl.ANY)
+
+        def add(*refs):
+            add_body(layer, *refs)
+
+        parts = call(
+            2, add, [smem] + [anywhere] * 2, [row] * 4, [product] * 2, idx, made, got, sems=8
+        )
         routes = [None]
         for k in range(1, 4):
             routes.append([(4 * layer + i, 4 * layer + (i + k) % 4) for i in range(4)])

time: 222 us -> 222 us (level)
  transfers between devices with their start and end apart: 16 -> 16, of which waited for: 8 -> 8; matrix products, arithmetic and copies ran while one was open for 0% -> 0% of each run, Pallas kernels for 12% -> 11%
where the time goes in v6:
time: 222 us; the launch traced here: 219 us
  blocking collectives  79.3 us (36%)
  Pallas kernels  45.8 us (21%)
  starting transfers between devices  42.9 us (19%)
  waiting for transfers between devices  41.9 us (19%)
  local copies, waits for them, and re-layouts  7.86 us (4%)
    all_to_all x7, blocking collectives, turn(): return near(lax.all_to_all(value, 'x', 0, 0, tiled=True))  79.3 us
    pallas_call x18, Pallas kernels, call(): pl.pallas_call(body, in_specs=ins, out_specs=outs or ([vmem] * len(shapes...  45.8 us
    all_to_all x1, waiting for transfers between devices, local(): recv = near(lax.all_to_all(packed, ('z', 'x'), 0, 0, tiled=True))  25.2 us
    ppermute x10, starting transfers between devices, exchange(): lax.ppermute(part, axes, route)  22.7 us
    ppermute x10, waiting for transfers between devices, exchange(): lax.ppermute(part, axes, route)  10.3 us
    all_to_all x1, starting transfers between devices, local(): recv = near(lax.all_to_all(packed, ('z', 'x'), 0, 0, tiled=True))  7.97 us
    unnamed x38, local copies, waits for them, and re-layouts  7.86 us
    all_to_all x1, starting transfers between devices, local(): ends = near(lax.all_to_all(ends, ('section', 'z', 'x'), 0, 0, tiled=True))  4.8 us
  transfers between devices with their start and end apart: 16, of which 8 were waited for; matrix products, arithmetic and copies ran while one was open for 0% of the time, Pallas kernels for 11%

profile of v6, /device:TPU:0, one launch (start us, length us, event | category | flops | bytes accessed | tf_op | source)
XLA Modules:
  0.0 218.9 jit_solution(6319901363201378481)
XLA Ops:
  0.8 3.5 %shard_map.86 = bf16[16,2,2,128,128]{4,3,2,1,0:T(8,128)(2,1)} custom-call(s32[4]{0:T(128)S(1)} %pad_add_fusion.idx_ref.refs_0_, bf16[8,4,128,256]{3,2,1,0:T(8,128)(2,1)} %field_hbm.1, bf16[8,4,128,256]{3,2,1,0:T(8,128)(2,1)} %cot_hbm.1), custom_call_target="tpu_custom_call" | custom-call | flops 3300000000 | bytes 1048576 | tf_op jit(solution)/shard_map/pallas_call | solution.py:489
  4.3 8.0 %all-to-all-start = ((bf16[16,2,2,128,128]{4,3,2,1,0:T(8,128)(2,1)}), bf16[16,2,2,128,128]{4,3,2,1,0:T(8,128)(2,1)S(1)}, u32[]{:S(2)}, u32[]{:S(2)}) async-start(bf16[16,2,2,128,128]{4,3,2,1,0:T(8,128)(2,1)} %shard_map.86), calls=%async_computation | async-start | bytes 4194304 | tf_op jit(solution)/shard_map/all_to_all | solution.py:511
  14.2 3.4 %shard_map.87 = (bf16[2,8,256,256]{3,2,1,0:T(8,128)(2,1)S(1)}, bf16[2,8,256,256]{3,2,1,0:T(8,128)(2,1)S(1)}, bf16[65,64,64]{2,1,0:T(8,128)(2,1)S(1)}, bf16[64,64,64]{2,1,0:T(8,128)(2,1)S(1)}) custom-call(s32[4]{0:T(128)S(1)} %pad_add_fusion.idx_ref.refs_0_, bf16[1,64,256,256]{3,2,1,0:T(8,128)(2,1)} %own_hbm.1, ...), custom_call_target="tpu_custom_call" | custom-call | flops 2200000000 | bytes 1048576 | tf_op jit(solution)/shard_map/pallas_call | solution.py:489
  21.3 25.2 %all-to-all-done.recv_ref = bf16[16,2,2,128,128]{4,3,2,1,0:T(8,128)(2,1)S(1)} async-done(((bf16[16,2,2,128,128]{4,3,2,1,0:T(8,128)(2,1)}), bf16[16,2,2,128,128]{4,3,2,1,0:T(8,128)(2,1)S(1)}, u32[]{:S(2)}, u32[]{:S(2)}) %all-to-all-start) | async-done | bytes 2097184 | tf_op jit(solution)/shard_map/all_to_all | solution.py:511
  48.7 12.4 %all_to_all.50.refs_1_ = bf16[4,576,128]{2,1,0:T(8,128)(2,1)S(1)} all-to-all(bf16[4,576,128]{2,1,0:T(8,128)(2,1)S(1)} %shard_map.88), channel_id=1, replica_groups=mesh['section'=2,'z'=4,'x'=4,'dp'=4] {'x'}, dimensions={0} | all-to-all | bytes 1179648 | tf_op jit(solution)/shard_map/all_to_all | solution.py:514
  62.3 11.3 %all_to_all.51.in_ref = bf16[4,576,128]{2,1,0:T(8,128)(2,1)S(1)} all-to-all(bf16[4,576,128]{2,1,0:T(8,128)(2,1)S(1)} %get-tuple-element.39), channel_id=1, replica_groups=mesh['section'=2,'z'=4,'x'=4,'dp'=4] {'x'}, dimensions={0} | all-to-all | bytes 1179648 | tf_op jit(solution)/shard_map/all_to_all | solution.py:514
  73.6 4.8 %shard_map.90 = (bf16[16,2,128,128]{3,2,1,0:T(8,128)(2,1)S(1)}, bf16[16,2,128,128]{3,2,1,0:T(8,128)(2,1)S(1)}, bf16[4,576,128]{2,1,0:T(8,128)(2,1)S(1)}) custom-call(bf16[4,576,128]{2,1,0:T(8,128)(2,1)S(1)} %all_to_all.51.in_ref, bf16[16,2,2,128,128]{4,3,2,1,0:T(8,128)(2,1)S(1)} %all-to-all-done.recv_ref, bf16[128,128]{1,0:T(8,128)(2,1)S(1)} %copy-done.9, ...), custom_call_target="tpu_custom_call" | custom-call | flops 6600000000 | bytes 1048576 | tf_op jit(solution)/shard_map/pallas_call | solution.py:489
  78.4 10.8 %all_to_all.52.refs_1_ = bf16[4,576,128]{2,1,0:T(8,128)(2,1)S(1)} all-to-all(bf16[4,576,128]{2,1,0:T(8,128)(2,1)S(1)} %get-tuple-element.41), channel_id=1, replica_groups=mesh['section'=2,'z'=4,'x'=4,'dp'=4] {'x'}, dimensions={0} | all-to-all | bytes 1179648 | tf_op jit(solution)/shard_map/all_to_all | solution.py:514
  90.4 10.8 %all_to_all.53.in_ref = bf16[4,576,128]{2,1,0:T(8,128)(2,1)S(1)} all-to-all(bf16[4,576,128]{2,1,0:T(8,128)(2,1)S(1)} %get-tuple-element.43), channel_id=1, replica_groups=mesh['section'=2,'z'=4,'x'=4,'dp'=4] {'x'}, dimensions={0} | all-to-all | bytes 1179648 | tf_op jit(solution)/shard_map/all_to_all | solution.py:514
  101.2 4.9 %shard_map.92 = (bf16[16,2,128,128]{3,2,1,0:T(8,128)(2,1)S(1)}, bf16[4,576,128]{2,1,0:T(8,128)(2,1)S(1)}) custom-call(bf16[4,576,128]{2,1,0:T(8,128)(2,1)S(1)} %all_to_all.53.in_ref, bf16[16,2,2,128,128]{4,3,2,1,0:T(8,128)(2,1)S(1)} %all-to-all-done.recv_ref, bf16[16,2,128,128]{3,2,1,0:T(8,128)(2,1)S(1)} %get-tuple-element.44.h_ref, ...), custom_call_target="tpu_custom_call" | custom-call | flops 6600000000 | bytes 1048576 | tf_op jit(solution)/shard_map/pallas_call | solution.py:489
  106.1 10.8 %all_to_all.54.refs_1_ = bf16[4,576,128]{2,1,0:T(8,128)(2,1)S(1)} all-to-all(bf16[4,576,128]{2,1,0:T(8,128)(2,1)S(1)} %get-tuple-element.45), channel_id=1, replica_groups=mesh['section'=2,'z'=4,'x'=4,'dp'=4] {'x'}, dimensions={0} | all-to-all | bytes 1179648 | tf_op jit(solution)/shard_map/all_to_all | solution.py:514
  123.7 10.8 %all_to_all.55.in_ref = bf16[4,576,128]{2,1,0:T(8,128)(2,1)S(1)} all-to-all(bf16[4,576,128]{2,1,0:T(8,128)(2,1)S(1)} %get-tuple-element.46), channel_id=1, replica_groups=mesh['section'=2,'z'=4,'x'=4,'dp'=4] {'x'}, dimensions={0} | all-to-all | bytes 1179648 | tf_op jit(solution)/shard_map/all_to_all | solution.py:514
  134.5 5.2 %shard_map.94 = (bf16[16,2,128,128]{3,2,1,0:T(8,128)(2,1)S(1)}, bf16[4,576,128]{2,1,0:T(8,128)(2,1)}) custom-call(bf16[4,576,128]{2,1,0:T(8,128)(2,1)S(1)} %all_to_all.55.in_ref, bf16[16,2,2,128,128]{4,3,2,1,0:T(8,128)(2,1)S(1)} %all-to-all-done.recv_ref, bf16[16,2,128,128]{3,2,1,0:T(8,128)(2,1)S(1)} %get-tuple-element.47.slope_ref, ...), custom_call_target="tpu_custom_call" | custom-call | flops 5500000256 | bytes 1048576 | tf_op jit(solution)/shard_map/pallas_call | solution.py:489
  140.6 3.5 %all-to-all-start.7 = ((bf16[4,576,128]{2,1,0:T(8,128)(2,1)}), bf16[4,576,128]{2,1,0:T(8,128)(2,1)S(1)}, u32[]{:S(2)}, u32[]{:S(2)}) async-start(bf16[4,576,128]{2,1,0:T(8,128)(2,1)} %get-tuple-element.48), calls=%async_computation.7 | async-start | bytes 1179648 | tf_op jit(solution)/shard_map/all_to_all | solution.py:514
  148.0 4.5 %all-to-all-done.7.refs_1_ = bf16[4,576,128]{2,1,0:T(8,128)(2,1)S(1)} async-done(((bf16[4,576,128]{2,1,0:T(8,128)(2,1)}), bf16[4,576,128]{2,1,0:T(8,128)(2,1)S(1)}, u32[]{:S(2)}, u32[]{:S(2)}) %all-to-all-start.7) | async-done | bytes 589856 | tf_op jit(solution)/shard_map/all_to_all | solution.py:514
  159.6 12.4 %all_to_all.56.in_ref = bf16[4,576,128]{2,1,0:T(8,128)(2,1)S(1)} all-to-all(bf16[4,576,128]{2,1,0:T(8,128)(2,1)S(1)} %get-tuple-element.49), channel_id=1, replica_groups=mesh['section'=2,'z'=4,'x'=4,'dp'=4] {'x'}, dimensions={0} | all-to-all | bytes 1179648 | tf_op jit(solution)/shard_map/all_to_all | solution.py:514
  172.1 3.8 %shard_map.96 = bf16[2,16,2,128,128]{4,3,2,1,0:T(8,128)(2,1)} custom-call(bf16[4,576,128]{2,1,0:T(8,128)(2,1)S(1)} %all_to_all.56.in_ref, bf16[16,2,128,128]{3,2,1,0:T(8,128)(2,1)S(1)} %copy-done.18, bf16[16,2,128,128]{3,2,1,0:T(8,128)(2,1)S(1)} %copy-done.16, bf16[128,128]{1,0:T(8,128)(2,1)S(1)} %copy-done.9, bf16[64,64,64]{2,1,0:T(8,128)(2,1)S(1)} %copy-done.7), custom_call_target="tpu_custom_call" | custom-call | flops 4400000000 | bytes 1048576 | tf_op jit(solution)/shard_map/pallas_call | solution.py:489
  175.8 4.8 %all-to-all-start.9 = ((bf16[32,2,128,128]{3,2,1,0:T(8,128)(2,1)}), bf16[32,2,128,128]{3,2,1,0:T(8,128)(2,1)S(1)}, u32[]{:S(2)}, u32[]{:S(2)}) async-start(bf16[32,2,128,128]{3,2,1,0:T(8,128)(2,1)} %bitcast.4), calls=%async_computation.9 | async-start | bytes 4194304 | tf_op jit(solution)/shard_map/all_to_all | solution.py:577
  181.5 2.9 %shard_map.101 = (bf16[4,256,256]{2,1,0:T(8,128)(2,1)S(1)}, bf16[4,256,256]{2,1,0:T(8,128)(2,1)S(1)}, bf16[4,256,256]{2,1,0:T(8,128)(2,1)S(1)}, bf16[4,256,256]{2,1,0:T(8,128)(2,1)S(1)}) custom-call(s32[4]{0:T(128)S(1)} %pad_add_fusion.idx_ref.refs_0_, bf16[16,256,256]{2,1,0:T(8,128)(2,1)} %shard_map.100.refs_1_, ...), custom_call_target="tpu_custom_call" | custom-call | flops 2200000000 | bytes 1048576 | tf_op jit(solution)/shard_map/pallas_call | solution.py:489
  184.4 3.5 %collective-permute-start.5 = (bf16[4,256,256]{2,1,0:T(8,128)(2,1)S(1)}, bf16[4,256,256]{2,1,0:T(8,128)(2,1)S(1)}, u32[]{:S(2)}, u32[]{:S(2)}) collective-permute-start(bf16[4,256,256]{2,1,0:T(8,128)(2,1)S(1)} %get-tuple-element.61), channel_id=1, source_target_pairs={{0,1},{1,2},{2,3},{3,0},{4,5},{5,6},{6,7},{7,4},{8,9},{9,10},{10,1... | collective-permute-start | bytes 1572872 | tf_op jit(solution)/shard_map/ppermute | solution.py:527
  187.9 4.8 %collective-permute-start.6 = (bf16[4,256,256]{2,1,0:T(8,128)(2,1)S(1)}, bf16[4,256,256]{2,1,0:T(8,128)(2,1)S(1)}, u32[]{:S(2)}, u32[]{:S(2)}) collective-permute-start(bf16[4,256,256]{2,1,0:T(8,128)(2,1)S(1)} %get-tuple-element.62), channel_id=1, source_target_pairs={{0,2},{1,3},{2,0},{3,1},{4,6},{5,7},{6,4},{7,5},{8,10},{9,11},{10,... | collective-permute-start | bytes 1572872 | tf_op jit(solution)/shard_map/ppermute | solution.py:527
  192.7 3.3 %collective-permute-start.7 = (bf16[4,256,256]{2,1,0:T(8,128)(2,1)S(1)}, bf16[4,256,256]{2,1,0:T(8,128)(2,1)S(1)}, u32[]{:S(2)}, u32[]{:S(2)}) collective-permute-start(bf16[4,256,256]{2,1,0:T(8,128)(2,1)S(1)} %get-tuple-element.63), channel_id=1, source_target_pairs={{0,3},{1,0},{2,1},{3,2},{4,7},{5,4},{6,5},{7,6},{8,11},{9,8},{10,9... | collective-permute-start | bytes 1572872 | tf_op jit(solution)/shard_map/ppermute | solution.py:527
  198.6 5.6 %collective-permute-done.6.refs_2_ = bf16[4,256,256]{2,1,0:T(8,128)(2,1)S(1)} collective-permute-done((bf16[4,256,256]{2,1,0:T(8,128)(2,1)S(1)}, bf16[4,256,256]{2,1,0:T(8,128)(2,1)S(1)}, u32[]{:S(2)}, u32[]{:S(2)}) %collective-permute-start.6) | collective-permute-done | bytes 524320 | tf_op jit(solution)/shard_map/ppermute | solution.py:527
  208.3 4.8 %collective-permute-start.11 = (bf16[1,256,256]{2,1,0:T(8,128)(2,1)S(1)}, bf16[1,256,256]{2,1,0:T(8,128)(2,1)S(1)}, u32[]{:S(2)}, u32[]{:S(2)}) collective-permute-start(bf16[1,256,256]{2,1,0:T(8,128)(2,1)S(1)} %get-tuple-element.70), channel_id=1, source_target_pairs={{0,44},{4,40},{8,36},{12,32},{16,60},{20,56},{24,52},{28,48},{32,0... | collective-permute-start | bytes 393224 | tf_op jit(solution)/shard_map/ppermute | solution.py:527
  (72 shorter events, 42.2 us)
Async XLA Ops:
  0.6 13.6 %collective-permute-start = (bf16[1,64,256,256]{3,2,1,0:T(8,128)(2,1)}, bf16[1,64,256,256]{3,2,1,0:T(8,128)(2,1)}, u32[]{:S(2)}, u32[]{:S(2)}) collective-permute-start(bf16[1,64,256,256]{3,2,1,0:T(8,128)(2,1)} %own_hbm.1), channel_id=1, source_target_pairs={{0,64},{64,0},{1,65},{65,1},{2,66},{66,2},{3,67},{67,3},{4,68},{68... | collective-permute-start | bytes 25165832 | tf_op jit(solution)/shard_map/ppermute | solution.py:505
  4.3 42.1 %all-to-all-start = ((bf16[16,2,2,128,128]{4,3,2,1,0:T(8,128)(2,1)}), bf16[16,2,2,128,128]{4,3,2,1,0:T(8,128)(2,1)S(1)}, u32[]{:S(2)}, u32[]{:S(2)}) async-start(bf16[16,2,2,128,128]{4,3,2,1,0:T(8,128)(2,1)} %shard_map.86), calls=%async_computation | async-start | bytes 4194304 | tf_op jit(solution)/shard_map/all_to_all | solution.py:511
  12.3 34.2 %copy-start.10 = (bf16[128,128]{1,0:T(8,128)(2,1)S(1)}, bf16[128,128]{1,0:T(8,128)(2,1)}, u32[]{:S(2)}) copy-start(bf16[128,128]{1,0:T(8,128)(2,1)} %constant.28.clone.ana_ref) | copy-start | bytes 98308
  46.5 14.6 %copy-start.1 = (bf16[2,8,256,256]{3,2,1,0:T(8,128)(2,1)S(1)}, bf16[2,8,256,256]{3,2,1,0:T(8,128)(2,1)}, u32[]{:S(2)}) copy-start(bf16[2,8,256,256]{3,2,1,0:T(8,128)(2,1)} %copy-done) | copy-start | bytes 6291460
  61.1 12.5 %copy-start.9 = (bf16[128,128]{1,0:T(8,128)(2,1)S(1)}, bf16[128,128]{1,0:T(8,128)(2,1)}, u32[]{:S(2)}) copy-start(bf16[128,128]{1,0:T(8,128)(2,1)} %constant.27.clone.syn_ref) | copy-start | bytes 98308
  73.6 15.6 %copy-start.4 = (bf16[2,8,256,256]{3,2,1,0:T(8,128)(2,1)S(1)}, bf16[2,8,256,256]{3,2,1,0:T(8,128)(2,1)}, u32[]{:S(2)}) copy-start(bf16[2,8,256,256]{3,2,1,0:T(8,128)(2,1)} %copy-done.3) | copy-start | bytes 6291460
  121.1 23.1 %collective-permute-start.1 = (bf16[16,256,256]{2,1,0:T(8,128)(2,1)}, bf16[16,256,256]{2,1,0:T(8,128)(2,1)}, u32[]{:S(2)}, u32[]{:S(2)}) collective-permute-start(bf16[16,256,256]{2,1,0:T(8,128)(2,1)} %shard_map.98.refs_1_), channel_id=1, source_target_pairs={{0,64},{1,65},{2,66},{3,67},{4,68},{5,69},{6,70},{7,71},{8,72},{9,... | collective-permute-start | bytes 6291464 | tf_op jit(solution)/shard_map/ppermute | solution.py:533
  140.6 11.9 %all-to-all-start.7 = ((bf16[4,576,128]{2,1,0:T(8,128)(2,1)}), bf16[4,576,128]{2,1,0:T(8,128)(2,1)S(1)}, u32[]{:S(2)}, u32[]{:S(2)}) async-start(bf16[4,576,128]{2,1,0:T(8,128)(2,1)} %get-tuple-element.48), calls=%async_computation.7 | async-start | bytes 1179648 | tf_op jit(solution)/shard_map/all_to_all | solution.py:514
  146.4 9.2 %collective-permute-start.2 = (bf16[4,256,256]{2,1,0:T(8,128)(2,1)S(1)}, bf16[4,256,256]{2,1,0:T(8,128)(2,1)S(1)}, u32[]{:S(2)}, u32[]{:S(2)}) collective-permute-start(bf16[4,256,256]{2,1,0:T(8,128)(2,1)S(1)} %get-tuple-element.57), channel_id=1, source_target_pairs={{64,65},{65,66},{66,67},{67,64},{68,69},{69,70},{70,71},{71,68},{7... | collective-permute-start | bytes 1572872 | tf_op jit(solution)/shard_map/ppermute | solution.py:527
  147.1 8.6 %collective-permute-start.3 = (bf16[4,256,256]{2,1,0:T(8,128)(2,1)S(1)}, bf16[4,256,256]{2,1,0:T(8,128)(2,1)S(1)}, u32[]{:S(2)}, u32[]{:S(2)}) collective-permute-start(bf16[4,256,256]{2,1,0:T(8,128)(2,1)S(1)} %get-tuple-element.58), channel_id=1, source_target_pairs={{64,67},{65,64},{66,65},{67,66},{68,71},{69,68},{70,69},{71,70},{7... | collective-permute-start | bytes 1572872 | tf_op jit(solution)/shard_map/ppermute | solution.py:527
  155.6 16.4 %copy-start.7 = (bf16[64,64,64]{2,1,0:T(8,128)(2,1)S(1)}, bf16[64,64,64]{2,1,0:T(8,128)(2,1)}, u32[]{:S(2)}) copy-start(bf16[64,64,64]{2,1,0:T(8,128)(2,1)} %copy-done.5) | copy-start | bytes 1572868
  155.6 16.4 %copy-start.16 = (bf16[16,2,128,128]{3,2,1,0:T(8,128)(2,1)S(1)}, bf16[16,2,128,128]{3,2,1,0:T(8,128)(2,1)}, u32[]{:S(2)}) copy-start(bf16[16,2,128,128]{3,2,1,0:T(8,128)(2,1)} %copy-done.15) | copy-start | bytes 3145732
  155.6 16.4 %copy-start.18 = (bf16[16,2,128,128]{3,2,1,0:T(8,128)(2,1)S(1)}, bf16[16,2,128,128]{3,2,1,0:T(8,128)(2,1)}, u32[]{:S(2)}) copy-start(bf16[16,2,128,128]{3,2,1,0:T(8,128)(2,1)} %copy-done.17) | copy-start | bytes 3145732
  158.3 23.1 %collective-permute-start.4 = (bf16[16,256,256]{2,1,0:T(8,128)(2,1)}, bf16[16,256,256]{2,1,0:T(8,128)(2,1)}, u32[]{:S(2)}, u32[]{:S(2)}) collective-permute-start(bf16[16,256,256]{2,1,0:T(8,128)(2,1)} %shard_map.100.refs_1_), channel_id=1, source_target_pairs={{64,0},{65,1},{66,2},{67,3},{68,4},{69,5},{70,6},{71,7},{72,8},{73... | collective-permute-start | bytes 6291464 | tf_op jit(solution)/shard_map/ppermute | solution.py:533
  175.8 39.4 %all-to-all-start.9 = ((bf16[32,2,128,128]{3,2,1,0:T(8,128)(2,1)}), bf16[32,2,128,128]{3,2,1,0:T(8,128)(2,1)S(1)}, u32[]{:S(2)}, u32[]{:S(2)}) async-start(bf16[32,2,128,128]{3,2,1,0:T(8,128)(2,1)} %bitcast.4), calls=%async_computation.9 | async-start | bytes 4194304 | tf_op jit(solution)/shard_map/all_to_all | solution.py:577
  180.6 24.4 %copy-start.12 = (bf16[4,256,256]{2,1,0:T(8,128)(2,1)S(1)}, bf16[4,256,256]{2,1,0:T(8,128)(2,1)}, u32[]{:S(2)}) copy-start(bf16[4,256,256]{2,1,0:T(8,128)(2,1)} %copy-done.11) | copy-start | bytes 1572868
  180.7 15.3 %collective-permute-start.8 = (bf16[4,256,256]{2,1,0:T(8,128)(2,1)}, bf16[4,256,256]{2,1,0:T(8,128)(2,1)S(1)}, u32[]{:S(2)}, u32[]{:S(2)}) collective-permute-start(bf16[4,256,256]{2,1,0:T(8,128)(2,1)} %copy-done.8), channel_id=1, source_target_pairs={{64,66},{65,67},{66,64},{67,65},{68,70},{69,71},{70,68},{71,69},{7... | collective-permute-start | bytes 1572872 | tf_op jit(solution)/shard_map/ppermute | solution.py:527
  184.4 14.2 %collective-permute-start.5 = (bf16[4,256,256]{2,1,0:T(8,128)(2,1)S(1)}, bf16[4,256,256]{2,1,0:T(8,128)(2,1)S(1)}, u32[]{:S(2)}, u32[]{:S(2)}) collective-permute-start(bf16[4,256,256]{2,1,0:T(8,128)(2,1)S(1)} %get-tuple-element.61), channel_id=1, source_target_pairs={{0,1},{1,2},{2,3},{3,0},{4,5},{5,6},{6,7},{7,4},{8,9},{9,10},{10,1... | collective-permute-start | bytes 1572872 | tf_op jit(solution)/shard_map/ppermute | solution.py:527
  187.9 16.3 %collective-permute-start.6 = (bf16[4,256,256]{2,1,0:T(8,128)(2,1)S(1)}, bf16[4,256,256]{2,1,0:T(8,128)(2,1)S(1)}, u32[]{:S(2)}, u32[]{:S(2)}) collective-permute-start(bf16[4,256,256]{2,1,0:T(8,128)(2,1)S(1)} %get-tuple-element.62), channel_id=1, source_target_pairs={{0,2},{1,3},{2,0},{3,1},{4,6},{5,7},{6,4},{7,5},{8,10},{9,11},{10,... | collective-permute-start | bytes 1572872 | tf_op jit(solution)/shard_map/ppermute | solution.py:527
  192.7 12.4 %collective-permute-start.7 = (bf16[4,256,256]{2,1,0:T(8,128)(2,1)S(1)}, bf16[4,256,256]{2,1,0:T(8,128)(2,1)S(1)}, u32[]{:S(2)}, u32[]{:S(2)}) collective-permute-start(bf16[4,256,256]{2,1,0:T(8,128)(2,1)S(1)} %get-tuple-element.63), channel_id=1, source_target_pairs={{0,3},{1,0},{2,1},{3,2},{4,7},{5,4},{6,5},{7,6},{8,11},{9,8},{10,9... | collective-permute-start | bytes 1572872 | tf_op jit(solution)/shard_map/ppermute | solution.py:527
  206.5 10.4 %collective-permute-start.10 = (bf16[1,256,256]{2,1,0:T(8,128)(2,1)}, bf16[1,256,256]{2,1,0:T(8,128)(2,1)S(1)}, u32[]{:S(2)}, u32[]{:S(2)}) collective-permute-start(bf16[1,256,256]{2,1,0:T(8,128)(2,1)} %get-tuple-element.69), channel_id=1, source_target_pairs={{0,16},{4,20},{8,24},{12,28},{16,44},{20,40},{24,36},{28,32},{32,6... | collective-permute-start | bytes 393224 | tf_op jit(solution)/shard_map/ppermute | solution.py:527
  208.3 9.1 %collective-permute-start.11 = (bf16[1,256,256]{2,1,0:T(8,128)(2,1)S(1)}, bf16[1,256,256]{2,1,0:T(8,128)(2,1)S(1)}, u32[]{:S(2)}, u32[]{:S(2)}) collective-permute-start(bf16[1,256,256]{2,1,0:T(8,128)(2,1)S(1)} %get-tuple-element.70), channel_id=1, source_target_pairs={{0,44},{4,40},{8,36},{12,32},{16,60},{20,56},{24,52},{28,48},{32,0... | collective-permute-start | bytes 393224 | tf_op jit(solution)/shard_map/ppermute | solution.py:527
  213.1 5.0 %collective-permute-start.12 = (bf16[1,256,256]{2,1,0:T(8,128)(2,1)S(1)}, bf16[1,256,256]{2,1,0:T(8,128)(2,1)S(1)}, u32[]{:S(2)}, u32[]{:S(2)}) collective-permute-start(bf16[1,256,256]{2,1,0:T(8,128)(2,1)S(1)} %get-tuple-element.71), channel_id=1, source_target_pairs={{0,60},{4,56},{8,52},{12,48},{16,0},{20,4},{24,8},{28,12},{32,16},... | collective-permute-start | bytes 393224 | tf_op jit(solution)/shard_map/ppermute | solution.py:527
  214.6 3.5 %collective-permute-start.9 = (bf16[1,256,256]{2,1,0:T(8,128)(2,1)S(1)}, bf16[1,256,256]{2,1,0:T(8,128)(2,1)S(1)}, u32[]{:S(2)}, u32[]{:S(2)}) collective-permute-start(bf16[1,256,256]{2,1,0:T(8,128)(2,1)S(1)} %get-tuple-element.68), channel_id=1, source_target_pairs={{0,0},{4,4},{8,8},{12,12},{16,16},{20,20},{24,24},{28,28},{32,44},... | collective-permute-start | bytes 393224 | tf_op jit(solution)/shard_map/ppermute | solution.py:527
  (11 other events, 45.4 us)
